TPU v7x, 128 devices: a whole 4x4x4 slice. The times are simulated.
128 devices in a mesh: prow: 8 (over x, core), pcol: 16 (over y, z).
Axes of the slice: x: 4, y: 4, z: 4, core: 2. Of those that a mesh axis runs over, the one named last changes fastest.
Arguments:
- child_fronts: float32 [8192, 16384], P('prow', 'pcol'), as said below
- parent_own: float32 [16384, 16384], P('prow', 'pcol'), as said below
- pattern: int32 [128, 128], P('prow', 'pcol'), may hold values from 0 to 1, as said below
- child_map: int32 [8, 32], replicated, may hold values from 0 to 127, as said below
Outputs:
- factored_front: float32 [16384, 16384], P('prow', 'pcol')
Inputs may be any that keep to these rules, and one draw needn't show every extreme that they name: `child_map`: each row lists 32 distinct parent blocks. In each aligned run of 8 entries of a row, at most 1 lie in any one aligned run of 16 parent blocks, and so at most 1 in any aligned run of 8. `pattern`: Symmetric, with ones on the diagonal. `child_fronts`: each child's tile is symmetric positive definite. `parent_own`: Symmetric; masked by a symmetric pattern with ones on the diagonal it stays positive definite.
All inputs are finite; a program needn't handle non-finite values.
Results may differ from a plain program's by a relative error of at most 0.0001.
Values sent between devices are 32-bit elements; how exact they have to be, the bound alone decides.
No kernel may reach another device: no remote copies, remote signals or barrier semaphores. Data moves between devices by JAX's collectives and lax.ppermute only.
A program may use at most 128 MiB of HBM per device.

v0:
```python
import jax
import jax.numpy as jnp
from jax import lax
from jax.sharding import PartitionSpec as P

BLK = 128
PANB = 4
NPAN = 2


def spread(value, axis, source):
    kept = jnp.where(lax.axis_index(axis) == source, value, 0).astype(value.dtype)
    return lax.psum(kept, axis)


def rank_within(stripes, groups):
    entries = stripes.shape[1]
    earlier = jnp.arange(entries)[:, None] > jnp.arange(entries)[None, :]
    same_group = groups[:, None] == groups[None, :]
    same_stripe = stripes[:, :, None] == stripes[:, None, :]
    return jnp.sum(same_stripe & (earlier & same_group)[None], axis=2)


def first_match(slot_keys, places):
    matches = slot_keys[..., None, :] == places[:, None]
    source = jnp.sum(jnp.where(matches, jnp.arange(slot_keys.shape[-1]), 0), axis=-1)
    return (source, jnp.any(matches, axis=-1))


def slot_targets(positions, targets, wanted, length):
    matches = (positions[None, :] == jnp.arange(length)[:, None]) & wanted[None, :]
    return jnp.sum(jnp.where(matches, targets[None, :] + 1, 0), axis=1) - 1


def device_part(table, child_at, group_at, span):
    table_row = lax.dynamic_index_in_dim(table, child_at, 0, keepdims=False)
    return lax.dynamic_slice_in_dim(table_row, group_at * span, span, 0)


def settle(solved, factor, places, start_at):
    panel_width = factor.shape[0]
    inside = (places >= start_at) & (places < start_at + panel_width)
    local_at = jnp.clip(places - start_at, 0, panel_width - 1)
    beyond = jnp.where((places >= start_at + panel_width)[:, None], solved, 0.0)
    return jnp.where(inside[:, None], jnp.take(factor, local_at, axis=0), beyond)


def body(child_fronts, parent_own, pattern, child_map):
    row_count = lax.axis_size("prow")
    col_count = lax.axis_size("pcol")
    row_index = lax.axis_index("prow")
    col_index = lax.axis_index("pcol")
    block_size = BLK
    child_dev = child_fronts.shape[0] // block_size
    row_stripe = parent_own.shape[0] // block_size
    col_stripe = parent_own.shape[1] // block_size
    child_blocks = child_map.shape[1]
    per_row = col_count // 4
    capacity = max(1, child_dev // row_count)
    groups = jnp.arange(child_blocks) // child_dev
    row_dest = child_map // row_stripe
    col_dest = child_map // col_stripe
    row_rank = rank_within(row_dest, groups)
    col_rank = rank_within(col_dest, groups)
    child_ids = jnp.arange(child_map.shape[0])
    source_row = (child_ids // per_row * 4)[:, None] + groups[None, :]
    source_col = (child_ids % per_row * 4)[:, None] + groups[None, :]
    wanted = (row_dest == row_index)[:, :, None] & (col_dest == col_index)[:, None, :]
    targets = (child_map - row_index * row_stripe)[:, :, None] * col_stripe + (
        child_map - col_index * col_stripe
    )[:, None, :]
    my_child = row_index // 4 * per_row + col_index // 4
    mine_row_dest = device_part(row_dest, my_child, row_index % 4, child_dev)
    mine_row_rank = device_part(row_rank, my_child, row_index % 4, child_dev)
    slot_count = capacity * capacity
    devices = row_count * col_count
    mine_col_dest = device_part(col_dest, my_child, col_index % 4, child_dev)
    mine_col_rank = device_part(col_rank, my_child, col_index % 4, child_dev)
    slot_keys = (
        (mine_row_dest[:, None] * col_count + mine_col_dest[None, :]) * slot_count
        + mine_row_rank[:, None] * capacity
        + mine_col_rank[None, :]
    )
    source, filled = first_match(slot_keys.reshape(-1), jnp.arange(devices * slot_count))
    pieces = (
        child_fronts.reshape(child_dev, block_size, child_dev, block_size)
        .transpose(0, 2, 1, 3)
        .reshape(-1, block_size, block_size)
    )
    outgoing = jnp.where(filled[:, None, None], jnp.take(pieces, source, axis=0), 0.0)
    outgoing = outgoing.reshape(devices, slot_count, block_size, block_size)
    incoming = lax.all_to_all(outgoing, ("prow", "pcol"), split_axis=0, concat_axis=0, tiled=True)
    positions = (
        (source_row[:, :, None] * col_count + source_col[:, None, :]) * slot_count
        + row_rank[:, :, None] * capacity
        + col_rank[:, None, :]
    )
    length = devices * slot_count
    slot_target = slot_targets(
        positions.reshape(-1), targets.reshape(-1), wanted.reshape(-1), length
    )
    selector = (slot_target[None, :] == jnp.arange(row_stripe * col_stripe)[:, None]).astype(
        jnp.float32
    )
    gathered = jnp.dot(
        selector,
        incoming.reshape(length, -1),
        precision=lax.Precision.HIGHEST,
        preferred_element_type=jnp.float32,
    )
    assembled = gathered.reshape(row_stripe, col_stripe, block_size, block_size).transpose(
        0, 2, 1, 3
    )
    assembled = assembled.reshape(row_stripe * block_size, col_stripe * block_size)
    own_part = (
        parent_own.reshape(row_stripe, block_size, col_stripe, block_size)
        * pattern.astype(jnp.float32)[:, None, :, None]
    )
    front_tile = own_part.reshape(row_stripe * block_size, col_stripe * block_size) + assembled
    rows_dev = front_tile.shape[0]
    cols_dev = front_tile.shape[1]
    panel_width = PANB * BLK
    row_global = row_index * rows_dev + jnp.arange(rows_dev)
    col_global = col_index * cols_dev + jnp.arange(cols_dev)
    for panel_step in range(NPAN):
        start_at = panel_step * panel_width
        end_at = start_at + panel_width
        owner_col = start_at // cols_dev
        owner_row = start_at // rows_dev
        col_offset = start_at - owner_col * cols_dev
        row_offset = start_at - owner_row * rows_dev
        rows_panel = spread(front_tile[:, col_offset : col_offset + panel_width], "pcol", owner_col)
        pivot_here = rows_panel[row_offset : row_offset + panel_width, :]
        pivot_block = spread(pivot_here, "prow", owner_row)
        factor = jnp.linalg.cholesky(pivot_block)
        solved_rows = lax.linalg.triangular_solve(
            factor, rows_panel, left_side=False, lower=True, transpose_a=True
        )
        row_factor = settle(solved_rows, factor, row_global, start_at)
        mirror_at = col_index * cols_dev % rows_dev
        mirror_owner = col_index * cols_dev // rows_dev
        mirror_piece = lax.dynamic_slice_in_dim(row_factor, mirror_at, cols_dev, 0)
        col_factor = spread(mirror_piece, "prow", mirror_owner)
        update = jnp.dot(
            row_factor,
            col_factor.T,
            precision=lax.Precision.HIGHEST,
            preferred_element_type=jnp.float32,
        )
        trailing = (row_global >= end_at)[:, None] & (col_global >= end_at)[None, :]
        front_tile = jnp.where(trailing, front_tile - update, front_tile)
        panel_cols = (col_global >= start_at) & (col_global < end_at)
        column_values = jnp.take(
            row_factor, jnp.clip(col_global - start_at, 0, panel_width - 1), axis=1
        )
        front_tile = jnp.where(panel_cols[None, :], column_values, front_tile)
        upper_rows = (row_global >= start_at) & (row_global < end_at)
        front_tile = jnp.where(
            upper_rows[:, None] & (col_global >= end_at)[None, :], 0.0, front_tile
        )
    return front_tile


def solution(mesh):
    return jax.shard_map(
        body,
        mesh=mesh,
        in_specs=(P("prow", "pcol"), P("prow", "pcol"), P("prow", "pcol"), P()),
        out_specs=P("prow", "pcol"),
        check_vma=False,
    )
```

profile of v0, /device:TPU:14, one launch (start us, length us, event | category | flops | bytes accessed | tf_op | source)
XLA Modules:
  0.0 1064.1 jit_solution(3988275454889256079)
XLA Ops:
  8.3 3.2 copy.89
  11.8 2.7 copy.60
  14.5 6.7 gather_fusion
  21.1 6.6 fusion.8
  27.7 10.8 %all-to-all-start = ((f32[128,1,128,128]{3,2,1,0:T(8,128)}), f32[128,1,128,128]{3,2,1,0:T(8,128)}, u32[]{:S(2)}, u32[]{:S(2)}) async-start(f32[128,1,128,128]{3,2,1,0:T(8,128)} %fusion.8), calls=%async_computation | async-start | bytes 16777216 | tf_op jit(solution)/shard_map/all_to_all | solution.py:92
  39.6 9.2 copy.59
  49.7 97.7 %all-to-all-done = f32[128,1,128,128]{3,2,1,0:T(8,128)} async-done(((f32[128,1,128,128]{3,2,1,0:T(8,128)}), f32[128,1,128,128]{3,2,1,0:T(8,128)}, u32[]{:S(2)}, u32[]{:S(2)}) %all-to-all-start) | async-done | bytes 8388640 | tf_op jit(solution)/shard_map/all_to_all | solution.py:92
  147.4 9.3 copy.86
  156.7 7.1 fusion.5
  163.8 5.5 copy.93
  169.3 9.1 copy.87
  178.4 4.9 mul.83
  184.8 9.4 fusion.4
  194.2 3.4 copy-done.3
  199.9 103.4 %all-reduce.8.cloned.1.call-done = f32[2048,512]{0,1:T(8,128)} async-done(((f32[2048,512]{0,1:T(8,128)}), f32[2048,512]{0,1:T(8,128)}) %all-reduce.8.cloned.1.call-update) | async-done | bytes 4194320 | tf_op jit(solution)/shard_map/psum | solution.py:13
  306.2 59.3 %all-reduce.10.cloned.1.call-done = f32[512,512]{0,1:T(8,128)} async-done(((f32[512,512]{0,1:T(8,128)}), f32[512,512]{0,1:T(8,128)}) %all-reduce.10.cloned.1.call-update) | async-done | bytes 1048592 | tf_op jit(solution)/shard_map/psum | solution.py:13
  368.5 11.7 %cholesky.286 = f32[128,128]{1,0:T(8,128)S(1)} custom-call(f32[128,128]{1,0:T(8,128)S(1)} %cholesky.426), custom_call_target="Cholesky" | custom-call | tf_op jit(solution)/shard_map/jit(cholesky)/cholesky | solution.py:135
  380.4 9.8 custom-call.27
  390.9 11.7 %cholesky.305 = f32[128,128]{1,0:T(8,128)S(1)} custom-call(f32[128,128]{1,0:T(8,128)S(1)} %cholesky.430), custom_call_target="Cholesky" | custom-call | tf_op jit(solution)/shard_map/jit(cholesky)/cholesky | solution.py:135
  404.1 9.9 custom-call.28
  414.7 11.7 %cholesky.326 = f32[128,128]{1,0:T(8,128)S(1)} custom-call(f32[128,128]{1,0:T(8,128)S(1)} %cholesky.435), custom_call_target="Cholesky" | custom-call | tf_op jit(solution)/shard_map/jit(cholesky)/cholesky | solution.py:135
  427.2 9.8 custom-call.29
  437.6 11.7 %cholesky.343 = f32[128,128]{1,0:T(8,128)S(1)} custom-call(f32[128,128]{1,0:T(8,128)S(1)} %convolution_subtract_fusion.9), custom_call_target="Cholesky" | custom-call | tf_op jit(solution)/shard_map/jit(cholesky)/cholesky | solution.py:135
  453.1 9.0 gather_fusion.1
  462.0 5.4 copy.65
  467.5 8.3 while.4
  475.8 39.3 %custom-call.30 = f32[4,128,128]{1,2,0:T(8,128)S(1)} custom-call(f32[4,128,128]{2,1,0:T(8,128)S(1)} %get-tuple-element.23), custom_call_target="InvertDiagBlocksLowerTriangular" | custom-call | tf_op jit(solution)/shard_map/triangular_solve/custom-call.3 | solution.py:136
  532.1 11.2 %gather_fusion.2 = f32[1024,2048]{1,0:T(8,128)} fusion(f32[2048,512]{0,1:T(8,128)} %copy-done.1, s32[1024]{0:T(1024)S(1)} %fusion.115), kind=kCustom, calls=%fused_computation.1.clone | custom fusion | bytes 16781312 | tf_op jit(solution)/shard_map/jit(_take)/gather | solution.py:153
  543.3 53.7 %all-reduce.12.cloned.1.call-done = f32[1024,512]{0,1:T(8,128)} async-done(((f32[1024,512]{0,1:T(8,128)}), f32[1024,512]{0,1:T(8,128)}) %all-reduce.12.cloned.1.call-update) | async-done | bytes 2097168 | tf_op jit(solution)/shard_map/psum | solution.py:13
  597.0 22.8 %fusion.1 = f32[2048,1024]{0,1:T(8,128)S(1)} fusion(f32[2048,1024]{0,1:T(8,128)} %copy-done.3, f32[1024,2048]{1,0:T(8,128)} %gather_fusion.2, pred[1024]{0:T(1024)(128)(4,1)S(1)} %get-tuple-element.96, pred[1024]{0:T(1024)(128)(4,1)S(1)} %fusion.124, pred[2048]{0:T(1024)(128)(4,1)S(1)} %get-tuple-element.93, pred[2048]{0:T(1024)(128)(4,1)S(1)} %get-tuple-element.94, ...), kind=kOutput, calls=%fused_computation.12 | convolution fusion | flops 12899581952 | bytes 31464448 | tf_op jit(solution)/shard_map/dot_general | solution.py:144
  619.8 3.4 copy-done.2
  625.6 105.7 %all-reduce.14.cloned.1.call-done = f32[2048,512]{0,1:T(8,128)} async-done(((f32[2048,512]{0,1:T(8,128)}), f32[2048,512]{0,1:T(8,128)}) %all-reduce.14.cloned.1.call-update) | async-done | bytes 4194320 | tf_op jit(solution)/shard_map/psum | solution.py:13
  734.0 59.6 %all-reduce.16.cloned.1.call-done = f32[512,512]{0,1:T(8,128)} async-done(((f32[512,512]{0,1:T(8,128)}), f32[512,512]{0,1:T(8,128)}) %all-reduce.16.cloned.1.call-update) | async-done | bytes 1048592 | tf_op jit(solution)/shard_map/psum | solution.py:13
  796.5 11.7 %cholesky.358 = f32[128,128]{1,0:T(8,128)S(1)} custom-call(f32[128,128]{1,0:T(8,128)S(1)} %cholesky.439), custom_call_target="Cholesky" | custom-call | tf_op jit(solution)/shard_map/jit(cholesky)/cholesky | solution.py:135
  808.4 9.8 custom-call.31
  818.9 11.7 %cholesky.377 = f32[128,128]{1,0:T(8,128)S(1)} custom-call(f32[128,128]{1,0:T(8,128)S(1)} %cholesky.443), custom_call_target="Cholesky" | custom-call | tf_op jit(solution)/shard_map/jit(cholesky)/cholesky | solution.py:135
  832.0 10.2 custom-call.32
  842.8 11.7 %cholesky.398 = f32[128,128]{1,0:T(8,128)S(1)} custom-call(f32[128,128]{1,0:T(8,128)S(1)} %cholesky.448), custom_call_target="Cholesky" | custom-call | tf_op jit(solution)/shard_map/jit(cholesky)/cholesky | solution.py:135
  855.3 9.8 custom-call.33
  865.7 11.7 %cholesky.415 = f32[128,128]{1,0:T(8,128)S(1)} custom-call(f32[128,128]{1,0:T(8,128)S(1)} %convolution_subtract_fusion.8), custom_call_target="Cholesky" | custom-call | tf_op jit(solution)/shard_map/jit(cholesky)/cholesky | solution.py:135
  881.0 9.0 gather_fusion.3
  890.0 5.4 copy.71
  895.4 7.6 while.5
  903.0 39.3 %custom-call.34 = f32[4,128,128]{1,2,0:T(8,128)S(1)} custom-call(f32[4,128,128]{2,1,0:T(8,128)S(1)} %get-tuple-element.24), custom_call_target="InvertDiagBlocksLowerTriangular" | custom-call | tf_op jit(solution)/shard_map/triangular_solve/custom-call.3 | solution.py:136
  959.2 11.2 %gather_fusion.4 = f32[1024,2048]{1,0:T(8,128)} fusion(f32[2048,512]{0,1:T(8,128)} %copy-done, s32[1024]{0:T(1024)S(1)} %fusion.118), kind=kCustom, calls=%fused_computation.3.clone | custom fusion | bytes 16781312 | tf_op jit(solution)/shard_map/jit(_take)/gather | solution.py:153
  970.3 53.8 %all-reduce.18.cloned.1.call-done = f32[1024,512]{0,1:T(8,128)} async-done(((f32[1024,512]{0,1:T(8,128)}), f32[1024,512]{0,1:T(8,128)}) %all-reduce.18.cloned.1.call-update) | async-done | bytes 2097168 | tf_op jit(solution)/shard_map/psum | solution.py:13
  1024.1 23.6 %fusion.3 = f32[2048,1024]{0,1:T(8,128)} fusion(f32[2048,1024]{0,1:T(8,128)} %copy-done.2, f32[1024,2048]{1,0:T(8,128)} %gather_fusion.4, pred[1024]{0:T(1024)(128)(4,1)S(1)} %get-tuple-element.98, pred[1024]{0:T(1024)(128)(4,1)S(1)} %fusion.123, pred[2048]{0:T(1024)(128)(4,1)S(1)} %get-tuple-element.91, pred[2048]{0:T(1024)(128)(4,1)S(1)} %fusion.106, ...), kind=kOutput, calls=%fused_computation.14 | convolution fusion | flops 12899581952 | bytes 31464448 | tf_op jit(solution)/shard_map/dot_general | solution.py:144
  1047.7 9.2 copy.76
  (163 shorter events, 81.6 us)
Async XLA Ops:
  27.7 11.7 %copy-start.9 = (s32[8,32]{1,0:T(8,128)S(1)}, s32[8,32]{1,0:T(8,128)}, u32[]{:S(2)}) copy-start(s32[8,32]{1,0:T(8,128)} %param.14) | copy-start | bytes 3076
  27.7 11.9 %copy-start.10 = (s32[16,8]{0,1:T(8,128)S(1)}, s32[16,8]{0,1:T(8,128)}, u32[]{:S(2)}) copy-start(s32[16,8]{0,1:T(8,128)} %param.13) | copy-start | bytes 1540
  27.7 119.7 %all-to-all-start = ((f32[128,1,128,128]{3,2,1,0:T(8,128)}), f32[128,1,128,128]{3,2,1,0:T(8,128)}, u32[]{:S(2)}, u32[]{:S(2)}) async-start(f32[128,1,128,128]{3,2,1,0:T(8,128)} %fusion.8), calls=%async_computation | async-start | bytes 16777216 | tf_op jit(solution)/shard_map/all_to_all | solution.py:92
  38.6 264.8 %all-reduce.8.cloned.1.call-start = ((), (), s32[]{:S(2)}) async-start(), calls=%async_computation.1 | async-start | bytes 8388608 | tf_op jit(solution)/shard_map/psum | solution.py:13
  178.4 6.4 copy-start.4
  194.2 3.4 copy-start.3
  199.9 165.7 %all-reduce.10.cloned.1.call-start = ((), (), s32[]{:S(2)}) async-start(), calls=%async_computation.2 | async-start | bytes 2097152 | tf_op jit(solution)/shard_map/psum | solution.py:13
  305.7 291.3 %all-reduce.12.cloned.1.call-start = ((), (), s32[]{:S(2)}) async-start(), calls=%async_computation.3 | async-start | bytes 4194304 | tf_op jit(solution)/shard_map/psum | solution.py:13
  515.1 5.8 copy-start.7
  523.3 3.3 copy-start.6
  528.4 2.0 copy-start.1
  532.0 199.3 %all-reduce.14.cloned.1.call-start = ((), (), s32[]{:S(2)}) async-start(), calls=%async_computation.4 | async-start | bytes 8388608 | tf_op jit(solution)/shard_map/psum | solution.py:13
  619.8 3.4 copy-start.2
  625.5 168.0 %all-reduce.16.cloned.1.call-start = ((), (), s32[]{:S(2)}) async-start(), calls=%async_computation.5 | async-start | bytes 2097152 | tf_op jit(solution)/shard_map/psum | solution.py:13
  733.7 290.4 %all-reduce.18.cloned.1.call-start = ((), (), s32[]{:S(2)}) async-start(), calls=%async_computation.6 | async-start | bytes 4194304 | tf_op jit(solution)/shard_map/psum | solution.py:13
  942.4 5.8 copy-start.8
  950.6 3.3 copy-start.5
  955.5 2.0 copy-start
Sparse Core Ops, SparseCore 0:
  200.0 103.2 all-reduce.7
  305.8 59.6 all-reduce.9
  532.1 64.8 all-reduce.11
  625.6 105.6 all-reduce.13
  733.8 59.6 all-reduce.15
  959.2 64.8 all-reduce.17
where the time goes:
time: 1070 us; the launch traced here: 1060 us
  waiting for transfers between devices  533 us (50%)
  other arithmetic  276 us (26%)
  local copies, waits for them, and re-layouts  143 us (13%)
  matrix products  80.2 us (7%)
  between operations  19.6 us (2%)
  starting transfers between devices  11.9 us (1%)
    psum x6, waiting for transfers between devices, spread(): return lax.psum(kept, axis)  435 us
    another operation x30, other arithmetic, body(): factor = jnp.linalg.cholesky(pivot_block)  159 us
    all_to_all x1, waiting for transfers between devices, body(): lax.all_to_all(outgoing, ('prow', 'pcol'), split_axis=0, concat_axis=0, t...  97.7 us
    another operation x5, other arithmetic, body(): lax.linalg.triangular_solve(factor, rows_panel, left_side=False, lower=Tr...  79.5 us
    dot_general x2, matrix products, body(): jnp.dot(row_factor, col_factor.T, precision=lax.Precision.HIGHEST, prefer...  46.5 us
    unnamed x25, local copies, waits for them, and re-layouts  30.1 us
    gather x4, local copies, waits for them, and re-layouts, settle(): jnp.take(factor, local_at, axis=0)  28.7 us
    another operation x14, matrix products, body(): lax.linalg.triangular_solve(factor, rows_panel, left_side=False, lower=Tr...  22.9 us
  transfers between devices with their start and end apart: 7, of which 7 were waited for; matrix products, arithmetic and copies ran while one was open for 3% of the time, Pallas kernels for 0%

commit v1 on v0

v1 whole, which is shorter than its diff:
```python
import jax
import jax.numpy as jnp
from jax import lax
from jax.experimental import pallas as pl
from jax.experimental.pallas import tpu as pltpu
from jax.sharding import PartitionSpec as P

B = 128
NB = 8
W = B * NB
ROWS = 8
COLS = 16
AXES = ("prow", "pcol")
F32 = jnp.float32
BF16 = jnp.bfloat16
HBM = pl.BlockSpec(memory_space=pl.ANY)
SMEM = pl.BlockSpec(memory_space=pltpu.SMEM)
VMEM = pl.BlockSpec(memory_space=pltpu.VMEM)
MIB = 1024 * 1024


def params(mib):
    return pltpu.CompilerParams(vmem_limit_bytes=mib * MIB)


def block(at):
    return pl.ds(pl.multiple_of(at * B, B), B)


def find(cmap, child, group, test):
    at = jnp.int32(-1)
    entry = jnp.int32(0)
    for k in range(8):
        value = cmap[child, group * 8 + k]
        hit = test(value)
        at = jnp.where(hit, k, at)
        entry = jnp.where(hit, value, entry)
    return at, entry


def pack_kernel(ids, cmap, child, bulk, small, sems, small_sems):
    r, c = ids[0], ids[1]
    mine = r // 4 * 4 + c // 4
    gi, gj = r % 4, c % 4
    ja, _ = find(cmap, mine, gj, lambda v: v < 8)
    ia, iv = find(cmap, mine, gi, lambda v: v < 8)
    ja = jnp.maximum(ja, 0)
    ia = jnp.maximum(ia, 0)

    def small_copy(a, slot, k, n):
        return pltpu.make_async_copy(
            child.at[block(a), block(ja)], small.at[slot, k], small_sems.at[n]
        )

    def bulk_copy(n):
        a, b = n // 8, n % 8
        slot = cmap[mine, gi * 8 + a] // 16 * COLS + cmap[mine, gj * 8 + b] // 8
        return pltpu.make_async_copy(child.at[block(a), block(b)], bulk.at[slot], sems.at[n])

    for a in range(8):
        small_copy(a, cmap[mine, gi * 8 + a] // 16, 0, a).start()
    small_copy(ia, jnp.minimum(iv, 7), 1, 8).start()
    lax.fori_loop(0, 64, lambda n, _: (bulk_copy(n).start(), 0)[1], 0)
    for a in range(8):
        small_copy(a, cmap[mine, gi * 8 + a] // 16, 0, a).wait()
    small_copy(ia, jnp.minimum(iv, 7), 1, 8).wait()
    lax.fori_loop(0, 64, lambda n, _: (bulk_copy(n).wait(), 0)[1], 0)


def pack(ids, cmap, child):
    return pl.pallas_call(
        pack_kernel,
        out_shape=(
            jax.ShapeDtypeStruct((ROWS * COLS, B, B), F32),
            jax.ShapeDtypeStruct((ROWS, 2, B, B), F32),
        ),
        in_specs=[SMEM, SMEM, HBM],
        out_specs=(HBM, HBM),
        scratch_shapes=[pltpu.SemaphoreType.DMA((64,)), pltpu.SemaphoreType.DMA((9,))],
        name="pack",
    )(ids, cmap, child)


def relay_kernel(ids, cmap, came, owners, diag, sems):
    r, c = ids[0], ids[1]
    copies = []
    for half in range(2):
        child = half * 4 + c // 4
        pick = jnp.int32(half * 4)
        for k in range(4):
            src = half * 4 + k
            _, entry = find(cmap, child, k, lambda v: v // 16 == r)
            copies.append((came.at[src, 0], owners.at[entry % 16, half]))
            at, _ = find(cmap, child, k, lambda v: v == r)
            pick = jnp.where(at >= 0, src, pick)
        copies.append((came.at[pick, 1], diag.at[half]))
    made = [pltpu.make_async_copy(s, d, sems.at[n]) for n, (s, d) in enumerate(copies)]
    for m in made:
        m.start()
    for m in made:
        m.wait()


def relay(ids, cmap, came):
    return pl.pallas_call(
        relay_kernel,
        out_shape=(
            jax.ShapeDtypeStruct((COLS, 2, B, B), F32),
            jax.ShapeDtypeStruct((2, B, B), F32),
        ),
        in_specs=[SMEM, SMEM, HBM],
        out_specs=(HBM, HBM),
        scratch_shapes=[pltpu.SemaphoreType.DMA((10,))],
        name="relay",
    )(ids, cmap, came)


def gather_rows(cmap, wanted, start, came, out):
    for k in range(NB):
        out[:, k * B : (k + 1) * B] = start[k * B : (k + 1) * B, :].T
    for child in range(8):
        half, quarter = child // 4, child % 4
        hit = lax.fori_loop(
            0, 32, lambda n, h: h | (cmap[child, n] == wanted).astype(jnp.int32), jnp.int32(0)
        )

        @pl.when(hit > 0)
        def _():
            for g in range(4):
                at, entry = find(cmap, child, g, lambda v: v < 8)

                @pl.when(at >= 0)
                def _():
                    where = block(jnp.minimum(entry, 7))
                    out[:, where] = out[:, where] + came[quarter * 4 + g, half]


def owner_kernel(ids, cmap, start, came, out):
    gather_rows(cmap, ids[0] * COLS + ids[1], start, came, out)


def diag_kernel(ids, cmap, start, came, out):
    gather_rows(cmap, ids[0], start, came, out)


def assemble(kernel, name, ids, cmap, start, came):
    return pl.pallas_call(
        kernel,
        out_shape=jax.ShapeDtypeStruct((B, W), F32),
        in_specs=[SMEM, SMEM, VMEM, VMEM],
        out_specs=VMEM,
        compiler_params=params(24),
        name=name,
    )(ids, cmap, start, came)


def spread_lane(x, k):
    return jnp.broadcast_to(x[:, k : k + 1], (8, B))


def spread_sub(x, k):
    return jnp.broadcast_to(x[k : k + 1, :], (8, B))


def eliminate_block(strips):
    sub = lax.broadcasted_iota(jnp.int32, (8, B), 0)
    lane = lax.broadcasted_iota(jnp.int32, (8, B), 1)
    strips = list(strips)
    for m in range(16):
        first = 8 * m
        inside = (lane >= first) & (lane < first + 8)
        w = strips[m]
        cols = [spread_lane(w, first + k) for k in range(8)]
        scales, rows, mults = [], [], []
        for k in range(8):
            rs = lax.rsqrt(spread_sub(cols[k], k))
            row = jnp.where(lane == first + k, rs, spread_sub(w, k) * rs)
            p = cols[k] * rs
            mult = [spread_sub(p, q) for q in range(k + 1, 8)]
            for n, q in enumerate(range(k + 1, 8)):
                cols[q] = cols[q] - p * mult[n]
            rest = jnp.where(lane == first + k, 0.0, w) - p * row
            w = jnp.where(sub > k, rest, jnp.where(sub == k, row, w))
            scales.append(rs)
            rows.append(jnp.where(inside & (lane > first + k), 0.0, row))
            mults.append(mult)
        strips[m] = w
        for s in range(m + 1, 16):
            v = strips[s]
            below = [spread_lane(v, first + k) for k in range(8)]
            v = jnp.where(inside, 0.0, v)
            for k in range(8):
                p = below[k] * scales[k]
                v = v - p * rows[k]
                for n, q in enumerate(range(k + 1, 8)):
                    below[q] = below[q] - p * mults[k][n]
            strips[s] = v
    return strips


def dot32(a, b, ca, cb):
    return lax.dot_general(
        a, b, (((ca,), (cb,)), ((), ())), precision=lax.Precision.HIGHEST, preferred_element_type=F32
    )


def factor_kernel(a_ref, w_ref, d_ref, q_ref):
    row = lax.broadcasted_iota(jnp.int32, (B, B), 0)
    col = lax.broadcasted_iota(jnp.int32, (B, B), 1)
    w_ref[...] = a_ref[...]

    def step(kb, _):
        here = block(kb)
        d_ref[...] = w_ref[here, here]
        strips = eliminate_block([d_ref[8 * s : 8 * s + 8, :] for s in range(16)])
        for s in range(16):
            d_ref[8 * s : 8 * s + 8, :] = strips[s]
        inverse = jnp.where(row >= col, d_ref[...], 0.0)
        q_ref[...] = dot32(inverse, w_ref[here, :], 1, 0)
        q_ref[:, here] = inverse

        def below(i, _):
            rows = block(i)
            w_ref[rows, here] = jnp.zeros((B, B), F32)
            w_ref[rows, :] = w_ref[rows, :] - dot32(q_ref[:, rows], q_ref[...], 0, 0)
            return 0

        lax.fori_loop(kb + 1, NB, below, 0)
        w_ref[here, :] = q_ref[...]
        w_ref[here, here] = d_ref[...]
        return 0

    lax.fori_loop(0, NB, step, 0)


def factor(a):
    return pl.pallas_call(
        factor_kernel,
        out_shape=jax.ShapeDtypeStruct((W, W), F32),
        in_specs=[VMEM],
        out_specs=VMEM,
        scratch_shapes=[pltpu.VMEM((B, B), F32), pltpu.VMEM((B, W), F32)],
        compiler_params=params(32),
        name="factor",
    )(a)


def halves(x):
    high = x.astype(BF16)
    return high, (x - high.astype(F32)).astype(BF16)


def dot_nt(a, b):
    return lax.dot_general(a, b, (((1,), (1,)), ((), ())), preferred_element_type=F32)


def dot3(ah, al, bh, bl):
    return dot_nt(ah, bh) + (dot_nt(ah, bl) + dot_nt(al, bh))


SOLVE = 256
CHUNK = 256


def solve_rows(raw, out, eh, el):
    xh, xl = halves(raw)
    for j in range(W // SOLVE):
        upto = (j + 1) * SOLVE
        rows = slice(j * SOLVE, upto)
        out[:, rows] = dot3(xh[:, :upto], xl[:, :upto], eh[rows, :upto], el[rows, :upto])


def update_kernel(ids, pattern, w_ref, xc_ref, xr_ref, own_ref, out_ref, eh, el, ch, cl, x):
    step = pl.program_id(0)
    r, c = ids[0], ids[1]

    @pl.when(step == 0)
    def _():
        row = lax.broadcasted_iota(jnp.int32, (B, W), 0)
        col = lax.broadcasted_iota(jnp.int32, (B, W), 1)

        def split(i, _):
            rows = block(i)
            high, low = halves(jnp.where(row + i * B >= col, w_ref[rows, :], 0.0))
            eh[rows, :] = high
            el[rows, :] = low
            return 0

        lax.fori_loop(0, NB, split, 0)

        def columns(i, _):
            rows = pl.ds(pl.multiple_of(i * CHUNK, CHUNK), CHUNK)
            solve_rows(xc_ref[rows, :], x, eh, el)
            high, low = halves(x[...])
            ch[rows, :] = high
            cl[rows, :] = low
            return 0

        lax.fori_loop(0, W // CHUNK, columns, 0)

    solve_rows(xr_ref[...], x, eh, el)
    top = (r == 0) & (step < W // CHUNK)

    @pl.when((c > 0) & top)
    def _():
        out_ref[...] = jnp.zeros_like(out_ref)

    @pl.when((c > 0) & jnp.logical_not(top))
    def _():
        high, low = halves(x[...])
        for j in range(W // SOLVE):
            cols = slice(j * SOLVE, (j + 1) * SOLVE)
            change = dot3(high, low, ch[cols, :], cl[cols, :])
            for a in range(CHUNK // B):
                for b in range(SOLVE // B):
                    rs = slice(a * B, (a + 1) * B)
                    at = j * (SOLVE // B) + b
                    cs = slice(at * B, (at + 1) * B)
                    keep = pattern[step * (CHUNK // B) + a, at].astype(F32)
                    out_ref[rs, cs] = own_ref[rs, cs] * keep - change[rs, b * B : (b + 1) * B]

    @pl.when((c == 0) & jnp.logical_not(top))
    def _():
        out_ref[...] = x[...]

    @pl.when((c == 0) & top)
    def _():
        row = lax.broadcasted_iota(jnp.int32, (CHUNK, B), 0)
        col = lax.broadcasted_iota(jnp.int32, (CHUNK, B), 1)
        for j in range(NB):
            cols = slice(j * B, (j + 1) * B)
            rows = pl.ds(pl.multiple_of(step * CHUNK, CHUNK), CHUNK)
            above = w_ref[cols, rows].T
            here = w_ref[rows, cols]
            gap = row + step * CHUNK - (col + j * B)
            out_ref[:, cols] = jnp.where(gap > 0, above, jnp.where(gap == 0, 1.0 / here, 0.0))


def update(ids, pattern, w, xc, xr, own):
    rows = own.shape[0]
    whole = pl.BlockSpec((W, W), lambda i: (0, 0), pipeline_mode=pl.Buffered(1))
    part = pl.BlockSpec((CHUNK, W), lambda i: (i, 0))
    return pl.pallas_call(
        update_kernel,
        grid=(rows // CHUNK,),
        out_shape=jax.ShapeDtypeStruct(own.shape, F32),
        in_specs=[SMEM, SMEM, whole, whole, part, part],
        out_specs=part,
        scratch_shapes=[pltpu.VMEM((W, W), BF16)] * 4 + [pltpu.VMEM((CHUNK, W), F32)],
        compiler_params=params(48),
        name="update",
    )(ids, pattern, w, xc, xr, own)


def add_kernel(ids, cmap, came, base, out, tile, parts, tile_sem, sems):
    r, c = ids[0], ids[1]
    load = pltpu.make_async_copy(base, tile, tile_sem)
    load.start()

    def visit(n, act):
        src_r, src_c = n // COLS, n % COLS
        child = src_r // 4 * 4 + src_c // 4
        ra, rv = find(cmap, child, src_r % 4, lambda v: v // 16 == r)
        ca, cv = find(cmap, child, src_c % 4, lambda v: v // 8 == c)
        low, col = rv % 16, cv % 8
        ok = (ra >= 0) & (ca >= 0) & (c > 0) & ((r > 0) | (low >= 8))

        @pl.when(ok)
        def _():
            act(n, low, col)

        return 0

    def copy(n):
        return pltpu.make_async_copy(came.at[n], parts.at[n], sems.at[n])

    def begin(n, low, col):
        copy(n).start()

    def finish(n, low, col):
        copy(n).wait()
        rows, cols = block(low), block(col)
        tile[rows, cols] = tile[rows, cols] + parts[n]

    lax.fori_loop(0, ROWS * COLS, lambda n, _: visit(n, begin), 0)
    load.wait()
    lax.fori_loop(0, ROWS * COLS, lambda n, _: visit(n, finish), 0)
    store = pltpu.make_async_copy(tile, out, tile_sem)
    store.start()
    store.wait()


def add(ids, cmap, came, base):
    return pl.pallas_call(
        add_kernel,
        out_shape=jax.ShapeDtypeStruct(base.shape, F32),
        in_specs=[SMEM, SMEM, HBM, HBM],
        out_specs=HBM,
        scratch_shapes=[
            pltpu.VMEM(base.shape, F32),
            pltpu.VMEM((ROWS * COLS, B, B), F32),
            pltpu.SemaphoreType.DMA(()),
            pltpu.SemaphoreType.DMA((ROWS * COLS,)),
        ],
        compiler_params=params(32),
        name="add",
    )(ids, cmap, came, base)


def at(r, c):
    return r * COLS + c


def body(child, own, pattern, cmap):
    ids = jnp.stack([lax.axis_index("prow"), lax.axis_index("pcol")]).astype(jnp.int32)
    bulk, small = pack(ids, cmap, child)
    small = lax.all_to_all(small, "prow", 0, 0, tiled=True)

    start = None
    keep = jnp.repeat(pattern[:NB].astype(F32), B, axis=0)
    for k in range(NB):
        piece = own[:W, k * B : (k + 1) * B] * keep[:, k : k + 1]
        moves = [(at(0, c), at(c // 2, 8 * (c % 2) + k)) for c in range(COLS)]
        piece = lax.ppermute(piece, AXES, moves)
        mine = lax.axis_index("pcol") % 8 == k
        start = jnp.where(mine, piece, 0.0 if start is None else start)
    diag_start = lax.ppermute(start, AXES, [(at(0, k), at(k, 0)) for k in range(NB)])
    diag_start = lax.all_to_all(diag_start, "pcol", 0, 0, tiled=True)[: W // COLS]
    diag_start = lax.all_gather(diag_start, "pcol", axis=0, tiled=True)

    owners, diag = relay(ids, cmap, small)
    diag = lax.all_gather(diag, "pcol", axis=0).reshape(COLS, 2, B, B)
    owners = lax.all_to_all(owners, "pcol", 0, 0, tiled=True)

    diag_rows = assemble(diag_kernel, "diag_rows", ids, cmap, diag_start, diag)
    pivot = lax.all_gather(diag_rows, "prow", axis=0, tiled=True)
    owned = assemble(owner_kernel, "owner_rows", ids, cmap, start, owners)
    moves = [
        (at(r, c), at(c % 8, 2 * r + c // 8)) for r in range(ROWS) for c in range(COLS)
    ]
    xc = lax.ppermute(owned, AXES, moves)
    xc = lax.all_gather(xc, "prow", axis=0, tiled=True)
    xr = lax.all_gather(owned, "pcol", axis=0, tiled=True)

    bulk = lax.all_to_all(bulk, AXES, 0, 0, tiled=True)
    w = factor(pivot)
    base = update(ids, pattern, w, xc, xr, own)
    return add(ids, cmap, bulk, base)


def solution(mesh):
    return jax.shard_map(
        body,
        mesh=mesh,
        in_specs=(P("prow", "pcol"), P("prow", "pcol"), P("prow", "pcol"), P()),
        out_specs=P("prow", "pcol"),
        check_vma=False,
    )
```

time: 1070 us -> 636 us (0.59)
  waiting for transfers between devices: 533 us -> 150 us
  Pallas kernels: 0 us -> 310 us
  other arithmetic: 276 us -> 7.82 us
  local copies, waits for them, and re-layouts: 143 us -> 13.7 us
  blocking collectives: 0 us -> 114 us
  matrix products: 80.2 us -> 0 us
  starting transfers between devices: 11.9 us -> 25.9 us
    psum x6 -> x0, waiting for transfers between devices: 435 us -> none  [spread(): return lax.psum(kept, axis)]
    pallas_call x0 -> x7, Pallas kernels: none -> 310 us  [the longest x1 147 us: pack(): pl.pallas_call(pack_kernel, out_shape=(jax.ShapeDtypeStruct((ROWS * COLS,...]
    another operation x35 -> x1, other arithmetic: 238 us -> 0.65 us  [body(): jnp.stack([lax.axis_index('prow'), lax.axis_index('pcol')])]
    all_gather x0 -> x4, waiting for transfers between devices: none -> 101 us  [the longest x1 101 us: body(): xr = lax.all_gather(owned, 'pcol', axis=0, tiled=True)]
    all_to_all x1, waiting for transfers between devices: 97.7 us -> 0.01 us  [body(): bulk = lax.all_to_all(bulk, AXES, 0, 0, tiled=True)]
    all_to_all x0 -> x3, blocking collectives: none -> 91.2 us  [the longest x1 44.3 us: body(): lax.all_to_all(diag_start, 'pcol', 0, 0, tiled=True)[:W // COLS]]
    gather x7 -> x0, local copies, waits for them, and re-layouts: 57.7 us -> none  [the longest x4 28.7 us: settle(): jnp.take(factor, local_at, axis=0)]
    dot_general x3 -> x0, matrix products: 53.5 us -> none  [the longest x2 46.5 us: body(): jnp.dot(row_factor, col_factor.T, precision=lax.Precision.HIGHEST, prefer...]
  transfers between devices with their start and end apart: 7 -> 15, of which waited for: 7 -> 3; matrix products, arithmetic and copies ran while one was open for 3% -> 1% of each run, Pallas kernels for 0% -> 15%
where the time goes in v1:
time: 636 us; the launch traced here: 634 us
  Pallas kernels  310 us (49%)
  waiting for transfers between devices  150 us (24%)
  blocking collectives  114 us (18%)
  starting transfers between devices  25.9 us (4%)
  local copies, waits for them, and re-layouts  13.7 us (2%)
  between operations  13.3 us (2%)
  other arithmetic  7.82 us (1%)
    pallas_call x1, Pallas kernels, pack(): pl.pallas_call(pack_kernel, out_shape=(jax.ShapeDtypeStruct((ROWS * COLS,...  147 us
    all_gather x1, waiting for transfers between devices, body(): xr = lax.all_gather(owned, 'pcol', axis=0, tiled=True)  101 us
    pallas_call x1, Pallas kernels, factor(): pl.pallas_call(factor_kernel, out_shape=jax.ShapeDtypeStruct((W, W), F32)...  55.5 us
    all_to_all x1, blocking collectives, body(): lax.all_to_all(diag_start, 'pcol', 0, 0, tiled=True)[:W // COLS]  44.3 us
    pallas_call x1, Pallas kernels, add(): pl.pallas_call(add_kernel, out_shape=jax.ShapeDtypeStruct(base.shape, F32...  42.5 us
    pallas_call x1, Pallas kernels, update(): pl.pallas_call(update_kernel, grid=(rows // CHUNK,), out_shape=jax.ShapeD...  34.7 us
    all_to_all x1, blocking collectives, body(): owners = lax.all_to_all(owners, 'pcol', 0, 0, tiled=True)  27.9 us
    ppermute x8, waiting for transfers between devices, body(): piece = lax.ppermute(piece, AXES, moves)  26.1 us
  transfers between devices with their start and end apart: 15, of which 3 were waited for; matrix products, arithmetic and copies ran while one was open for 1% of the time, Pallas kernels for 15%

profile of v1, /device:TPU:14, one launch (start us, length us, event | category | flops | bytes accessed | tf_op | source)
XLA Modules:
  0.0 634.4 jit_solution(12416120637578744743)
XLA Ops:
  6.5 0.7 pad_add_fusion.ids
  7.2 147.5 %pack.1 = (f32[128,128,128]{2,1,0:T(8,128)}, f32[8,2,128,128]{3,2,1,0:T(8,128)}) custom-call(s32[2]{0:T(128)} %pad_add_fusion.ids, s32[8,32]{1,0:T(8,128)} %cmap.9, f32[1024,1024]{1,0:T(8,128)} %child.1), custom_call_target="tpu_custom_call" | custom-call | tf_op jit(solution)/shard_map/pack/pallas_call | solution.py:71
  154.7 18.9 %all_to_all.24.came = f32[8,2,128,128]{3,2,1,0:T(8,128)} all-to-all(f32[8,2,128,128]{3,2,1,0:T(8,128)} %get-tuple-element.10), channel_id=1, replica_groups=mesh['prow'=8,'pcol'=16] {'prow'}, dimensions={0} | all-to-all | bytes 2097152 | tf_op jit(solution)/shard_map/all_to_all | solution.py:417
  173.6 22.0 %relay.1 = (f32[16,2,128,128]{3,2,1,0:T(8,128)}, f32[2,128,128]{2,1,0:T(8,128)}) custom-call(s32[2]{0:T(128)} %pad_add_fusion.ids, s32[8,32]{1,0:T(8,128)} %cmap.9, f32[8,2,128,128]{3,2,1,0:T(8,128)} %all_to_all.24.came), custom_call_target="tpu_custom_call" | custom-call | tf_op jit(solution)/shard_map/relay/pallas_call | solution.py:105
  195.6 0.0 all-gather.13.cloned.1.call-update
  195.6 0.0 all-gather.7.cloned.1.call-start
  195.7 0.7 slice_convert_fusion
  196.4 0.1 copy.9
  196.4 0.1 broadcast_bitcast_fusion
  196.6 5.2 slice_multiply_fusion
  201.8 0.7 collective-permute-start.7
  202.5 0.7 collective-permute-start.6
  203.2 0.7 collective-permute-start.5
  203.9 1.5 collective-permute-start.4
  205.4 1.3 collective-permute-start.3
  206.7 1.5 collective-permute-start.2
  208.1 0.0 collective-permute-done.6
  208.1 1.5 collective-permute-start.1
  209.6 0.8 copy-done.11
  210.5 1.5 collective-permute-start
  211.9 26.1 %collective-permute-done.3 = f32[1024,128]{1,0:T(8,128)} collective-permute-done((f32[1024,128]{1,0:T(8,128)}, f32[1024,128]{1,0:T(8,128)}, u32[]{:S(2)}, u32[]{:S(2)}) %collective-permute-start.3) | collective-permute-done | bytes 524320 | tf_op jit(solution)/shard_map/ppermute | solution.py:424
  238.1 1.3 select_select_fusion.start
  239.3 0.7 collective-permute-start.8
  240.1 44.3 %all_to_all.25 = f32[16,64,128]{2,1,0:T(8,128)S(1)} all-to-all(f32[16,64,128]{2,1,0:T(8,128)S(1)} %bitcast.17), channel_id=1, replica_groups=mesh['prow'=8,'pcol'=16] {'pcol'}, dimensions={0} | all-to-all | bytes 1048576 | tf_op jit(solution)/shard_map/all_to_all | solution.py:428
  284.3 23.2 %all-gather = f32[1,1024,128]{2,1,0:T(8,128)S(1)} all-gather(f32[1,64,128]{2,1,0:T(8,128)S(1)} %slice.84), channel_id=2, replica_groups=mesh['prow'=8,'pcol'=16] {'pcol'}, dimensions={1}, use_global_device_ids=true | all-gather | bytes 557056 | tf_op jit(solution)/shard_map/all_gather | solution.py:429
  307.5 1.6 copy-done.4
  309.1 3.8 diag_rows.1
  312.9 0.0 all-gather.7.cloned.1.call-update
  313.0 0.0 all-gather.9.cloned.1.call-start
  313.0 27.9 %all_to_all.26.came = f32[16,2,128,128]{3,2,1,0:T(8,128)S(1)} all-to-all(f32[16,2,128,128]{3,2,1,0:T(8,128)S(1)} %copy-done.7), channel_id=1, replica_groups=mesh['prow'=8,'pcol'=16] {'pcol'}, dimensions={0} | all-to-all | bytes 4194304 | tf_op jit(solution)/shard_map/all_to_all | solution.py:433
  341.0 3.9 owner_rows.1
  344.9 1.9 collective-permute-start.9
  346.8 22.0 %collective-permute-done.9 = f32[128,1024]{1,0:T(8,128)S(1)} collective-permute-done((f32[128,1024]{1,0:T(8,128)}, f32[128,1024]{1,0:T(8,128)S(1)}, u32[]{:S(2)}, u32[]{:S(2)}) %collective-permute-start.9) | collective-permute-done | bytes 524320 | tf_op jit(solution)/shard_map/ppermute | solution.py:441
  368.8 0.8 copy-done.8
  369.6 0.0 all-gather.9.cloned.1.call-update
  369.6 0.0 all-gather.11.cloned.1.call-start
  369.7 0.5 all-gather.11.cloned.1.call-update
  370.2 0.0 copy-start.12
  370.2 13.9 %all-to-all-start = ((f32[128,128,128]{2,1,0:T(8,128)}), f32[128,128,128]{2,1,0:T(8,128)}, u32[]{:S(2)}, u32[]{:S(2)}) async-start(f32[128,128,128]{2,1,0:T(8,128)} %get-tuple-element.9), calls=%async_computation | async-start | bytes 16777216 | tf_op jit(solution)/shard_map/all_to_all | solution.py:445
  384.1 0.1 copy.10.pattern
  384.2 2.6 copy-done.3
  386.8 55.5 %factor.1.w_ref = f32[1024,1024]{1,0:T(8,128)S(1)} custom-call(f32[1024,1024]{1,0:T(8,128)S(1)} %copy-done.3), custom_call_target="tpu_custom_call" | custom-call | tf_op jit(solution)/shard_map/factor/pallas_call | solution.py:237
  442.3 2.0 copy-done.1
  444.3 100.8 %all-gather.11.cloned.1.call-done.xr_ref = f32[2048,1024]{1,0:T(8,128)} async-done(((f32[128,1024]{1,0:T(8,128)}), f32[2048,1024]{1,0:T(8,128)}) %all-gather.11.cloned.1.call-update) | async-done | bytes 8388624 | tf_op jit(solution)/shard_map/all_gather | solution.py:443
  545.1 2.2 copy-done.2
  547.3 34.7 %update.1.base = f32[2048,1024]{1,0:T(8,128)} custom-call(s32[2]{0:T(128)S(1)} %copy-done.6, s32[16,8]{1,0:T(8,128)S(1)} %copy.10.pattern, f32[1024,1024]{1,0:T(8,128)S(1)} %copy-done.2, f32[1024,1024]{1,0:T(8,128)} %all-gather.9.cloned.1.call-done.xc_ref, f32[2048,1024]{1,0:T(8,128)} %all-gather.11.cloned.1.call-done.xr_ref, f32[2048,1024]{1,0:T(8,128)} %own_ref.1), custom_call_target="tpu_custom_call" | custom-call | tf_op jit(solution)/shard_map/update/pallas_call | solution.py:343
  582.0 3.4 copy-done
  585.3 42.5 %add.15 = f32[2048,1024]{1,0:T(8,128)} custom-call(s32[2]{0:T(128)S(1)} %copy-done.6, s32[8,32]{1,0:T(8,128)S(1)} %copy-done.5, f32[128,128,128]{2,1,0:T(8,128)} %all-to-all-done.came, f32[2048,1024]{1,0:T(8,128)S(1)} %copy-done), custom_call_target="tpu_custom_call" | custom-call | tf_op jit(solution)/shard_map/add/pallas_call | solution.py:394
  (32 shorter events, 0.1 us)
Async XLA Ops:
  6.5 301.0 %all-gather.13.cloned.1.call-start = ((), (), s32[]{:S(2)}) async-start(), calls=%async_computation.7 | async-start | bytes 2228224 | tf_op jit(solution)/shard_map/all_gather | solution.py:432
  173.6 133.9 %copy-start.5 = (s32[8,32]{1,0:T(8,128)S(1)}, s32[8,32]{1,0:T(8,128)}, u32[]{:S(2)}) copy-start(s32[8,32]{1,0:T(8,128)} %cmap.9) | copy-start | bytes 3076
  173.6 133.9 %copy-start.6 = (s32[2]{0:T(128)S(1)}, s32[2]{0:T(128)}, u32[]{:S(2)}) copy-start(s32[2]{0:T(128)} %pad_add_fusion.ids) | copy-start | bytes 28
  195.6 188.5 %all-gather.7.cloned.1.call-start = ((), (), s32[]{:S(2)}) async-start(), calls=%async_computation.4 | async-start | bytes 4718592 | tf_op jit(solution)/shard_map/all_gather | solution.py:436
  196.6 116.5 %copy-start.7 = (f32[16,2,128,128]{3,2,1,0:T(8,128)S(1)}, f32[16,2,128,128]{3,2,1,0:T(8,128)}, u32[]{:S(2)}) copy-start(f32[16,2,128,128]{3,2,1,0:T(8,128)} %get-tuple-element.12) | copy-start | bytes 6291460
  201.8 4.9 collective-permute-start.7
  202.5 5.7 collective-permute-start.6
  203.2 6.4 %collective-permute-start.5 = (f32[1024,128]{1,0:T(8,128)S(1)}, f32[1024,128]{1,0:T(8,128)S(1)}, u32[]{:S(2)}, u32[]{:S(2)}) collective-permute-start(f32[1024,128]{1,0:T(8,128)S(1)} %get-tuple-element.15), channel_id=1, source_target_pairs={{0,2},{1,10},{2,18},{3,26},{4,34},{5,42},{6,50},{7,58},{8,66},{9,7... | collective-permute-start | bytes 1572872 | tf_op jit(solution)/shard_map/ppermute | solution.py:424
  203.9 8.1 %collective-permute-start.4 = (f32[1024,128]{1,0:T(8,128)}, f32[1024,128]{1,0:T(8,128)}, u32[]{:S(2)}, u32[]{:S(2)}) collective-permute-start(f32[1024,128]{1,0:T(8,128)} %get-tuple-element.16), channel_id=1, source_target_pairs={{0,3},{1,11},{2,19},{3,27},{4,35},{5,43},{6,51},{7,59},{8,67},{9,7... | collective-permute-start | bytes 1572872 | tf_op jit(solution)/shard_map/ppermute | solution.py:424
  205.4 32.7 %collective-permute-start.3 = (f32[1024,128]{1,0:T(8,128)}, f32[1024,128]{1,0:T(8,128)}, u32[]{:S(2)}, u32[]{:S(2)}) collective-permute-start(f32[1024,128]{1,0:T(8,128)} %get-tuple-element.17), channel_id=1, source_target_pairs={{0,4},{1,12},{2,20},{3,28},{4,36},{5,44},{6,52},{7,60},{8,68},{9,7... | collective-permute-start | bytes 1572872 | tf_op jit(solution)/shard_map/ppermute | solution.py:424
  206.7 2.9 copy-start.9
  206.7 31.4 %collective-permute-start.2 = (f32[1024,128]{1,0:T(8,128)}, f32[1024,128]{1,0:T(8,128)}, u32[]{:S(2)}, u32[]{:S(2)}) collective-permute-start(f32[1024,128]{1,0:T(8,128)} %get-tuple-element.18), channel_id=1, source_target_pairs={{0,5},{1,13},{2,21},{3,29},{4,37},{5,45},{6,53},{7,61},{8,69},{9,7... | collective-permute-start | bytes 1572872 | tf_op jit(solution)/shard_map/ppermute | solution.py:424
  208.1 1.5 copy-start.10
  208.1 29.9 %collective-permute-start.1 = (f32[1024,128]{1,0:T(8,128)S(1)}, f32[1024,128]{1,0:T(8,128)}, u32[]{:S(2)}, u32[]{:S(2)}) collective-permute-start(f32[1024,128]{1,0:T(8,128)S(1)} %get-tuple-element.19), channel_id=1, source_target_pairs={{0,6},{1,14},{2,22},{3,30},{4,38},{5,46},{6,54},{7,62},{8,70},{9,7... | collective-permute-start | bytes 1572872 | tf_op jit(solution)/shard_map/ppermute | solution.py:424
  209.6 0.8 copy-start.11
  210.5 27.6 %collective-permute-start = (f32[1024,128]{1,0:T(8,128)S(1)}, f32[1024,128]{1,0:T(8,128)}, u32[]{:S(2)}, u32[]{:S(2)}) collective-permute-start(f32[1024,128]{1,0:T(8,128)S(1)} %get-tuple-element.20), channel_id=1, source_target_pairs={{0,7},{1,15},{2,23},{3,31},{4,39},{5,47},{6,55},{7,63},{8,71},{9,7... | collective-permute-start | bytes 1572872 | tf_op jit(solution)/shard_map/ppermute | solution.py:424
  239.3 0.7 collective-permute-start.8
  307.5 1.6 copy-start.4
  313.0 131.3 %all-gather.9.cloned.1.call-start = ((), (), s32[]{:S(2)}) async-start(), calls=%async_computation.5 | async-start | bytes 4718592 | tf_op jit(solution)/shard_map/all_gather | solution.py:442
  344.9 23.9 %collective-permute-start.9 = (f32[128,1024]{1,0:T(8,128)}, f32[128,1024]{1,0:T(8,128)S(1)}, u32[]{:S(2)}, u32[]{:S(2)}) collective-permute-start(f32[128,1024]{1,0:T(8,128)} %owner_rows.1), channel_id=1, source_target_pairs={{0,0},{1,16},{2,32},{3,48},{4,64},{5,80},{6,96},{7,112},{8,1},{9,1... | collective-permute-start | bytes 1572872 | tf_op jit(solution)/shard_map/ppermute | solution.py:441
  368.8 0.8 copy-start.8
  369.6 175.5 %all-gather.11.cloned.1.call-start = ((), (), s32[]{:S(2)}) async-start(), calls=%async_computation.6 | async-start | bytes 8912896 | tf_op jit(solution)/shard_map/all_gather | solution.py:443
  370.2 13.9 %copy-start.12 = (s32[16,8]{0,1:T(8,128)S(1)}, s32[16,8]{0,1:T(8,128)}, u32[]{:S(2)}) copy-start(s32[16,8]{0,1:T(8,128)} %param.6) | copy-start | bytes 1540
  370.2 211.8 %all-to-all-start = ((f32[128,128,128]{2,1,0:T(8,128)}), f32[128,128,128]{2,1,0:T(8,128)}, u32[]{:S(2)}, u32[]{:S(2)}) async-start(f32[128,128,128]{2,1,0:T(8,128)} %get-tuple-element.9), calls=%async_computation | async-start | bytes 16777216 | tf_op jit(solution)/shard_map/all_to_all | solution.py:445
  384.2 2.6 copy-start.3
  442.3 2.0 copy-start.1
  545.1 2.2 copy-start.2
  582.0 3.4 copy-start
Sparse Core Ops, SparseCore 0:
  195.8 88.7 all-gather.12
  313.1 30.3 all-gather.6
  369.7 67.6 all-gather.8
  439.5 105.5 all-gather.10

commit v2 on v1

v2 whole, which is shorter than its diff:
```python
import jax
import jax.numpy as jnp
from jax import lax
from jax.experimental import pallas as pl
from jax.experimental.pallas import tpu as pltpu
from jax.sharding import PartitionSpec as P

B = 128
NB = 8
W = B * NB
ROWS = 8
COLS = 16
AXES = ("prow", "pcol")
F32 = jnp.float32
BF16 = jnp.bfloat16
HBM = pl.BlockSpec(memory_space=pltpu.HBM)
SMEM = pl.BlockSpec(memory_space=pltpu.SMEM)
VMEM = pl.BlockSpec(memory_space=pltpu.VMEM)
MIB = 1024 * 1024
PARTS = 4
PART = B // PARTS


def params(mib):
    return pltpu.CompilerParams(vmem_limit_bytes=mib * MIB)


def block(at):
    return pl.ds(pl.multiple_of(at * B, B), B)


def find(cmap, child, group, test):
    at = jnp.int32(-1)
    entry = jnp.int32(0)
    for k in range(8):
        value = cmap[child, group * 8 + k]
        hit = test(value)
        at = jnp.where(hit, k, at)
        entry = jnp.where(hit, value, entry)
    return at, entry


def pack_small_kernel(ids, cmap, child, *rest):
    outs, sems = rest[:ROWS], rest[ROWS]
    r, c = ids[0], ids[1]
    mine = r // 4 * 4 + c // 4
    ja, _ = find(cmap, mine, c % 4, lambda v: v < 8)
    ia, _ = find(cmap, mine, r % 4, lambda v: v < 8)
    ja = jnp.maximum(ja, 0)
    ia = jnp.maximum(ia, 0)
    made = []
    for d in range(ROWS):
        a, _ = find(cmap, mine, r % 4, lambda v: v // 16 == (r + d) % ROWS)
        for k, row in enumerate((jnp.maximum(a, 0), ia)):
            src = child.at[block(row), block(ja)]
            made.append(pltpu.make_async_copy(src, outs[d].at[k], sems.at[2 * d + k]))
    for m in made:
        m.start()
    for m in made:
        m.wait()


def pack_small(ids, cmap, child):
    return pl.pallas_call(
        pack_small_kernel,
        out_shape=(jax.ShapeDtypeStruct((2, B, B), F32),) * ROWS,
        in_specs=[SMEM, SMEM, VMEM],
        out_specs=(HBM,) * ROWS,
        scratch_shapes=[pltpu.SemaphoreType.DMA((2 * ROWS,))],
        compiler_params=params(12),
        name="pack_small",
    )(ids, cmap, child)


def pack_kernel(ids, cmap, child, *rest):
    bulk, sems = rest[:PARTS], rest[PARTS]
    r, c = ids[0], ids[1]
    mine = r // 4 * 4 + c // 4
    gi, gj = r % 4, c % 4

    def copies(n):
        a, b = n // 8, n % 8
        slot = cmap[mine, gi * 8 + a] // 16 * COLS + cmap[mine, gj * 8 + b] // 8
        for part in range(PARTS):
            rows = pl.ds(pl.multiple_of(a * B + part * PART, PART), PART)
            src = child.at[rows, block(b)]
            yield pltpu.make_async_copy(src, bulk[part].at[slot], sems.at[n, part])

    def start(n, _):
        for m in copies(n):
            m.start()
        return 0

    def wait(n, _):
        for m in copies(n):
            m.wait()
        return 0

    lax.fori_loop(0, 64, start, 0)
    lax.fori_loop(0, 64, wait, 0)


def pack(ids, cmap, child):
    return pl.pallas_call(
        pack_kernel,
        out_shape=(jax.ShapeDtypeStruct((ROWS * COLS, PART, B), F32),) * PARTS,
        in_specs=[SMEM, SMEM, VMEM],
        out_specs=(HBM,) * PARTS,
        scratch_shapes=[pltpu.SemaphoreType.DMA((64, PARTS))],
        compiler_params=params(60),
        name="pack",
    )(ids, cmap, child)


def relay_kernel(ids, cmap, *rest):
    came, outs, sems = rest[:ROWS], rest[ROWS : ROWS + COLS], rest[ROWS + COLS]
    r, c = ids[0], ids[1]
    source, goes = [], []
    for d in range(ROWS):
        src = (r + ROWS - d) % ROWS
        child = src // 4 * 4 + c // 4
        _, entry = find(cmap, child, src % 4, lambda v: v // 16 == r)
        source.append(src // 4)
        goes.append((entry % 16 - c + COLS) % COLS)

    def each(act):
        for d in range(ROWS):
            for e in range(COLS):

                @pl.when(goes[d] == e)
                def _():
                    act(pltpu.make_async_copy(came[d].at[0], outs[e].at[source[d]], sems.at[d]))

    each(lambda m: m.start())
    each(lambda m: m.wait())


def relay(ids, cmap, came):
    return pl.pallas_call(
        relay_kernel,
        out_shape=(jax.ShapeDtypeStruct((2, B, B), F32),) * COLS,
        in_specs=[SMEM, SMEM] + [VMEM] * ROWS,
        out_specs=(HBM,) * COLS,
        scratch_shapes=[pltpu.SemaphoreType.DMA((ROWS,))],
        compiler_params=params(12),
        name="relay",
    )(ids, cmap, *came)


def relay_diag_kernel(ids, cmap, *rest):
    came, out = rest[:ROWS], rest[ROWS]
    r, c = ids[0], ids[1]
    for d in range(ROWS):
        src = (r + ROWS - d) % ROWS
        child = src // 4 * 4 + c // 4
        at, _ = find(cmap, child, src % 4, lambda v: v == r)

        @pl.when(at >= 0)
        def _():
            out[src // 4] = came[d][1]


def relay_diag(ids, cmap, came):
    return pl.pallas_call(
        relay_diag_kernel,
        out_shape=jax.ShapeDtypeStruct((2, B, B), F32),
        in_specs=[SMEM, SMEM] + [VMEM] * ROWS,
        out_specs=VMEM,
        compiler_params=params(12),
        name="relay_diag",
    )(ids, cmap, *came)


def listed(cmap, child, wanted):
    hit = lax.fori_loop(
        0, 32, lambda n, h: h | (cmap[child, n] == wanted).astype(jnp.int32), jnp.int32(0)
    )
    return hit > 0


def add_block(cmap, child, group, ok, part, out):
    at, entry = find(cmap, child, group, lambda v: v < 8)

    @pl.when(ok & (at >= 0))
    def _():
        where = block(jnp.minimum(entry, 7))
        out[:, where] = out[:, where] + part[...]


def owner_kernel(ids, cmap, start, *rest):
    came, out = rest[:COLS], rest[COLS]
    r, c = ids[0], ids[1]
    for k in range(NB):
        out[:, k * B : (k + 1) * B] = start[k * B : (k + 1) * B, :].T
    ok = [listed(cmap, child, r * COLS + c) for child in range(8)]
    for d in range(COLS):
        src = (c + COLS - d) % COLS
        for half in range(2):
            hit = jnp.bool_(False)
            for q in range(4):
                hit = hit | (ok[half * 4 + q] & (src // 4 == q))
            add_block(cmap, half * 4 + src // 4, src % 4, hit, came[d].at[half], out)


def owner_rows(ids, cmap, start, came):
    return pl.pallas_call(
        owner_kernel,
        out_shape=jax.ShapeDtypeStruct((B, W), F32),
        in_specs=[SMEM, SMEM, VMEM] + [VMEM] * COLS,
        out_specs=VMEM,
        compiler_params=params(24),
        name="owner_rows",
    )(ids, cmap, start, *came)


def diag_kernel(ids, cmap, parent, came, out):
    for k in range(NB):
        out[:, k * B : (k + 1) * B] = parent[k]
    for child in range(8):
        ok = listed(cmap, child, ids[0])
        for g in range(4):
            add_block(cmap, child, g, ok, came.at[child % 4 * 4 + g, child // 4], out)


def diag_rows(ids, cmap, parent, came):
    return pl.pallas_call(
        diag_kernel,
        out_shape=jax.ShapeDtypeStruct((B, W), F32),
        in_specs=[SMEM, SMEM, VMEM, VMEM],
        out_specs=VMEM,
        compiler_params=params(24),
        name="diag_rows",
    )(ids, cmap, parent, came)


def spread_lane(x, k):
    return jnp.broadcast_to(x[:, k : k + 1], (8, B))


def spread_sub(x, k):
    return jnp.broadcast_to(x[k : k + 1, :], (8, B))


def eliminate_block(strips):
    sub = lax.broadcasted_iota(jnp.int32, (8, B), 0)
    lane = lax.broadcasted_iota(jnp.int32, (8, B), 1)
    strips = list(strips)
    for m in range(16):
        first = 8 * m
        inside = (lane >= first) & (lane < first + 8)
        w = strips[m]
        cols = [spread_lane(w, first + k) for k in range(8)]
        scales, rows, mults = [], [], []
        for k in range(8):
            rs = lax.rsqrt(spread_sub(cols[k], k))
            row = jnp.where(lane == first + k, rs, spread_sub(w, k) * rs)
            p = cols[k] * rs
            mult = [spread_sub(p, q) for q in range(k + 1, 8)]
            for n, q in enumerate(range(k + 1, 8)):
                cols[q] = cols[q] - p * mult[n]
            rest = jnp.where(lane == first + k, 0.0, w) - p * row
            w = jnp.where(sub > k, rest, jnp.where(sub == k, row, w))
            scales.append(rs)
            rows.append(jnp.where(inside & (lane > first + k), 0.0, row))
            mults.append(mult)
        strips[m] = w
        for s in range(m + 1, 16):
            v = strips[s]
            below = [spread_lane(v, first + k) for k in range(8)]
            v = jnp.where(inside, 0.0, v)
            for k in range(8):
                p = below[k] * scales[k]
                v = v - p * rows[k]
                for n, q in enumerate(range(k + 1, 8)):
                    below[q] = below[q] - p * mults[k][n]
            strips[s] = v
    return strips


def dot32(a, b, ca, cb):
    return lax.dot_general(
        a, b, (((ca,), (cb,)), ((), ())), precision=lax.Precision.HIGHEST, preferred_element_type=F32
    )


def factor_kernel(a_ref, w_ref, d_ref, q_ref):
    row = lax.broadcasted_iota(jnp.int32, (B, B), 0)
    col = lax.broadcasted_iota(jnp.int32, (B, B), 1)
    w_ref[...] = a_ref[...]

    def step(kb, _):
        here = block(kb)
        d_ref[...] = w_ref[here, here]
        strips = eliminate_block([d_ref[8 * s : 8 * s + 8, :] for s in range(16)])
        for s in range(16):
            d_ref[8 * s : 8 * s + 8, :] = strips[s]
        inverse = jnp.where(row >= col, d_ref[...], 0.0)
        q_ref[...] = dot32(inverse, w_ref[here, :], 1, 0)
        q_ref[:, here] = inverse

        def below(i, _):
            rows = block(i)
            w_ref[rows, here] = jnp.zeros((B, B), F32)
            w_ref[rows, :] = w_ref[rows, :] - dot32(q_ref[:, rows], q_ref[...], 0, 0)
            return 0

        lax.fori_loop(kb + 1, NB, below, 0)
        w_ref[here, :] = q_ref[...]
        w_ref[here, here] = d_ref[...]
        return 0

    lax.fori_loop(0, NB, step, 0)


def factor(a):
    return pl.pallas_call(
        factor_kernel,
        out_shape=jax.ShapeDtypeStruct((W, W), F32),
        in_specs=[VMEM],
        out_specs=VMEM,
        scratch_shapes=[pltpu.VMEM((B, B), F32), pltpu.VMEM((B, W), F32)],
        compiler_params=params(32),
        name="factor",
    )(a)


def halves(x):
    high = x.astype(BF16)
    return high, (x - high.astype(F32)).astype(BF16)


def dot_nt(a, b):
    return lax.dot_general(a, b, (((1,), (1,)), ((), ())), preferred_element_type=F32)


def dot3(ah, al, bh, bl):
    return dot_nt(ah, bh) + (dot_nt(ah, bl) + dot_nt(al, bh))


SOLVE = 256
CHUNK = 256


def solve_rows(raw, out, eh, el):
    xh, xl = halves(raw)
    for j in range(W // SOLVE):
        upto = (j + 1) * SOLVE
        rows = slice(j * SOLVE, upto)
        out[:, rows] = dot3(xh[:, :upto], xl[:, :upto], eh[rows, :upto], el[rows, :upto])


def update_kernel(ids, w_ref, xc_ref, xr_ref, own_ref, out_ref, eh, el, ch, cl, x):
    step = pl.program_id(0)
    r, c = ids[0], ids[1]

    @pl.when(step == 0)
    def _():
        row = lax.broadcasted_iota(jnp.int32, (B, W), 0)
        col = lax.broadcasted_iota(jnp.int32, (B, W), 1)

        def split(i, _):
            rows = block(i)
            high, low = halves(jnp.where(row + i * B >= col, w_ref[rows, :], 0.0))
            eh[rows, :] = high
            el[rows, :] = low
            return 0

        lax.fori_loop(0, NB, split, 0)

        def columns(i, _):
            rows = pl.ds(pl.multiple_of(i * CHUNK, CHUNK), CHUNK)
            solve_rows(xc_ref[rows, :], x, eh, el)
            high, low = halves(x[...])
            ch[rows, :] = high
            cl[rows, :] = low
            return 0

        lax.fori_loop(0, W // CHUNK, columns, 0)

    solve_rows(xr_ref[...], x, eh, el)
    top = (r == 0) & (step < W // CHUNK)

    @pl.when((c > 0) & top)
    def _():
        out_ref[...] = jnp.zeros_like(out_ref)

    @pl.when((c > 0) & jnp.logical_not(top))
    def _():
        high, low = halves(x[...])
        for j in range(W // SOLVE):
            cols = slice(j * SOLVE, (j + 1) * SOLVE)
            change = dot3(high, low, ch[cols, :], cl[cols, :])
            out_ref[:, cols] = own_ref[:, cols] - change

    @pl.when((c == 0) & jnp.logical_not(top))
    def _():
        out_ref[...] = x[...]

    @pl.when((c == 0) & top)
    def _():
        row = lax.broadcasted_iota(jnp.int32, (CHUNK, B), 0)
        col = lax.broadcasted_iota(jnp.int32, (CHUNK, B), 1)
        for j in range(NB):
            cols = slice(j * B, (j + 1) * B)
            rows = pl.ds(pl.multiple_of(step * CHUNK, CHUNK), CHUNK)
            above = w_ref[cols, rows].T
            here = w_ref[rows, cols]
            gap = row + step * CHUNK - (col + j * B)
            out_ref[:, cols] = jnp.where(gap > 0, above, jnp.where(gap == 0, 1.0 / here, 0.0))


def update(ids, w, xc, xr, own):
    rows = own.shape[0]
    whole = pl.BlockSpec((W, W), lambda i: (0, 0), pipeline_mode=pl.Buffered(1))
    part = pl.BlockSpec((CHUNK, W), lambda i: (i, 0))
    return pl.pallas_call(
        update_kernel,
        grid=(rows // CHUNK,),
        out_shape=jax.ShapeDtypeStruct(own.shape, F32),
        in_specs=[SMEM, whole, whole, part, part],
        out_specs=part,
        scratch_shapes=[pltpu.VMEM((W, W), BF16)] * 4 + [pltpu.VMEM((CHUNK, W), F32)],
        compiler_params=params(60),
        name="update",
    )(ids, w, xc, xr, own)


def add_kernel(ids, pattern, cmap, *rest):
    came, (own, out, tile, held, places, tile_sem, sems) = rest[:PARTS], rest[PARTS:]
    r, c = ids[0], ids[1]
    load = pltpu.make_async_copy(own, tile, tile_sem)
    load.start()

    def table(n, _):
        ra, rv = find(cmap, n // 4, n % 4, lambda v: v // 16 == r)
        ca, cv = find(cmap, n // 4, n % 4, lambda v: v // 8 == c)
        low = rv % 16
        rok = (ra >= 0) & ((r > 0) | (low >= 8))
        cok = (ca >= 0) & (c > 0)
        places[0, n] = jnp.where(rok, low, -1)
        places[1, n] = jnp.where(cok, cv % 8, -1)
        return 0

    lax.fori_loop(0, 32, table, 0)

    def copies(n):
        for part in range(PARTS):
            dst = held.at[n, pl.ds(part * PART, PART)]
            yield pltpu.make_async_copy(came[part].at[n], dst, sems.at[n, part])

    def visit(act):
        def one(n, _):
            src_r, src_c = n // COLS, n % COLS
            child = src_r // 4 * 4 + src_c // 4
            low = places[0, child * 4 + src_r % 4]
            col = places[1, child * 4 + src_c % 4]

            @pl.when((low >= 0) & (col >= 0))
            def _():
                act(n, low, col)

            return 0

        lax.fori_loop(0, ROWS * COLS, one, 0)

    def begin(n, low, col):
        for m in copies(n):
            m.start()

    def finish(n, low, col):
        for m in copies(n):
            m.wait()
        rows, cols = block(low), block(col)
        tile[rows, cols] = tile[rows, cols] + held[n]

    visit(begin)
    load.wait()

    def mask(n, _):
        i, j = n // 8, n % 8

        @pl.when(pattern[i, j] == 0)
        def _():
            tile[block(i), block(j)] = jnp.zeros((B, B), F32)

        return 0

    lax.fori_loop(0, 128, mask, 0)
    visit(finish)
    store = pltpu.make_async_copy(tile, out, tile_sem)
    store.start()
    store.wait()


def add(ids, pattern, cmap, came, own):
    return pl.pallas_call(
        add_kernel,
        out_shape=jax.ShapeDtypeStruct(own.shape, F32),
        in_specs=[SMEM, SMEM, SMEM] + [HBM] * (PARTS + 1),
        out_specs=HBM,
        scratch_shapes=[
            pltpu.VMEM(own.shape, F32),
            pltpu.VMEM((ROWS * COLS, B, B), F32),
            pltpu.SMEM((2, 32), jnp.int32),
            pltpu.SemaphoreType.DMA(()),
            pltpu.SemaphoreType.DMA((ROWS * COLS, PARTS)),
        ],
        compiler_params=params(60),
        name="add",
    )(ids, pattern, cmap, *came, own)


def at(r, c):
    return r * COLS + c


def shift(parts, axis, count):
    return [parts[0]] + [
        lax.ppermute(parts[d], axis, [(k, (k + d) % count) for k in range(count)])
        for d in range(1, count)
    ]


def after(value, first):
    return lax.optimization_barrier((value, first))[0]


def body(child, own, pattern, cmap):
    ids = jnp.stack([lax.axis_index("prow"), lax.axis_index("pcol")]).astype(jnp.int32)

    row, col = ids[0], ids[1]
    small = pack_small(ids, cmap, child)
    bulk = pack(ids, cmap, child)
    came = shift(small, "prow", ROWS)

    keep = pattern[:NB].astype(F32)
    start = None
    turn = (col % NB - (2 * row + col // NB) // 2) % NB
    for k in range(NB):
        n = (k + col // 2) % NB
        mask = jnp.repeat(lax.dynamic_slice_in_dim(keep, n, 1, 1), B, axis=0)
        piece = lax.dynamic_slice_in_dim(own, n * B, B, 1)[:W] * mask
        moves = [(at(0, c), at(c // 2, 8 * (c % 2) + (k + c // 2) % NB)) for c in range(COLS)]
        piece = lax.ppermute(piece, AXES, moves)
        start = jnp.where(turn == k, piece, 0.0 if start is None else start)
    top = jnp.where(row == 0, start, 0.0).reshape(NB, B, B)
    parent = lax.psum_scatter(top, "prow", scatter_dimension=0, tiled=True)
    parent = lax.all_gather(parent, "pcol", axis=0, tiled=True)

    done = []

    def part(first, values):
        sent = after(bulk[len(done)], first)
        got = lax.all_to_all(sent, AXES, 0, 0, tiled=True)
        values, got = lax.optimization_barrier((values, got))
        done.append(got)
        return values

    diag = relay_diag(ids, cmap, came)
    diag_all = lax.all_gather(diag, "pcol", axis=0)
    owners = shift(relay(ids, cmap, part(diag, came)), "pcol", COLS)
    pivot = diag_rows(ids, cmap, parent, after(diag_all, owners))
    pivot = lax.all_gather(pivot, "prow", axis=0, tiled=True)
    owned = owner_rows(ids, cmap, start, part(done[0], owners))
    moves = [
        (at(r, c), at(c % 8, 2 * r + c // 8)) for r in range(ROWS) for c in range(COLS)
    ]
    xc = lax.ppermute(owned, AXES, moves)
    xc = lax.all_gather(xc, "prow", axis=0, tiled=True)
    xr = lax.all_gather(owned, "pcol", axis=0, tiled=True)

    w = factor(part(owned, pivot))
    w = part(done[2], w)
    base = add(ids, pattern, cmap, done, own)
    return update(ids, w, xc, xr, base)


def solution(mesh):
    return jax.shard_map(
        body,
        mesh=mesh,
        in_specs=(P("prow", "pcol"), P("prow", "pcol"), P("prow", "pcol"), P()),
        out_specs=P("prow", "pcol"),
        check_vma=False,
    )
```

time: 636 us -> 506 us (0.80)
  Pallas kernels: 310 us -> 138 us
  starting transfers between devices: 25.9 us -> 110 us
  waiting for transfers between devices: 150 us -> 111 us
    pallas_call x1, Pallas kernels: 147 us -> 7.49 us  [pack(): pl.pallas_call(pack_kernel, out_shape=(jax.ShapeDtypeStruct((ROWS * COLS,...]
    all_gather x1, waiting for transfers between devices: 101 us -> 0.02 us  [body(): xr = lax.all_gather(owned, 'pcol', axis=0, tiled=True)]
    ppermute x1 -> x22, starting transfers between devices: 0.69 us -> 83 us  [shift(): lax.ppermute(parts[d], axis, [(k, (k + d) % count) for k in range(count)])]
    pallas_call x4 -> x6, Pallas kernels: 72.2 us -> 39.6 us  [the longest x1 24.4 us: add(): pl.pallas_call(add_kernel, out_shape=jax.ShapeDtypeStruct(own.shape, F32)...]
    all_gather x2 -> x3, waiting for transfers between devices: 0.01 us -> 29.5 us  [the longest x1 29.5 us: body(): parent = lax.all_gather(parent, 'pcol', axis=0, tiled=True)]
    all_to_all x1 -> x2, waiting for transfers between devices: 0.01 us -> 27.6 us  [part(): got = lax.all_to_all(sent, AXES, 0, 0, tiled=True)]
    all_gather x1 -> x0, blocking collectives: 23.2 us -> none  [body(): diag_start = lax.all_gather(diag_start, 'pcol', axis=0, tiled=True)]
    all_to_all x3 -> x2, blocking collectives: 91.2 us -> 111 us  [part(): got = lax.all_to_all(sent, AXES, 0, 0, tiled=True)]
  transfers between devices with their start and end apart: 15 -> 39, of which waited for: 3 -> 10; matrix products, arithmetic and copies ran while one was open for 1% -> 0% of each run, Pallas kernels for 15% -> 19%
where the time goes in v2:
time: 506 us; the launch traced here: 504 us
  Pallas kernels  138 us (27%)
  waiting for transfers between devices  111 us (22%)
  blocking collectives  111 us (22%)
  starting transfers between devices  110 us (22%)
  between operations  14.9 us (3%)
  local copies, waits for them, and re-layouts  13.1 us (3%)
  other arithmetic  5.97 us (1%)
    all_to_all x2, blocking collectives, part(): got = lax.all_to_all(sent, AXES, 0, 0, tiled=True)  111 us
    ppermute x22, starting transfers between devices, shift(): lax.ppermute(parts[d], axis, [(k, (k + d) % count) for k in range(count)])  83 us
    pallas_call x1, Pallas kernels, factor(): pl.pallas_call(factor_kernel, out_shape=jax.ShapeDtypeStruct((W, W), F32)...  55.2 us
    pallas_call x1, Pallas kernels, update(): pl.pallas_call(update_kernel, grid=(rows // CHUNK,), out_shape=jax.ShapeD...  35.8 us
    all_gather x1, waiting for transfers between devices, body(): parent = lax.all_gather(parent, 'pcol', axis=0, tiled=True)  29.5 us
    all_to_all x2, waiting for transfers between devices, part(): got = lax.all_to_all(sent, AXES, 0, 0, tiled=True)  27.6 us
    pallas_call x1, Pallas kernels, add(): pl.pallas_call(add_kernel, out_shape=jax.ShapeDtypeStruct(own.shape, F32)...  24.4 us
    ppermute x1, waiting for transfers between devices, body(): xc = lax.ppermute(owned, AXES, moves)  22.7 us
  transfers between devices with their start and end apart: 39, of which 10 were waited for; matrix products, arithmetic and copies ran while one was open for 0% of the time, Pallas kernels for 19%

profile of v2, /device:TPU:14, one launch (start us, length us, event | category | flops | bytes accessed | tf_op | source)
XLA Modules:
  0.0 503.5 jit_solution(13925250189530552271)
XLA Ops:
  8.4 4.1 dynamic-slice_multiply_fusion
  13.1 1.3 collective-permute-start.1
  17.3 16.8 %collective-permute-done.1 = f32[1024,128]{1,0:T(8,128)S(1)} collective-permute-done((f32[1024,128]{1,0:T(8,128)S(1)}, f32[1024,128]{1,0:T(8,128)S(1)}, u32[]{:S(2)}, u32[]{:S(2)}) %collective-permute-start.1) | collective-permute-done | bytes 524320 | tf_op jit(solution)/shard_map/ppermute | solution.py:544
  34.1 1.5 collective-permute-start.6
  35.6 1.4 collective-permute-start.7
  37.8 1.1 broadcast_select_fusion
  39.1 2.2 copy-done
  42.4 7.8 %collective-permute-start.10 = (f32[2,128,128]{2,1,0:T(8,128)S(1)}, f32[2,128,128]{2,1,0:T(8,128)S(1)}, u32[]{:S(2)}, u32[]{:S(2)}) collective-permute-start(f32[2,128,128]{2,1,0:T(8,128)S(1)} %get-tuple-element.71), channel_id=1, source_target_pairs={{0,48},{16,64},{32,80},{48,96},{64,112},{80,0},{96,16},{112,32},{1... | collective-permute-start | bytes 393224 | tf_op jit(solution)/shard_map/ppermute | solution.py:519
  50.3 10.6 %collective-permute-start.11 = (f32[2,128,128]{2,1,0:T(8,128)S(1)}, f32[2,128,128]{2,1,0:T(8,128)S(1)}, u32[]{:S(2)}, u32[]{:S(2)}) collective-permute-start(f32[2,128,128]{2,1,0:T(8,128)S(1)} %get-tuple-element.72), channel_id=1, source_target_pairs={{0,64},{16,80},{32,96},{48,112},{64,0},{80,16},{96,32},{112,48},{1... | collective-permute-start | bytes 393224 | tf_op jit(solution)/shard_map/ppermute | solution.py:519
  60.8 5.8 %collective-permute-start.12 = (f32[2,128,128]{2,1,0:T(8,128)S(1)}, f32[2,128,128]{2,1,0:T(8,128)S(1)}, u32[]{:S(2)}, u32[]{:S(2)}) collective-permute-start(f32[2,128,128]{2,1,0:T(8,128)S(1)} %get-tuple-element.73), channel_id=1, source_target_pairs={{0,80},{16,96},{32,112},{48,0},{64,16},{80,32},{96,48},{112,64},{1... | collective-permute-start | bytes 393224 | tf_op jit(solution)/shard_map/ppermute | solution.py:519
  66.7 13.3 %collective-permute-start.13 = (f32[2,128,128]{2,1,0:T(8,128)S(1)}, f32[2,128,128]{2,1,0:T(8,128)S(1)}, u32[]{:S(2)}, u32[]{:S(2)}) collective-permute-start(f32[2,128,128]{2,1,0:T(8,128)S(1)} %get-tuple-element.74), channel_id=1, source_target_pairs={{0,96},{16,112},{32,0},{48,16},{64,32},{80,48},{96,64},{112,80},{1... | collective-permute-start | bytes 393224 | tf_op jit(solution)/shard_map/ppermute | solution.py:519
  80.5 3.8 collective-permute-start.9
  86.0 1.9 collective-permute-done.9.rest_2_
  87.9 1.6 relay_diag.1
  89.5 7.5 %pack.1 = (f32[128,32,128]{2,1,0:T(8,128)}, f32[128,32,128]{2,1,0:T(8,128)}, f32[128,32,128]{2,1,0:T(8,128)}, f32[128,32,128]{2,1,0:T(8,128)}) custom-call(s32[2]{0:T(128)} %copy-done.7, s32[8,32]{1,0:T(8,128)} %cmap.13, f32[1024,1024]{1,0:T(8,128)} %child.3), custom_call_target="tpu_custom_call" | custom-call | tf_op jit(solution)/shard_map/pack/pallas_call | solution.py:104
  97.0 11.0 %all-to-all-start = ((f32[128,32,128]{2,1,0:T(8,128)}), f32[128,32,128]{2,1,0:T(8,128)}, u32[]{:S(2)}, u32[]{:S(2)}) async-start(f32[128,32,128]{2,1,0:T(8,128)} %get-tuple-element.77), calls=%async_computation.1 | async-start | bytes 4194304 | tf_op jit(solution)/shard_map/all_to_all | solution.py:554
  108.7 27.6 %all-to-all-done.rest_0_ = f32[128,32,128]{2,1,0:T(8,128)} async-done(((f32[128,32,128]{2,1,0:T(8,128)}), f32[128,32,128]{2,1,0:T(8,128)}, u32[]{:S(2)}, u32[]{:S(2)}) %all-to-all-start) | async-done | bytes 2097184 | tf_op jit(solution)/shard_map/all_to_all | solution.py:554
  136.3 3.1 relay.1
  140.3 1.2 collective-permute-start.16
  141.5 1.4 collective-permute-start.17
  143.0 1.5 collective-permute-start.18
  144.5 2.1 collective-permute-start.19
  146.6 4.5 collective-permute-done.15.rest_1_
  151.1 2.1 collective-permute-done.16.rest_2_
  153.3 1.5 collective-permute-start.21
  154.8 3.7 collective-permute-start.22
  158.5 2.1 collective-permute-start.23
  160.6 14.1 %collective-permute-start.24 = (f32[2,128,128]{2,1,0:T(8,128)S(1)}, f32[2,128,128]{2,1,0:T(8,128)S(1)}, u32[]{:S(2)}, u32[]{:S(2)}) collective-permute-start(f32[2,128,128]{2,1,0:T(8,128)S(1)} %get-tuple-element.96), channel_id=1, source_target_pairs={{0,10},{1,11},{2,12},{3,13},{4,14},{5,15},{6,0},{7,1},{8,2},{9,3},... | collective-permute-start | bytes 393224 | tf_op jit(solution)/shard_map/ppermute | solution.py:519
  174.7 2.2 collective-permute-start.26
  177.0 5.3 %collective-permute-start.28 = (f32[2,128,128]{2,1,0:T(8,128)S(1)}, f32[2,128,128]{2,1,0:T(8,128)S(1)}, u32[]{:S(2)}, u32[]{:S(2)}) collective-permute-start(f32[2,128,128]{2,1,0:T(8,128)S(1)} %get-tuple-element.100), channel_id=1, source_target_pairs={{0,14},{1,15},{2,0},{3,1},{4,2},{5,3},{6,4},{7,5},{8,6},{9,7},{10,... | collective-permute-start | bytes 393224 | tf_op jit(solution)/shard_map/ppermute | solution.py:519
  182.2 4.9 collective-permute-start.29
  187.2 2.5 collective-permute-done.29.rest_15_
  189.7 29.5 %all-gather.7.cloned.1.call-done.parent = f32[16,128,128]{2,1,0:T(8,128)} async-done(((f32[1,128,128]{2,1,0:T(8,128)}), f32[16,128,128]{2,1,0:T(8,128)}) %all-gather.7.cloned.1.call-update) | async-done | bytes 1048592 | tf_op jit(solution)/shard_map/all_gather | solution.py:548
  219.2 1.6 copy-done.3
  220.8 1.2 copy-done.4
  222.0 4.3 diag_rows.1
  226.4 53.0 %all_to_all.20.rest_1_ = f32[128,32,128]{2,1,0:T(8,128)} all-to-all(f32[128,32,128]{2,1,0:T(8,128)} %get-tuple-element.106), channel_id=1, replica_groups=mesh['prow'=8,'pcol'=16] {'prow','pcol'}, dimensions={0} | all-to-all | bytes 4194304 | tf_op jit(solution)/shard_map/all_to_all | solution.py:554
  279.4 5.2 %owner_rows.1 = f32[128,1024]{1,0:T(8,128)} custom-call(s32[2]{0:T(128)S(1)} %copy-done.8, s32[8,32]{1,0:T(8,128)S(1)} %copy-done.6, f32[1024,128]{1,0:T(8,128)S(1)} %get-tuple-element.132.start, f32[2,128,128]{2,1,0:T(8,128)S(1)} %get-tuple-element.107.rest_0_, f32[2,128,128]{2,1,0:T(8,128)S(1)} %collective-permute-done.15.rest_1_, ...), custom_call_target="tpu_custom_call" | custom-call | tf_op jit(solution)/shard_map/owner_rows/pallas_call | solution.py:206
  284.6 2.2 collective-permute-start.30
  286.8 22.7 %collective-permute-done.30 = f32[128,1024]{1,0:T(8,128)S(1)} collective-permute-done((f32[128,1024]{1,0:T(8,128)}, f32[128,1024]{1,0:T(8,128)S(1)}, u32[]{:S(2)}, u32[]{:S(2)}) %collective-permute-start.30) | collective-permute-done | bytes 524320 | tf_op jit(solution)/shard_map/ppermute | solution.py:568
  310.9 57.8 %all_to_all.21.rest_2_ = f32[128,32,128]{2,1,0:T(8,128)} all-to-all(f32[128,32,128]{2,1,0:T(8,128)} %get-tuple-element.123), channel_id=1, replica_groups=mesh['prow'=8,'pcol'=16] {'prow','pcol'}, dimensions={0} | all-to-all | bytes 4194304 | tf_op jit(solution)/shard_map/all_to_all | solution.py:554
  368.7 6.1 %all-to-all-start.3 = ((f32[128,32,128]{2,1,0:T(8,128)}), f32[128,32,128]{2,1,0:T(8,128)S(1)}, u32[]{:S(2)}, u32[]{:S(2)}) async-start(f32[128,32,128]{2,1,0:T(8,128)} %get-tuple-element.127), calls=%async_computation.4 | async-start | bytes 4194304 | tf_op jit(solution)/shard_map/all_to_all | solution.py:554
  375.4 2.2 copy-done.2
  377.6 55.2 %factor.1.w_ref = f32[1024,1024]{1,0:T(8,128)S(1)} custom-call(f32[1024,1024]{1,0:T(8,128)S(1)} %copy-done.2), custom_call_target="tpu_custom_call" | custom-call | tf_op jit(solution)/shard_map/factor/pallas_call | solution.py:316
  432.8 2.0 copy-done.1
  434.8 1.3 copy-done.9
  436.2 24.4 %add.146.own_ref = f32[2048,1024]{1,0:T(8,128)} custom-call(s32[2]{0:T(128)} %copy-done.7, s32[16,8]{1,0:T(8,128)} %copy.6.pattern, s32[8,32]{1,0:T(8,128)} %cmap.13, f32[128,32,128]{2,1,0:T(8,128)} %all-to-all-done.rest_0_, f32[128,32,128]{2,1,0:T(8,128)} %all_to_all.20.rest_1_, f32[128,32,128]{2,1,0:T(8,128)} %all_to_all.21.rest_2_, ...), custom_call_target="tpu_custom_call" | custom-call | tf_op jit(solution)/shard_map/add/pallas_call | solution.py:496
  460.6 35.8 %update.1 = f32[2048,1024]{1,0:T(8,128)} custom-call(s32[2]{0:T(128)} %copy-done.7, f32[1024,1024]{1,0:T(8,128)} %copy-done.1, f32[1024,1024]{1,0:T(8,128)} %all-gather.11.cloned.1.call-done.xc_ref, f32[2048,1024]{1,0:T(8,128)} %all-gather.13.cloned.1.call-done.xr_ref, f32[2048,1024]{1,0:T(8,128)} %add.146.own_ref), custom_call_target="tpu_custom_call" | custom-call | tf_op jit(solution)/shard_map/update/pallas_call | solution.py:416
  (83 shorter events, 12.6 us)
Async XLA Ops:
  7.4 100.7 %reduce-scatter.2.cloned.1.call-start = ((), (), s32[]{:S(2)}) async-start(), calls=%async_computation.5 | async-start | bytes 589824 | tf_op jit(solution)/shard_map/reduce_scatter | solution.py:547
  12.4 26.7 %copy-start.5 = (s32[8,32]{1,0:T(8,128)S(1)}, s32[8,32]{1,0:T(8,128)}, u32[]{:S(2)}) copy-start(s32[8,32]{1,0:T(8,128)} %cmap.13) | copy-start | bytes 3076
  12.4 4.1 collective-permute-start
  13.1 21.0 %collective-permute-start.1 = (f32[1024,128]{1,0:T(8,128)S(1)}, f32[1024,128]{1,0:T(8,128)S(1)}, u32[]{:S(2)}, u32[]{:S(2)}) collective-permute-start(f32[1024,128]{1,0:T(8,128)S(1)} %get-tuple-element.139), channel_id=1, source_target_pairs={{0,6},{1,14},{2,23},{3,31},{4,32},{5,40},{6,49},{7,57},{8,66},{9,7... | collective-permute-start | bytes 1572872 | tf_op jit(solution)/shard_map/ppermute | solution.py:544
  14.4 21.1 %collective-permute-start.2 = (f32[1024,128]{1,0:T(8,128)S(1)}, f32[1024,128]{1,0:T(8,128)S(1)}, u32[]{:S(2)}, u32[]{:S(2)}) collective-permute-start(f32[1024,128]{1,0:T(8,128)S(1)} %get-tuple-element.138), channel_id=1, source_target_pairs={{0,5},{1,13},{2,22},{3,30},{4,39},{5,47},{6,48},{7,56},{8,65},{9,7... | collective-permute-start | bytes 1572872 | tf_op jit(solution)/shard_map/ppermute | solution.py:544
  15.1 21.9 %collective-permute-start.3 = (f32[1024,128]{1,0:T(8,128)}, f32[1024,128]{1,0:T(8,128)S(1)}, u32[]{:S(2)}, u32[]{:S(2)}) collective-permute-start(f32[1024,128]{1,0:T(8,128)} %get-tuple-element.137), channel_id=1, source_target_pairs={{0,4},{1,12},{2,21},{3,29},{4,38},{5,46},{6,55},{7,63},{8,64},{9,7... | collective-permute-start | bytes 1572872 | tf_op jit(solution)/shard_map/ppermute | solution.py:544
  15.8 21.2 %collective-permute-start.4 = (f32[1024,128]{1,0:T(8,128)}, f32[1024,128]{1,0:T(8,128)S(1)}, u32[]{:S(2)}, u32[]{:S(2)}) collective-permute-start(f32[1024,128]{1,0:T(8,128)} %get-tuple-element.136), channel_id=1, source_target_pairs={{0,3},{1,11},{2,20},{3,28},{4,37},{5,45},{6,54},{7,62},{8,71},{9,7... | collective-permute-start | bytes 1572872 | tf_op jit(solution)/shard_map/ppermute | solution.py:544
  16.6 20.5 %collective-permute-start.5 = (f32[1024,128]{1,0:T(8,128)}, f32[1024,128]{1,0:T(8,128)S(1)}, u32[]{:S(2)}, u32[]{:S(2)}) collective-permute-start(f32[1024,128]{1,0:T(8,128)} %get-tuple-element.135), channel_id=1, source_target_pairs={{0,2},{1,10},{2,19},{3,27},{4,36},{5,44},{6,53},{7,61},{8,70},{9,7... | collective-permute-start | bytes 1572872 | tf_op jit(solution)/shard_map/ppermute | solution.py:544
  34.1 3.0 collective-permute-start.6
  35.6 2.3 collective-permute-start.7
  39.0 150.7 %all-gather.15.cloned.1.call-start = ((), (), s32[]{:S(2)}) async-start(), calls=%async_computation.10 | async-start | bytes 2228224 | tf_op jit(solution)/shard_map/all_gather | solution.py:560
  39.1 2.2 copy-start
  41.3 48.2 %copy-start.7 = (s32[2]{0:T(128)}, s32[2]{0:T(128)S(1)}, u32[]{:S(2)}) copy-start(s32[2]{0:T(128)S(1)} %pad_add_fusion.ids) | copy-start | bytes 28
  42.4 37.9 %collective-permute-start.10 = (f32[2,128,128]{2,1,0:T(8,128)S(1)}, f32[2,128,128]{2,1,0:T(8,128)S(1)}, u32[]{:S(2)}, u32[]{:S(2)}) collective-permute-start(f32[2,128,128]{2,1,0:T(8,128)S(1)} %get-tuple-element.71), channel_id=1, source_target_pairs={{0,48},{16,64},{32,80},{48,96},{64,112},{80,0},{96,16},{112,32},{1... | collective-permute-start | bytes 393224 | tf_op jit(solution)/shard_map/ppermute | solution.py:519
  50.3 30.3 %collective-permute-start.11 = (f32[2,128,128]{2,1,0:T(8,128)S(1)}, f32[2,128,128]{2,1,0:T(8,128)S(1)}, u32[]{:S(2)}, u32[]{:S(2)}) collective-permute-start(f32[2,128,128]{2,1,0:T(8,128)S(1)} %get-tuple-element.72), channel_id=1, source_target_pairs={{0,64},{16,80},{32,96},{48,112},{64,0},{80,16},{96,32},{112,48},{1... | collective-permute-start | bytes 393224 | tf_op jit(solution)/shard_map/ppermute | solution.py:519
  60.8 23.5 %collective-permute-start.12 = (f32[2,128,128]{2,1,0:T(8,128)S(1)}, f32[2,128,128]{2,1,0:T(8,128)S(1)}, u32[]{:S(2)}, u32[]{:S(2)}) collective-permute-start(f32[2,128,128]{2,1,0:T(8,128)S(1)} %get-tuple-element.73), channel_id=1, source_target_pairs={{0,80},{16,96},{32,112},{48,0},{64,16},{80,32},{96,48},{112,64},{1... | collective-permute-start | bytes 393224 | tf_op jit(solution)/shard_map/ppermute | solution.py:519
  66.7 18.7 %collective-permute-start.13 = (f32[2,128,128]{2,1,0:T(8,128)S(1)}, f32[2,128,128]{2,1,0:T(8,128)S(1)}, u32[]{:S(2)}, u32[]{:S(2)}) collective-permute-start(f32[2,128,128]{2,1,0:T(8,128)S(1)} %get-tuple-element.74), channel_id=1, source_target_pairs={{0,96},{16,112},{32,0},{48,16},{64,32},{80,48},{96,64},{112,80},{1... | collective-permute-start | bytes 393224 | tf_op jit(solution)/shard_map/ppermute | solution.py:519
  80.0 5.3 %collective-permute-start.14 = (f32[2,128,128]{2,1,0:T(8,128)S(1)}, f32[2,128,128]{2,1,0:T(8,128)S(1)}, u32[]{:S(2)}, u32[]{:S(2)}) collective-permute-start(f32[2,128,128]{2,1,0:T(8,128)S(1)} %get-tuple-element.75), channel_id=1, source_target_pairs={{0,112},{16,0},{32,16},{48,32},{64,48},{80,64},{96,80},{112,96},{1... | collective-permute-start | bytes 393224 | tf_op jit(solution)/shard_map/ppermute | solution.py:519
  80.4 5.6 %collective-permute-start.8 = (f32[2,128,128]{2,1,0:T(8,128)S(1)}, f32[2,128,128]{2,1,0:T(8,128)S(1)}, u32[]{:S(2)}, u32[]{:S(2)}) collective-permute-start(f32[2,128,128]{2,1,0:T(8,128)S(1)} %get-tuple-element.69), channel_id=1, source_target_pairs={{0,16},{16,32},{32,48},{48,64},{64,80},{80,96},{96,112},{112,0},{1... | collective-permute-start | bytes 393224 | tf_op jit(solution)/shard_map/ppermute | solution.py:519
  80.5 7.4 %collective-permute-start.9 = (f32[2,128,128]{2,1,0:T(8,128)S(1)}, f32[2,128,128]{2,1,0:T(8,128)S(1)}, u32[]{:S(2)}, u32[]{:S(2)}) collective-permute-start(f32[2,128,128]{2,1,0:T(8,128)S(1)} %get-tuple-element.70), channel_id=1, source_target_pairs={{0,32},{16,48},{32,64},{48,80},{64,96},{80,112},{96,0},{112,16},{1... | collective-permute-start | bytes 393224 | tf_op jit(solution)/shard_map/ppermute | solution.py:519
  89.5 46.8 %copy-start.6 = (s32[8,32]{1,0:T(8,128)S(1)}, s32[8,32]{1,0:T(8,128)}, u32[]{:S(2)}) copy-start(s32[8,32]{1,0:T(8,128)} %cmap.13) | copy-start | bytes 3076
  97.0 39.3 %copy-start.8 = (s32[2]{0:T(128)S(1)}, s32[2]{0:T(128)}, u32[]{:S(2)}) copy-start(s32[2]{0:T(128)} %copy-done.7) | copy-start | bytes 28
  97.0 39.2 %all-to-all-start = ((f32[128,32,128]{2,1,0:T(8,128)}), f32[128,32,128]{2,1,0:T(8,128)}, u32[]{:S(2)}, u32[]{:S(2)}) async-start(f32[128,32,128]{2,1,0:T(8,128)} %get-tuple-element.77), calls=%async_computation.1 | async-start | bytes 4194304 | tf_op jit(solution)/shard_map/all_to_all | solution.py:554
  108.0 111.2 %all-gather.7.cloned.1.call-start = ((), (), s32[]{:S(2)}) async-start(), calls=%async_computation.6 | async-start | bytes 1114112 | tf_op jit(solution)/shard_map/all_gather | solution.py:548
  108.6 260.1 %all-gather.9.cloned.1.call-start = ((), (), s32[]{:S(2)}) async-start(), calls=%async_computation.7 | async-start | bytes 4718592 | tf_op jit(solution)/shard_map/all_gather | solution.py:563
  139.4 11.8 %collective-permute-start.15 = (f32[2,128,128]{2,1,0:T(8,128)S(1)}, f32[2,128,128]{2,1,0:T(8,128)S(1)}, u32[]{:S(2)}, u32[]{:S(2)}) collective-permute-start(f32[2,128,128]{2,1,0:T(8,128)S(1)} %get-tuple-element.87), channel_id=1, source_target_pairs={{0,1},{1,2},{2,3},{3,4},{4,5},{5,6},{6,7},{7,8},{8,9},{9,10},{10,1... | collective-permute-start | bytes 393224 | tf_op jit(solution)/shard_map/ppermute | solution.py:519
  140.3 13.0 %collective-permute-start.16 = (f32[2,128,128]{2,1,0:T(8,128)S(1)}, f32[2,128,128]{2,1,0:T(8,128)S(1)}, u32[]{:S(2)}, u32[]{:S(2)}) collective-permute-start(f32[2,128,128]{2,1,0:T(8,128)S(1)} %get-tuple-element.88), channel_id=1, source_target_pairs={{0,2},{1,3},{2,4},{3,5},{4,6},{5,7},{6,8},{7,9},{8,10},{9,11},{10,... | collective-permute-start | bytes 393224 | tf_op jit(solution)/shard_map/ppermute | solution.py:519
  141.5 13.2 %collective-permute-start.17 = (f32[2,128,128]{2,1,0:T(8,128)S(1)}, f32[2,128,128]{2,1,0:T(8,128)S(1)}, u32[]{:S(2)}, u32[]{:S(2)}) collective-permute-start(f32[2,128,128]{2,1,0:T(8,128)S(1)} %get-tuple-element.89), channel_id=1, source_target_pairs={{0,3},{1,4},{2,5},{3,6},{4,7},{5,8},{6,9},{7,10},{8,11},{9,12},{10... | collective-permute-start | bytes 393224 | tf_op jit(solution)/shard_map/ppermute | solution.py:519
  143.0 15.5 %collective-permute-start.18 = (f32[2,128,128]{2,1,0:T(8,128)S(1)}, f32[2,128,128]{2,1,0:T(8,128)S(1)}, u32[]{:S(2)}, u32[]{:S(2)}) collective-permute-start(f32[2,128,128]{2,1,0:T(8,128)S(1)} %get-tuple-element.90), channel_id=1, source_target_pairs={{0,4},{1,5},{2,6},{3,7},{4,8},{5,9},{6,10},{7,11},{8,12},{9,13},{1... | collective-permute-start | bytes 393224 | tf_op jit(solution)/shard_map/ppermute | solution.py:519
  144.5 16.1 %collective-permute-start.19 = (f32[2,128,128]{2,1,0:T(8,128)S(1)}, f32[2,128,128]{2,1,0:T(8,128)S(1)}, u32[]{:S(2)}, u32[]{:S(2)}) collective-permute-start(f32[2,128,128]{2,1,0:T(8,128)S(1)} %get-tuple-element.91), channel_id=1, source_target_pairs={{0,5},{1,6},{2,7},{3,8},{4,9},{5,10},{6,11},{7,12},{8,13},{9,14},{... | collective-permute-start | bytes 393224 | tf_op jit(solution)/shard_map/ppermute | solution.py:519
  151.1 23.5 %collective-permute-start.20 = (f32[2,128,128]{2,1,0:T(8,128)S(1)}, f32[2,128,128]{2,1,0:T(8,128)S(1)}, u32[]{:S(2)}, u32[]{:S(2)}) collective-permute-start(f32[2,128,128]{2,1,0:T(8,128)S(1)} %get-tuple-element.92), channel_id=1, source_target_pairs={{0,6},{1,7},{2,8},{3,9},{4,10},{5,11},{6,12},{7,13},{8,14},{9,15},... | collective-permute-start | bytes 393224 | tf_op jit(solution)/shard_map/ppermute | solution.py:519
  153.3 21.4 %collective-permute-start.21 = (f32[2,128,128]{2,1,0:T(8,128)S(1)}, f32[2,128,128]{2,1,0:T(8,128)S(1)}, u32[]{:S(2)}, u32[]{:S(2)}) collective-permute-start(f32[2,128,128]{2,1,0:T(8,128)S(1)} %get-tuple-element.93), channel_id=1, source_target_pairs={{0,7},{1,8},{2,9},{3,10},{4,11},{5,12},{6,13},{7,14},{8,15},{9,0},... | collective-permute-start | bytes 393224 | tf_op jit(solution)/shard_map/ppermute | solution.py:519
  154.8 22.0 %collective-permute-start.22 = (f32[2,128,128]{2,1,0:T(8,128)S(1)}, f32[2,128,128]{2,1,0:T(8,128)S(1)}, u32[]{:S(2)}, u32[]{:S(2)}) collective-permute-start(f32[2,128,128]{2,1,0:T(8,128)S(1)} %get-tuple-element.94), channel_id=1, source_target_pairs={{0,8},{1,9},{2,10},{3,11},{4,12},{5,13},{6,14},{7,15},{8,0},{9,1},... | collective-permute-start | bytes 393224 | tf_op jit(solution)/shard_map/ppermute | solution.py:519
  158.5 18.5 %collective-permute-start.23 = (f32[2,128,128]{2,1,0:T(8,128)S(1)}, f32[2,128,128]{2,1,0:T(8,128)S(1)}, u32[]{:S(2)}, u32[]{:S(2)}) collective-permute-start(f32[2,128,128]{2,1,0:T(8,128)S(1)} %get-tuple-element.95), channel_id=1, source_target_pairs={{0,9},{1,10},{2,11},{3,12},{4,13},{5,14},{6,15},{7,0},{8,1},{9,2},... | collective-permute-start | bytes 393224 | tf_op jit(solution)/shard_map/ppermute | solution.py:519
  160.6 21.7 %collective-permute-start.24 = (f32[2,128,128]{2,1,0:T(8,128)S(1)}, f32[2,128,128]{2,1,0:T(8,128)S(1)}, u32[]{:S(2)}, u32[]{:S(2)}) collective-permute-start(f32[2,128,128]{2,1,0:T(8,128)S(1)} %get-tuple-element.96), channel_id=1, source_target_pairs={{0,10},{1,11},{2,12},{3,13},{4,14},{5,15},{6,0},{7,1},{8,2},{9,3},... | collective-permute-start | bytes 393224 | tf_op jit(solution)/shard_map/ppermute | solution.py:519
  174.7 12.5 %collective-permute-start.25 = (f32[2,128,128]{2,1,0:T(8,128)S(1)}, f32[2,128,128]{2,1,0:T(8,128)S(1)}, u32[]{:S(2)}, u32[]{:S(2)}) collective-permute-start(f32[2,128,128]{2,1,0:T(8,128)S(1)} %get-tuple-element.97), channel_id=1, source_target_pairs={{0,11},{1,12},{2,13},{3,14},{4,15},{5,0},{6,1},{7,2},{8,3},{9,4},{... | collective-permute-start | bytes 393224 | tf_op jit(solution)/shard_map/ppermute | solution.py:519
  174.7 12.5 %collective-permute-start.26 = (f32[2,128,128]{2,1,0:T(8,128)S(1)}, f32[2,128,128]{2,1,0:T(8,128)S(1)}, u32[]{:S(2)}, u32[]{:S(2)}) collective-permute-start(f32[2,128,128]{2,1,0:T(8,128)S(1)} %get-tuple-element.98), channel_id=1, source_target_pairs={{0,12},{1,13},{2,14},{3,15},{4,0},{5,1},{6,2},{7,3},{8,4},{9,5},{1... | collective-permute-start | bytes 393224 | tf_op jit(solution)/shard_map/ppermute | solution.py:519
  176.8 10.4 %collective-permute-start.27 = (f32[2,128,128]{2,1,0:T(8,128)S(1)}, f32[2,128,128]{2,1,0:T(8,128)S(1)}, u32[]{:S(2)}, u32[]{:S(2)}) collective-permute-start(f32[2,128,128]{2,1,0:T(8,128)S(1)} %get-tuple-element.99), channel_id=1, source_target_pairs={{0,13},{1,14},{2,15},{3,0},{4,1},{5,2},{6,3},{7,4},{8,5},{9,6},{10... | collective-permute-start | bytes 393224 | tf_op jit(solution)/shard_map/ppermute | solution.py:519
  177.0 10.2 %collective-permute-start.28 = (f32[2,128,128]{2,1,0:T(8,128)S(1)}, f32[2,128,128]{2,1,0:T(8,128)S(1)}, u32[]{:S(2)}, u32[]{:S(2)}) collective-permute-start(f32[2,128,128]{2,1,0:T(8,128)S(1)} %get-tuple-element.100), channel_id=1, source_target_pairs={{0,14},{1,15},{2,0},{3,1},{4,2},{5,3},{6,4},{7,5},{8,6},{9,7},{10,... | collective-permute-start | bytes 393224 | tf_op jit(solution)/shard_map/ppermute | solution.py:519
  182.2 7.5 %collective-permute-start.29 = (f32[2,128,128]{2,1,0:T(8,128)S(1)}, f32[2,128,128]{2,1,0:T(8,128)S(1)}, u32[]{:S(2)}, u32[]{:S(2)}) collective-permute-start(f32[2,128,128]{2,1,0:T(8,128)S(1)} %get-tuple-element.101), channel_id=1, source_target_pairs={{0,15},{1,0},{2,1},{3,2},{4,3},{5,4},{6,5},{7,6},{8,7},{9,8},{10,9... | collective-permute-start | bytes 393224 | tf_op jit(solution)/shard_map/ppermute | solution.py:519
  219.2 1.6 copy-start.3
  226.3 234.2 %all-gather.11.cloned.1.call-start = ((), (), s32[]{:S(2)}) async-start(), calls=%async_computation.8 | async-start | bytes 4718592 | tf_op jit(solution)/shard_map/all_gather | solution.py:569
  284.6 24.8 %collective-permute-start.30 = (f32[128,1024]{1,0:T(8,128)}, f32[128,1024]{1,0:T(8,128)S(1)}, u32[]{:S(2)}, u32[]{:S(2)}) collective-permute-start(f32[128,1024]{1,0:T(8,128)} %owner_rows.1), channel_id=1, source_target_pairs={{0,0},{1,16},{2,32},{3,48},{4,64},{5,80},{6,96},{7,112},{8,1},{9,1... | collective-permute-start | bytes 1572872 | tf_op jit(solution)/shard_map/ppermute | solution.py:568
  310.3 150.3 %all-gather.13.cloned.1.call-start = ((), (), s32[]{:S(2)}) async-start(), calls=%async_computation.9 | async-start | bytes 8912896 | tf_op jit(solution)/shard_map/all_gather | solution.py:570
  310.9 63.9 %copy-start.12 = (s32[16,8]{0,1:T(8,128)S(1)}, s32[16,8]{0,1:T(8,128)}, u32[]{:S(2)}) copy-start(s32[16,8]{0,1:T(8,128)} %param.6) | copy-start | bytes 1540
  368.7 66.1 %all-to-all-start.3 = ((f32[128,32,128]{2,1,0:T(8,128)}), f32[128,32,128]{2,1,0:T(8,128)S(1)}, u32[]{:S(2)}, u32[]{:S(2)}) async-start(f32[128,32,128]{2,1,0:T(8,128)} %get-tuple-element.127), calls=%async_computation.4 | async-start | bytes 4194304 | tf_op jit(solution)/shard_map/all_to_all | solution.py:554
  375.4 2.2 copy-start.2
  432.8 2.0 copy-start.1
  (4 other events, 4.2 us)
Sparse Core Ops, SparseCore 0:
  39.1 60.5 reduce-scatter.1
  226.5 48.6 all-gather.8
  310.4 53.9 all-gather.10
  366.6 90.7 all-gather.12
Sparse Core Ops, SparseCore 1:
  89.6 76.0 all-gather.14
  167.9 51.2 all-gather.6

commit v3 on v1

--- a/solution.py
+++ b/solution.py
@@ -1,5 +1,6 @@
 import jax
 import jax.numpy as jnp
+import numpy as np
 from jax import lax
 from jax.experimental import pallas as pl
 from jax.experimental.pallas import tpu as pltpu
@@ -13,7 +14,7 @@
 AXES = ("prow", "pcol")
 F32 = jnp.float32
 BF16 = jnp.bfloat16
-HBM = pl.BlockSpec(memory_space=pl.ANY)
+HBM = pl.BlockSpec(memory_space=pltpu.HBM)
 SMEM = pl.BlockSpec(memory_space=pltpu.SMEM)
 VMEM = pl.BlockSpec(memory_space=pltpu.VMEM)
 MIB = 1024 * 1024
@@ -38,52 +39,114 @@
     return at, entry
 
 
-def pack_kernel(ids, cmap, child, bulk, small, sems, small_sems):
+def scatter_plan():
+    queues = {}
+    for r in range(ROWS):
+        for c in range(1, COLS):
+            if r == 0 and c < 8:
+                move = ((0, 0), 0, c)
+            elif c % 8 < 5:
+                move = ((0, 2 * r + c // 8), 0, c % 8)
+            else:
+                move = ((r, 0), 1, c)
+            queues.setdefault(move[0], []).append((move[1], move[2], (r, c)))
+    steps = max(len(q) for q in queues.values())
+    moves = [[] for _ in range(steps)]
+    sends = np.zeros((ROWS * COLS, steps, 2), np.int32)
+    gets = np.zeros((ROWS * COLS, 2), np.int32)
+    gets[:, 0] = -1
+    gets[:, 1] = 1
+    for (r, c), queue in queues.items():
+        turn = (r + c // 2) % len(queue) if (r, c) != (0, 0) else 0
+        for step, (form, index, to) in enumerate(queue[turn:] + queue[:turn]):
+            moves[step].append((at(r, c), at(*to)))
+            sends[at(r, c), step] = form, index
+            gets[at(*to)] = step, form
+    return moves, sends, gets
+
+
+def pack_parent_kernel(sends, pattern, own, *outs):
+    for step, out in enumerate(outs):
+        last = step == len(outs) - 1
+        form = 1 if last else sends[step, 0]
+        index = 0 if last else sends[step, 1]
+        for j in range(NB):
+            i, k = (index, j) if last else (
+                jnp.where(form == 0, j, index), jnp.where(form == 0, index, j)
+            )
+            keep = pattern[i, k].astype(F32)
+            out[j] = own[block(i), block(k)] * keep
+
+
+def pack_parent(sends, pattern, own):
+    return pl.pallas_call(
+        pack_parent_kernel,
+        out_shape=(jax.ShapeDtypeStruct((NB, B, B), F32),) * (sends.shape[0] + 1),
+        in_specs=[SMEM, SMEM, VMEM],
+        out_specs=(VMEM,) * (sends.shape[0] + 1),
+        compiler_params=params(60),
+        name="pack_parent",
+    )(sends, pattern, own)
+
+
+def pack_small_kernel(ids, cmap, child, small, sems):
     r, c = ids[0], ids[1]
     mine = r // 4 * 4 + c // 4
-    gi, gj = r % 4, c % 4
-    ja, _ = find(cmap, mine, gj, lambda v: v < 8)
-    ia, iv = find(cmap, mine, gi, lambda v: v < 8)
+    ja, _ = find(cmap, mine, c % 4, lambda v: v < 8)
+    ia, iv = find(cmap, mine, r % 4, lambda v: v < 8)
     ja = jnp.maximum(ja, 0)
-    ia = jnp.maximum(ia, 0)
-
-    def small_copy(a, slot, k, n):
-        return pltpu.make_async_copy(
-            child.at[block(a), block(ja)], small.at[slot, k], small_sems.at[n]
-        )
-
-    def bulk_copy(n):
+    made = []
+    for a in range(8):
+        dst = small.at[cmap[mine, r % 4 * 8 + a] // 16, 0]
+        made.append(pltpu.make_async_copy(child.at[block(a), block(ja)], dst, sems.at[a]))
+    src = child.at[block(jnp.maximum(ia, 0)), block(ja)]
+    made.append(pltpu.make_async_copy(src, small.at[jnp.minimum(iv, 7), 1], sems.at[8]))
+    for m in made:
+        m.start()
+    for m in made:
+        m.wait()
+
+
+def pack_small(ids, cmap, child):
+    return pl.pallas_call(
+        pack_small_kernel,
+        out_shape=jax.ShapeDtypeStruct((ROWS, 2, B, B), F32),
+        in_specs=[SMEM, SMEM, VMEM],
+        out_specs=HBM,
+        scratch_shapes=[pltpu.SemaphoreType.DMA((9,))],
+        compiler_params=params(12),
+        name="pack_small",
+    )(ids, cmap, child)
+
+
+def pack_kernel(ids, cmap, child, bulk, sems):
+    r, c = ids[0], ids[1]
+    mine = r // 4 * 4 + c // 4
+
+    def copy(n):
         a, b = n // 8, n % 8
-        slot = cmap[mine, gi * 8 + a] // 16 * COLS + cmap[mine, gj * 8 + b] // 8
+        slot = cmap[mine, r % 4 * 8 + a] // 16 * COLS + cmap[mine, c % 4 * 8 + b] // 8
         return pltpu.make_async_copy(child.at[block(a), block(b)], bulk.at[slot], sems.at[n])
 
-    for a in range(8):
-        small_copy(a, cmap[mine, gi * 8 + a] // 16, 0, a).start()
-    small_copy(ia, jnp.minimum(iv, 7), 1, 8).start()
-    lax.fori_loop(0, 64, lambda n, _: (bulk_copy(n).start(), 0)[1], 0)
-    for a in range(8):
-        small_copy(a, cmap[mine, gi * 8 + a] // 16, 0, a).wait()
-    small_copy(ia, jnp.minimum(iv, 7), 1, 8).wait()
-    lax.fori_loop(0, 64, lambda n, _: (bulk_copy(n).wait(), 0)[1], 0)
+    lax.fori_loop(0, 64, lambda n, _: (copy(n).start(), 0)[1], 0)
+    lax.fori_loop(0, 64, lambda n, _: (copy(n).wait(), 0)[1], 0)
 
 
 def pack(ids, cmap, child):
     return pl.pallas_call(
         pack_kernel,
-        out_shape=(
-            jax.ShapeDtypeStruct((ROWS * COLS, B, B), F32),
-            jax.ShapeDtypeStruct((ROWS, 2, B, B), F32),
-        ),
-        in_specs=[SMEM, SMEM, HBM],
-        out_specs=(HBM, HBM),
-        scratch_shapes=[pltpu.SemaphoreType.DMA((64,)), pltpu.SemaphoreType.DMA((9,))],
+        out_shape=jax.ShapeDtypeStruct((ROWS * COLS, B, B), F32),
+        in_specs=[SMEM, SMEM, VMEM],
+        out_specs=HBM,
+        scratch_shapes=[pltpu.SemaphoreType.DMA((64,))],
+        compiler_params=params(60),
         name="pack",
     )(ids, cmap, child)
 
 
-def relay_kernel(ids, cmap, came, owners, diag, sems):
+def relay_kernel(ids, cmap, came, parent, owners, diag, sems):
     r, c = ids[0], ids[1]
-    copies = []
+    copies = [(parent.at[0], diag.at[2])]
     for half in range(2):
         child = half * 4 + c // 4
         pick = jnp.int32(half * 4)
@@ -101,23 +164,22 @@
         m.wait()
 
 
-def relay(ids, cmap, came):
+def relay(ids, cmap, came, parent):
     return pl.pallas_call(
         relay_kernel,
         out_shape=(
             jax.ShapeDtypeStruct((COLS, 2, B, B), F32),
-            jax.ShapeDtypeStruct((2, B, B), F32),
+            jax.ShapeDtypeStruct((3, B, B), F32),
         ),
-        in_specs=[SMEM, SMEM, HBM],
+        in_specs=[SMEM, SMEM, VMEM, VMEM],
         out_specs=(HBM, HBM),
-        scratch_shapes=[pltpu.SemaphoreType.DMA((10,))],
+        scratch_shapes=[pltpu.SemaphoreType.DMA((11,))],
+        compiler_params=params(60),
         name="relay",
-    )(ids, cmap, came)
-
-
-def gather_rows(cmap, wanted, start, came, out):
-    for k in range(NB):
-        out[:, k * B : (k + 1) * B] = start[k * B : (k + 1) * B, :].T
+    )(ids, cmap, came, parent)
+
+
+def gather_rows(cmap, wanted, came, out):
     for child in range(8):
         half, quarter = child // 4, child % 4
         hit = lax.fori_loop(
@@ -136,22 +198,46 @@
 
 
 def owner_kernel(ids, cmap, start, came, out):
-    gather_rows(cmap, ids[0] * COLS + ids[1], start, came, out)
-
-
-def diag_kernel(ids, cmap, start, came, out):
-    gather_rows(cmap, ids[0], start, came, out)
-
-
-def assemble(kernel, name, ids, cmap, start, came):
-    return pl.pallas_call(
-        kernel,
+    @pl.when(ids[2] == 0)
+    def _():
+        for k in range(NB):
+            out[:, k * B : (k + 1) * B] = start[k].T
+
+    @pl.when(ids[2] != 0)
+    def _():
+        for k in range(NB):
+            out[:, k * B : (k + 1) * B] = start[k]
+
+    gather_rows(cmap, ids[0] * COLS + ids[1], came, out)
+
+
+def owner_rows(ids, cmap, start, came):
+    return pl.pallas_call(
+        owner_kernel,
         out_shape=jax.ShapeDtypeStruct((B, W), F32),
         in_specs=[SMEM, SMEM, VMEM, VMEM],
         out_specs=VMEM,
         compiler_params=params(24),
-        name=name,
+        name="owner_rows",
     )(ids, cmap, start, came)
+
+
+def diag_kernel(ids, cmap, came, out):
+    out[:, :B] = came[0, 2].T
+    for k in range(1, NB):
+        out[:, k * B : (k + 1) * B] = came[k, 2]
+    gather_rows(cmap, ids[0], came, out)
+
+
+def diag_rows(ids, cmap, came):
+    return pl.pallas_call(
+        diag_kernel,
+        out_shape=jax.ShapeDtypeStruct((B, W), F32),
+        in_specs=[SMEM, SMEM, VMEM],
+        out_specs=VMEM,
+        compiler_params=params(24),
+        name="diag_rows",
+    )(ids, cmap, came)
 
 
 def spread_lane(x, k):
@@ -314,9 +400,9 @@
             for a in range(CHUNK // B):
                 for b in range(SOLVE // B):
                     rs = slice(a * B, (a + 1) * B)
-                    at = j * (SOLVE // B) + b
-                    cs = slice(at * B, (at + 1) * B)
-                    keep = pattern[step * (CHUNK // B) + a, at].astype(F32)
+                    k = j * (SOLVE // B) + b
+                    cs = slice(k * B, (k + 1) * B)
+                    keep = pattern[step * (CHUNK // B) + a, k].astype(F32)
                     out_ref[rs, cs] = own_ref[rs, cs] * keep - change[rs, b * B : (b + 1) * B]
 
     @pl.when((c == 0) & jnp.logical_not(top))
@@ -347,105 +433,123 @@
         in_specs=[SMEM, SMEM, whole, whole, part, part],
         out_specs=part,
         scratch_shapes=[pltpu.VMEM((W, W), BF16)] * 4 + [pltpu.VMEM((CHUNK, W), F32)],
-        compiler_params=params(48),
+        compiler_params=params(60),
         name="update",
     )(ids, pattern, w, xc, xr, own)
 
 
-def add_kernel(ids, cmap, came, base, out, tile, parts, tile_sem, sems):
-    r, c = ids[0], ids[1]
-    load = pltpu.make_async_copy(base, tile, tile_sem)
-    load.start()
-
-    def visit(n, act):
-        src_r, src_c = n // COLS, n % COLS
-        child = src_r // 4 * 4 + src_c // 4
-        ra, rv = find(cmap, child, src_r % 4, lambda v: v // 16 == r)
-        ca, cv = find(cmap, child, src_c % 4, lambda v: v // 8 == c)
-        low, col = rv % 16, cv % 8
-        ok = (ra >= 0) & (ca >= 0) & (c > 0) & ((r > 0) | (low >= 8))
-
-        @pl.when(ok)
+def add_kernel(places, base, came, out, held, sems):
+    step = pl.program_id(0)
+
+    def visit(group, act):
+        def one(quarter, _):
+            child = group // 4
+            slot = (child // 4 * 4 + group % 4) * COLS + child % 4 * 4 + quarter
+            col = places[1, child * 4 + quarter]
+
+            @pl.when(col >= 0)
+            def _():
+                act(pltpu.make_async_copy(came.at[slot], held.at[slot], sems.at[slot]), slot, col)
+
+            return 0
+
+        lax.fori_loop(0, 4, one, 0)
+
+    @pl.when(step == 0)
+    def _():
+        def begin(group, _):
+            @pl.when(places[0, group] >= 0)
+            def _():
+                visit(group, lambda m, slot, col: m.start())
+
+            return 0
+
+        lax.fori_loop(0, 32, begin, 0)
+
+    out[...] = base[...]
+
+    def finish(group, _):
+        row = places[0, group]
+
+        def act(m, slot, col):
+            m.wait()
+            here = block(row % (CHUNK // B)), block(col)
+            out[here] = out[here] + held[slot]
+
+        @pl.when((row >= 0) & (row // (CHUNK // B) == step))
         def _():
-            act(n, low, col)
+            visit(group, act)
 
         return 0
 
-    def copy(n):
-        return pltpu.make_async_copy(came.at[n], parts.at[n], sems.at[n])
-
-    def begin(n, low, col):
-        copy(n).start()
-
-    def finish(n, low, col):
-        copy(n).wait()
-        rows, cols = block(low), block(col)
-        tile[rows, cols] = tile[rows, cols] + parts[n]
-
-    lax.fori_loop(0, ROWS * COLS, lambda n, _: visit(n, begin), 0)
-    load.wait()
-    lax.fori_loop(0, ROWS * COLS, lambda n, _: visit(n, finish), 0)
-    store = pltpu.make_async_copy(tile, out, tile_sem)
-    store.start()
-    store.wait()
-
-
-def add(ids, cmap, came, base):
+    lax.fori_loop(0, 32, finish, 0)
+
+
+def add(places, base, came):
+    part = pl.BlockSpec((CHUNK, W), lambda i: (i, 0))
     return pl.pallas_call(
         add_kernel,
+        grid=(base.shape[0] // CHUNK,),
         out_shape=jax.ShapeDtypeStruct(base.shape, F32),
-        in_specs=[SMEM, SMEM, HBM, HBM],
-        out_specs=HBM,
+        in_specs=[SMEM, part, HBM],
+        out_specs=part,
         scratch_shapes=[
-            pltpu.VMEM(base.shape, F32),
             pltpu.VMEM((ROWS * COLS, B, B), F32),
-            pltpu.SemaphoreType.DMA(()),
             pltpu.SemaphoreType.DMA((ROWS * COLS,)),
         ],
-        compiler_params=params(32),
+        compiler_params=params(60),
         name="add",
-    )(ids, cmap, came, base)
+    )(places, base, came)
 
 
 def at(r, c):
     return r * COLS + c
 
 
+def after(value, first):
+    return lax.optimization_barrier((value, first))[0]
+
+
 def body(child, own, pattern, cmap):
-    ids = jnp.stack([lax.axis_index("prow"), lax.axis_index("pcol")]).astype(jnp.int32)
-    bulk, small = pack(ids, cmap, child)
+    row, col = lax.axis_index("prow"), lax.axis_index("pcol")
+    moves, sends, gets = scatter_plan()
+    mine = lax.dynamic_index_in_dim(jnp.asarray(gets), at(row, col), 0, keepdims=False)
+    ids = jnp.stack([row, col, mine[1]]).astype(jnp.int32)
+    sends = lax.dynamic_index_in_dim(jnp.asarray(sends), at(row, col), 0, keepdims=False)
+
+    places = cmap.reshape(32, 8)
+    low, high = places % 16, places % 8
+    rok = (places // 16 == row) & ((row > 0) | (low >= 8))
+    cok = (places // 8 == col) & (col > 0)
+    places = jnp.stack(
+        [jnp.max(jnp.where(rok, low, -1), axis=1), jnp.max(jnp.where(cok, high, -1), axis=1)]
+    )
+
+    *pieces, start = pack_parent(sends, pattern, own)
+    small = pack_small(ids, cmap, child)
     small = lax.all_to_all(small, "prow", 0, 0, tiled=True)
-
-    start = None
-    keep = jnp.repeat(pattern[:NB].astype(F32), B, axis=0)
-    for k in range(NB):
-        piece = own[:W, k * B : (k + 1) * B] * keep[:, k : k + 1]
-        moves = [(at(0, c), at(c // 2, 8 * (c % 2) + k)) for c in range(COLS)]
-        piece = lax.ppermute(piece, AXES, moves)
-        mine = lax.axis_index("pcol") % 8 == k
-        start = jnp.where(mine, piece, 0.0 if start is None else start)
-    diag_start = lax.ppermute(start, AXES, [(at(0, k), at(k, 0)) for k in range(NB)])
-    diag_start = lax.all_to_all(diag_start, "pcol", 0, 0, tiled=True)[: W // COLS]
-    diag_start = lax.all_gather(diag_start, "pcol", axis=0, tiled=True)
-
-    owners, diag = relay(ids, cmap, small)
-    diag = lax.all_gather(diag, "pcol", axis=0).reshape(COLS, 2, B, B)
+    for step, piece in enumerate(pieces):
+        piece = lax.ppermute(piece, AXES, moves[step])
+        start = jnp.where(mine[0] == step, piece, start)
+    parent = lax.all_to_all(start, "prow", 0, 0, tiled=True)
+
+    owners, diag = relay(ids, cmap, small, parent)
+    diag = lax.all_gather(diag, "pcol", axis=0)
     owners = lax.all_to_all(owners, "pcol", 0, 0, tiled=True)
-
-    diag_rows = assemble(diag_kernel, "diag_rows", ids, cmap, diag_start, diag)
-    pivot = lax.all_gather(diag_rows, "prow", axis=0, tiled=True)
-    owned = assemble(owner_kernel, "owner_rows", ids, cmap, start, owners)
-    moves = [
-        (at(r, c), at(c % 8, 2 * r + c // 8)) for r in range(ROWS) for c in range(COLS)
-    ]
-    xc = lax.ppermute(owned, AXES, moves)
+    owned = owner_rows(ids, cmap, start, owners)
+    to = [(at(r, c), at(c % 8, 2 * r + c // 8)) for r in range(ROWS) for c in range(COLS)]
+    xc = lax.ppermute(owned, AXES, to)
+
+    bulk = after(pack(ids, cmap, child), owners)
+    bulk = lax.all_to_all(bulk, AXES, 0, 0, tiled=True)
+
+    pivot = diag_rows(ids, cmap, after(diag, xc))
+    pivot = lax.all_gather(pivot, "prow", axis=0, tiled=True)
+    xr = lax.all_gather(owned, "pcol", axis=0, tiled=True)
     xc = lax.all_gather(xc, "prow", axis=0, tiled=True)
-    xr = lax.all_gather(owned, "pcol", axis=0, tiled=True)
-
-    bulk = lax.all_to_all(bulk, AXES, 0, 0, tiled=True)
     w = factor(pivot)
     base = update(ids, pattern, w, xc, xr, own)
-    return add(ids, cmap, bulk, base)
+    return add(places, base, bulk)
 
 
 def solution(mesh):

time: 636 us -> 443 us (0.70)
  Pallas kernels: 310 us -> 133 us
  blocking collectives: 114 us -> 61.4 us
  waiting for transfers between devices: 150 us -> 184 us
  between operations: 13.3 us -> 19.8 us
    pallas_call x4 -> x6, Pallas kernels: 198 us -> 39.3 us  [the longest x1 18.3 us: add(): pl.pallas_call(add_kernel, grid=(base.shape[0] // CHUNK,), out_shape=jax....]
    all_gather x2, waiting for transfers between devices: 0.01 us -> 47.5 us  [the longest x1 36.9 us: body(): pivot = lax.all_gather(pivot, 'prow', axis=0, tiled=True)]
    all_to_all x2 -> x1, blocking collectives: 63.2 us -> 20 us  [body(): parent = lax.all_to_all(start, 'prow', 0, 0, tiled=True)]
    all_gather x1, waiting for transfers between devices: 101 us -> 75.1 us  [body(): xr = lax.all_gather(owned, 'pcol', axis=0, tiled=True)]
    all_gather x1 -> x0, blocking collectives: 23.2 us -> none  [body(): diag_start = lax.all_gather(diag_start, 'pcol', axis=0, tiled=True)]
    pallas_call x1, Pallas kernels: 22 us -> 2.53 us  [relay(): pl.pallas_call(relay_kernel, out_shape=(jax.ShapeDtypeStruct((COLS, 2, B,...]
    all_gather x1, waiting for transfers between devices: 0.01 us -> 14.9 us  [body(): xc = lax.all_gather(xc, 'prow', axis=0, tiled=True)]
    all_to_all x1, blocking collectives: 27.9 us -> 41.4 us  [body(): owners = lax.all_to_all(owners, 'pcol', 0, 0, tiled=True)]
  transfers between devices with their start and end apart: 15 -> 17, of which waited for: 3 -> 6; matrix products, arithmetic and copies ran while one was open for 1% -> 1% of each run, Pallas kernels for 15% -> 23%
where the time goes in v3:
time: 443 us; the launch traced here: 441 us
  waiting for transfers between devices  184 us (42%)
  Pallas kernels  133 us (30%)
  blocking collectives  61.4 us (14%)
  starting transfers between devices  28.6 us (6%)
  between operations  19.8 us (4%)
  local copies, waits for them, and re-layouts  12.3 us (3%)
    all_gather x1, waiting for transfers between devices, body(): xr = lax.all_gather(owned, 'pcol', axis=0, tiled=True)  75.1 us
    pallas_call x1, Pallas kernels, factor(): pl.pallas_call(factor_kernel, out_shape=jax.ShapeDtypeStruct((W, W), F32)...  55.2 us
    all_to_all x1, blocking collectives, body(): owners = lax.all_to_all(owners, 'pcol', 0, 0, tiled=True)  41.4 us
    all_gather x1, waiting for transfers between devices, body(): pivot = lax.all_gather(pivot, 'prow', axis=0, tiled=True)  36.9 us
    pallas_call x1, Pallas kernels, update(): pl.pallas_call(update_kernel, grid=(rows // CHUNK,), out_shape=jax.ShapeD...  35.9 us
    ppermute x1, waiting for transfers between devices, body(): xc = lax.ppermute(owned, AXES, to)  23.8 us
    ppermute x10, waiting for transfers between devices, body(): piece = lax.ppermute(piece, AXES, moves[step])  21.9 us
    all_to_all x1, blocking collectives, body(): parent = lax.all_to_all(start, 'prow', 0, 0, tiled=True)  20 us
  transfers between devices with their start and end apart: 17, of which 6 were waited for; matrix products, arithmetic and copies ran while one was open for 1% of the time, Pallas kernels for 23%

profile of v3, /device:TPU:14, one launch (start us, length us, event | category | flops | bytes accessed | tf_op | source)
XLA Modules:
  0.0 441.5 jit_solution(13392283517401110337)
XLA Ops:
  6.5 0.7 dynamic-slice_bitcast_fusion
  7.2 0.7 copy.13.sends
  7.9 1.4 copy.15.pattern
  9.3 6.7 %pack_parent.1 = (f32[8,128,128]{2,1,0:T(8,128)}, f32[8,128,128]{2,1,0:T(8,128)}, f32[8,128,128]{2,1,0:T(8,128)}, f32[8,128,128]{2,1,0:T(8,128)}, f32[8,128,128]...) custom-call(s32[10,2]{1,0:T(8,128)} %copy.13.sends, ...), custom_call_target="tpu_custom_call" | custom-call | tf_op jit(solution)/shard_map/pack_parent/pallas_call | solution.py:82
  15.9 0.7 collective-permute-start
  16.6 0.7 collective-permute-start.1
  17.3 0.7 collective-permute-start.2
  18.0 1.5 collective-permute-start.3
  19.5 1.5 collective-permute-start.4
  20.9 0.7 constant_dynamic-slice_fusion
  21.6 0.6 fusion.6
  22.2 0.7 pad_add_fusion.1.ids
  22.9 2.2 copy-done
  25.1 1.5 pack_small.1
  26.7 4.8 %all-to-all-start = ((f32[8,2,128,128]{3,2,1,0:T(8,128)}), f32[8,2,128,128]{3,2,1,0:T(8,128)S(1)}, u32[]{:S(2)}, u32[]{:S(2)}) async-start(f32[8,2,128,128]{3,2,1,0:T(8,128)} %pack_small.1), calls=%async_computation | async-start | bytes 2097152 | tf_op jit(solution)/shard_map/all_to_all | solution.py:530
  31.5 0.7 collective-permute-start.5
  32.2 0.7 collective-permute-start.6
  32.9 0.7 collective-permute-start.7
  33.6 1.3 collective-permute-start.8
  34.9 0.7 collective-permute-start.9
  42.0 21.9 %collective-permute-done.8 = f32[8,128,128]{2,1,0:T(8,128)S(1)} collective-permute-done((f32[8,128,128]{2,1,0:T(8,128)}, f32[8,128,128]{2,1,0:T(8,128)S(1)}, u32[]{:S(2)}, u32[]{:S(2)}) %collective-permute-start.8) | collective-permute-done | bytes 524320 | tf_op jit(solution)/shard_map/ppermute | solution.py:532
  63.9 0.5 select_select_fusion.start
  64.5 20.0 %all_to_all.20.parent = f32[8,128,128]{2,1,0:T(8,128)} all-to-all(f32[8,128,128]{2,1,0:T(8,128)S(1)} %select_select_fusion.start), channel_id=1, replica_groups=mesh['prow'=8,'pcol'=16] {'prow'}, dimensions={0} | all-to-all | bytes 1048576 | tf_op jit(solution)/shard_map/all_to_all | solution.py:534
  84.6 2.5 relay.1
  87.1 0.0 all-gather.6.cloned.1.call-start
  87.2 41.4 %all_to_all.21.came = f32[16,2,128,128]{3,2,1,0:T(8,128)S(1)} all-to-all(f32[16,2,128,128]{3,2,1,0:T(8,128)} %get-tuple-element.32), channel_id=1, replica_groups=mesh['prow'=8,'pcol'=16] {'pcol'}, dimensions={0} | all-to-all | bytes 4194304 | tf_op jit(solution)/shard_map/all_to_all | solution.py:538
  128.6 3.9 owner_rows.1
  132.5 3.3 collective-permute-start.10
  135.8 23.8 %collective-permute-done.10 = f32[128,1024]{1,0:T(8,128)S(1)} collective-permute-done((f32[128,1024]{1,0:T(8,128)}, f32[128,1024]{1,0:T(8,128)S(1)}, u32[]{:S(2)}, u32[]{:S(2)}) %collective-permute-start.10) | collective-permute-done | bytes 524320 | tf_op jit(solution)/shard_map/ppermute | solution.py:541
  159.6 10.6 %all-gather.12.cloned.1.call-done = f32[48,128,128]{2,1,0:T(8,128)} async-done(((f32[3,128,128]{2,1,0:T(8,128)}), f32[48,128,128]{2,1,0:T(8,128)}) %all-gather.12.cloned.1.call-update) | async-done | bytes 3145744 | tf_op jit(solution)/shard_map/all_gather | solution.py:537
  170.2 1.9 copy-done.3
  172.1 3.6 diag_rows.1
  175.7 0.0 all-gather.8.cloned.1.call-start
  175.8 0.7 all-gather.8.cloned.1.call-update
  176.5 0.5 all-gather.10.cloned.1.call-update
  177.1 5.3 %pack.1 = f32[128,128,128]{2,1,0:T(8,128)} custom-call(s32[3]{0:T(128)} %copy-done.7, s32[8,32]{1,0:T(8,128)} %cmap.9, f32[1024,1024]{1,0:T(8,128)} %child.3), custom_call_target="tpu_custom_call" | custom-call | tf_op jit(solution)/shard_map/pack/pallas_call | solution.py:136
  182.3 11.4 %all-to-all-start.3 = ((f32[128,128,128]{2,1,0:T(8,128)}), f32[128,128,128]{2,1,0:T(8,128)}, u32[]{:S(2)}, u32[]{:S(2)}) async-start(f32[128,128,128]{2,1,0:T(8,128)} %pack.1), calls=%async_computation.3 | async-start | bytes 16777216 | tf_op jit(solution)/shard_map/all_to_all | solution.py:544
  193.7 0.1 reshape.26
  193.8 0.2 select_reduce_fusion
  193.9 0.5 pad_add_fusion.places
  194.5 36.9 %all-gather.6.cloned.1.call-done.a_ref = f32[1024,1024]{1,0:T(8,128)} async-done(((f32[128,1024]{1,0:T(8,128)}), f32[1024,1024]{1,0:T(8,128)}) %all-gather.6.cloned.1.call-update) | async-done | bytes 4194320 | tf_op jit(solution)/shard_map/all_gather | solution.py:547
  231.4 2.2 copy-done.2
  233.6 55.2 %factor.1.w_ref = f32[1024,1024]{1,0:T(8,128)S(1)} custom-call(f32[1024,1024]{1,0:T(8,128)S(1)} %copy-done.2), custom_call_target="tpu_custom_call" | custom-call | tf_op jit(solution)/shard_map/factor/pallas_call | solution.py:323
  288.8 2.0 copy-done.1
  290.7 14.9 %all-gather.8.cloned.1.call-done.xc_ref = f32[1024,1024]{1,0:T(8,128)} async-done(((f32[128,1024]{1,0:T(8,128)}), f32[1024,1024]{1,0:T(8,128)}) %all-gather.8.cloned.1.call-update) | async-done | bytes 4194320 | tf_op jit(solution)/shard_map/all_gather | solution.py:549
  305.7 75.1 %all-gather.10.cloned.1.call-done.xr_ref = f32[2048,1024]{1,0:T(8,128)} async-done(((f32[128,1024]{1,0:T(8,128)}), f32[2048,1024]{1,0:T(8,128)}) %all-gather.10.cloned.1.call-update) | async-done | bytes 8388624 | tf_op jit(solution)/shard_map/all_gather | solution.py:548
  380.7 35.9 %update.1.base = f32[2048,1024]{1,0:T(8,128)} custom-call(s32[3]{0:T(128)} %copy-done.7, s32[16,8]{1,0:T(8,128)} %copy.15.pattern, f32[1024,1024]{1,0:T(8,128)} %copy-done.1, f32[1024,1024]{1,0:T(8,128)} %all-gather.8.cloned.1.call-done.xc_ref, f32[2048,1024]{1,0:T(8,128)} %all-gather.10.cloned.1.call-done.xr_ref, f32[2048,1024]{1,0:T(8,128)} %own_ref.1), custom_call_target="tpu_custom_call" | custom-call | tf_op jit(solution)/shard_map/update/pallas_call | solution.py:429
  416.6 18.3 %add.41 = f32[2048,1024]{1,0:T(8,128)} custom-call(s32[2,32]{1,0:T(2,128)} %pad_add_fusion.places, f32[2048,1024]{1,0:T(8,128)} %update.1.base, f32[128,128,128]{2,1,0:T(8,128)} %all-to-all-done.3.came), custom_call_target="tpu_custom_call" | custom-call | tf_op jit(solution)/shard_map/add/pallas_call | solution.py:490
  (37 shorter events, 0.1 us)
Async XLA Ops:
  9.3 13.7 %copy-start.4 = (s32[8,32]{1,0:T(8,128)S(1)}, s32[8,32]{1,0:T(8,128)}, u32[]{:S(2)}) copy-start(s32[8,32]{1,0:T(8,128)} %cmap.9) | copy-start | bytes 3076
  15.9 15.5 %collective-permute-start = (f32[8,128,128]{2,1,0:T(8,128)}, f32[8,128,128]{2,1,0:T(8,128)S(1)}, u32[]{:S(2)}, u32[]{:S(2)}) collective-permute-start(f32[8,128,128]{2,1,0:T(8,128)} %get-tuple-element.20), channel_id=1, source_target_pairs={{0,15}} | collective-permute-start | bytes 1572872 | tf_op jit(solution)/shard_map/ppermute | solution.py:532
  16.6 15.6 %collective-permute-start.1 = (f32[8,128,128]{2,1,0:T(8,128)}, f32[8,128,128]{2,1,0:T(8,128)S(1)}, u32[]{:S(2)}, u32[]{:S(2)}) collective-permute-start(f32[8,128,128]{2,1,0:T(8,128)} %get-tuple-element.21), channel_id=1, source_target_pairs={{0,14}} | collective-permute-start | bytes 1572872 | tf_op jit(solution)/shard_map/ppermute | solution.py:532
  17.3 15.6 %collective-permute-start.2 = (f32[8,128,128]{2,1,0:T(8,128)}, f32[8,128,128]{2,1,0:T(8,128)S(1)}, u32[]{:S(2)}, u32[]{:S(2)}) collective-permute-start(f32[8,128,128]{2,1,0:T(8,128)} %get-tuple-element.22), channel_id=1, source_target_pairs={{0,13}} | collective-permute-start | bytes 1572872 | tf_op jit(solution)/shard_map/ppermute | solution.py:532
  18.0 15.6 %collective-permute-start.3 = (f32[8,128,128]{2,1,0:T(8,128)}, f32[8,128,128]{2,1,0:T(8,128)}, u32[]{:S(2)}, u32[]{:S(2)}) collective-permute-start(f32[8,128,128]{2,1,0:T(8,128)} %get-tuple-element.23), channel_id=1, source_target_pairs={{0,7}} | collective-permute-start | bytes 1572872 | tf_op jit(solution)/shard_map/ppermute | solution.py:532
  19.5 15.4 %collective-permute-start.4 = (f32[8,128,128]{2,1,0:T(8,128)}, f32[8,128,128]{2,1,0:T(8,128)}, u32[]{:S(2)}, u32[]{:S(2)}) collective-permute-start(f32[8,128,128]{2,1,0:T(8,128)} %get-tuple-element.24), channel_id=1, source_target_pairs={{0,6},{16,21},{32,38},{48,55},{64,77},{80,94},{96,111},{112,117}} | collective-permute-start | bytes 1572872 | tf_op jit(solution)/shard_map/ppermute | solution.py:532
  22.9 2.2 copy-start
  25.1 39.3 %copy-start.7 = (s32[3]{0:T(128)}, s32[3]{0:T(128)S(1)}, u32[]{:S(2)}) copy-start(s32[3]{0:T(128)S(1)} %pad_add_fusion.1.ids) | copy-start | bytes 40
  25.1 38.8 %copy-start.10 = (f32[8,128,128]{2,1,0:T(8,128)S(1)}, f32[8,128,128]{2,1,0:T(8,128)}, u32[]{:S(2)}) copy-start(f32[8,128,128]{2,1,0:T(8,128)} %get-tuple-element.30) | copy-start | bytes 1572868
  26.7 37.8 %all-to-all-start = ((f32[8,2,128,128]{3,2,1,0:T(8,128)}), f32[8,2,128,128]{3,2,1,0:T(8,128)S(1)}, u32[]{:S(2)}, u32[]{:S(2)}) async-start(f32[8,2,128,128]{3,2,1,0:T(8,128)} %pack_small.1), calls=%async_computation | async-start | bytes 2097152 | tf_op jit(solution)/shard_map/all_to_all | solution.py:530
  31.5 138.7 %all-gather.12.cloned.1.call-start = ((), (), s32[]{:S(2)}) async-start(), calls=%async_computation.7 | async-start | bytes 3342336 | tf_op jit(solution)/shard_map/all_gather | solution.py:537
  31.5 10.5 %collective-permute-start.5 = (f32[8,128,128]{2,1,0:T(8,128)}, f32[8,128,128]{2,1,0:T(8,128)S(1)}, u32[]{:S(2)}, u32[]{:S(2)}) collective-permute-start(f32[8,128,128]{2,1,0:T(8,128)} %get-tuple-element.25), channel_id=1, source_target_pairs={{0,5},{1,12},{16,31},{3,24},{32,37},{5,41},{48,54},{7,58},{64,71},... | collective-permute-start | bytes 1572872 | tf_op jit(solution)/shard_map/ppermute | solution.py:532
  32.2 9.8 %collective-permute-start.6 = (f32[8,128,128]{2,1,0:T(8,128)}, f32[8,128,128]{2,1,0:T(8,128)S(1)}, u32[]{:S(2)}, u32[]{:S(2)}) collective-permute-start(f32[8,128,128]{2,1,0:T(8,128)} %get-tuple-element.26), channel_id=1, source_target_pairs={{0,4},{1,11},{2,17},{16,30},{3,28},{4,34},{32,47},{5,40},{6,51},{4... | collective-permute-start | bytes 1572872 | tf_op jit(solution)/shard_map/ppermute | solution.py:532
  32.9 31.0 %copy-start.11 = (f32[8,128,128]{2,1,0:T(8,128)}, f32[8,128,128]{2,1,0:T(8,128)S(1)}, u32[]{:S(2)}) copy-start(f32[8,128,128]{2,1,0:T(8,128)S(1)} %collective-permute-done.2) | copy-start | bytes 1572868
  32.9 9.1 %collective-permute-start.7 = (f32[8,128,128]{2,1,0:T(8,128)}, f32[8,128,128]{2,1,0:T(8,128)S(1)}, u32[]{:S(2)}, u32[]{:S(2)}) collective-permute-start(f32[8,128,128]{2,1,0:T(8,128)} %get-tuple-element.27), channel_id=1, source_target_pairs={{0,3},{1,10},{2,20},{16,29},{3,27},{4,33},{32,46},{5,44},{6,50},{4... | collective-permute-start | bytes 1572872 | tf_op jit(solution)/shard_map/ppermute | solution.py:532
  33.6 30.3 %collective-permute-start.8 = (f32[8,128,128]{2,1,0:T(8,128)}, f32[8,128,128]{2,1,0:T(8,128)S(1)}, u32[]{:S(2)}, u32[]{:S(2)}) collective-permute-start(f32[8,128,128]{2,1,0:T(8,128)} %get-tuple-element.28), channel_id=1, source_target_pairs={{0,2},{1,9},{2,19},{16,23},{3,26},{4,36},{32,45},{5,43},{6,49},{48... | collective-permute-start | bytes 1572872 | tf_op jit(solution)/shard_map/ppermute | solution.py:532
  34.9 29.0 %collective-permute-start.9 = (f32[8,128,128]{2,1,0:T(8,128)}, f32[8,128,128]{2,1,0:T(8,128)S(1)}, u32[]{:S(2)}, u32[]{:S(2)}) collective-permute-start(f32[8,128,128]{2,1,0:T(8,128)} %get-tuple-element.29), channel_id=1, source_target_pairs={{0,1},{1,8},{2,18},{16,22},{3,25},{4,35},{32,39},{5,42},{6,52},{48... | collective-permute-start | bytes 1572872 | tf_op jit(solution)/shard_map/ppermute | solution.py:532
  64.5 64.1 %copy-start.5 = (s32[8,32]{1,0:T(8,128)S(1)}, s32[8,32]{1,0:T(8,128)}, u32[]{:S(2)}) copy-start(s32[8,32]{1,0:T(8,128)} %cmap.9) | copy-start | bytes 3076
  64.5 20.1 %copy-start.9 = (f32[8,2,128,128]{3,2,1,0:T(8,128)}, f32[8,2,128,128]{3,2,1,0:T(8,128)S(1)}, u32[]{:S(2)}) copy-start(f32[8,2,128,128]{3,2,1,0:T(8,128)S(1)} %all-to-all-done.came) | copy-start | bytes 3145732
  64.5 64.0 %copy-start.8 = (s32[3]{0:T(128)S(1)}, s32[3]{0:T(128)}, u32[]{:S(2)}) copy-start(s32[3]{0:T(128)} %copy-done.7) | copy-start | bytes 40
  87.1 144.2 %all-gather.6.cloned.1.call-start = ((), (), s32[]{:S(2)}) async-start(), calls=%async_computation.4 | async-start | bytes 4718592 | tf_op jit(solution)/shard_map/all_gather | solution.py:547
  132.5 27.1 %collective-permute-start.10 = (f32[128,1024]{1,0:T(8,128)}, f32[128,1024]{1,0:T(8,128)S(1)}, u32[]{:S(2)}, u32[]{:S(2)}) collective-permute-start(f32[128,1024]{1,0:T(8,128)} %owner_rows.1), channel_id=1, source_target_pairs={{0,0},{1,16},{2,32},{3,48},{4,64},{5,80},{6,96},{7,112},{8,1},{9,1... | collective-permute-start | bytes 1572872 | tf_op jit(solution)/shard_map/ppermute | solution.py:541
  159.6 16.2 %copy-start.12 = (f32[128,1024]{1,0:T(8,128)}, f32[128,1024]{1,0:T(8,128)S(1)}, u32[]{:S(2)}) copy-start(f32[128,1024]{1,0:T(8,128)S(1)} %collective-permute-done.10) | copy-start | bytes 1572868
  170.2 1.9 copy-start.3
  175.7 129.9 %all-gather.8.cloned.1.call-start = ((), (), s32[]{:S(2)}) async-start(), calls=%async_computation.5 | async-start | bytes 4718592 | tf_op jit(solution)/shard_map/all_gather | solution.py:549
  176.5 204.2 %all-gather.10.cloned.1.call-start = ((), (), s32[]{:S(2)}) async-start(), calls=%async_computation.6 | async-start | bytes 8912896 | tf_op jit(solution)/shard_map/all_gather | solution.py:548
  182.3 11.4 %copy-start.6 = (s32[8,32]{1,0:T(8,128)S(1)}, s32[8,32]{1,0:T(8,128)}, u32[]{:S(2)}) copy-start(s32[8,32]{1,0:T(8,128)} %cmap.9) | copy-start | bytes 3076
  182.3 234.3 %all-to-all-start.3 = ((f32[128,128,128]{2,1,0:T(8,128)}), f32[128,128,128]{2,1,0:T(8,128)}, u32[]{:S(2)}, u32[]{:S(2)}) async-start(f32[128,128,128]{2,1,0:T(8,128)} %pack.1), calls=%async_computation.3 | async-start | bytes 16777216 | tf_op jit(solution)/shard_map/all_to_all | solution.py:544
  231.4 2.2 copy-start.2
  288.7 2.0 copy-start.1
Sparse Core Ops, SparseCore 0:
  87.2 82.8 all-gather.11
  175.9 55.4 all-gather.5
  233.1 72.5 all-gather.7
  307.6 73.0 all-gather.9

commit v4 on v3

--- a/solution.py
+++ b/solution.py
@@ -43,8 +43,8 @@
     queues = {}
     for r in range(ROWS):
         for c in range(1, COLS):
-            if r == 0 and c < 8:
-                move = ((0, 0), 0, c)
+            if r == 0:
+                move = ((0, c // 8), 0, c % 8)
             elif c % 8 < 5:
                 move = ((0, 2 * r + c // 8), 0, c % 8)
             else:
@@ -290,10 +290,20 @@
     )
 
 
-def factor_kernel(a_ref, w_ref, d_ref, q_ref):
+def piece_rows(r):
+    rows = []
+    for d in range(ROWS // 2):
+        x = (r // 2 + ROWS // 2 - d) % (ROWS // 2)
+        rows += [2 * x + r % 2, 2 * x + 1 - r % 2]
+    return rows
+
+
+def factor_kernel(ids, *refs):
+    pieces, (w_ref, d_ref, q_ref) = refs[:ROWS], refs[ROWS:]
     row = lax.broadcasted_iota(jnp.int32, (B, B), 0)
     col = lax.broadcasted_iota(jnp.int32, (B, B), 1)
-    w_ref[...] = a_ref[...]
+    for k, piece in zip(piece_rows(ids[0]), pieces):
+        w_ref[block(k), :] = piece[...]
 
     def step(kb, _):
         here = block(kb)
@@ -319,16 +329,16 @@
     lax.fori_loop(0, NB, step, 0)
 
 
-def factor(a):
+def factor(ids, pieces):
     return pl.pallas_call(
         factor_kernel,
         out_shape=jax.ShapeDtypeStruct((W, W), F32),
-        in_specs=[VMEM],
+        in_specs=[SMEM] + [VMEM] * ROWS,
         out_specs=VMEM,
         scratch_shapes=[pltpu.VMEM((B, B), F32), pltpu.VMEM((B, W), F32)],
         compiler_params=params(32),
         name="factor",
-    )(a)
+    )(ids, *pieces)
 
 
 def halves(x):
@@ -356,7 +366,8 @@
         out[:, rows] = dot3(xh[:, :upto], xl[:, :upto], eh[rows, :upto], el[rows, :upto])
 
 
-def update_kernel(ids, pattern, w_ref, xc_ref, xr_ref, own_ref, out_ref, eh, el, ch, cl, x):
+def update_kernel(ids, pattern, w_ref, *refs):
+    pieces, (xr_ref, own_ref, out_ref, eh, el, ch, cl, x) = refs[:ROWS], refs[ROWS:]
     step = pl.program_id(0)
     r, c = ids[0], ids[1]
 
@@ -374,15 +385,14 @@
 
         lax.fori_loop(0, NB, split, 0)
 
-        def columns(i, _):
-            rows = pl.ds(pl.multiple_of(i * CHUNK, CHUNK), CHUNK)
-            solve_rows(xc_ref[rows, :], x, eh, el)
-            high, low = halves(x[...])
-            ch[rows, :] = high
-            cl[rows, :] = low
-            return 0
-
-        lax.fori_loop(0, W // CHUNK, columns, 0)
+        at_row = piece_rows(r)
+        for n in range(0, ROWS, 2):
+            pair = jnp.concatenate([pieces[n][...], pieces[n + 1][...]], axis=0)
+            solve_rows(pair, x, eh, el)
+            for m in range(2):
+                high, low = halves(x[m * B : (m + 1) * B, :])
+                ch[block(at_row[n + m]), :] = high
+                cl[block(at_row[n + m]), :] = low
 
     solve_rows(xr_ref[...], x, eh, el)
     top = (r == 0) & (step < W // CHUNK)
@@ -425,17 +435,18 @@
 def update(ids, pattern, w, xc, xr, own):
     rows = own.shape[0]
     whole = pl.BlockSpec((W, W), lambda i: (0, 0), pipeline_mode=pl.Buffered(1))
+    piece = pl.BlockSpec((B, W), lambda i: (0, 0), pipeline_mode=pl.Buffered(1))
     part = pl.BlockSpec((CHUNK, W), lambda i: (i, 0))
     return pl.pallas_call(
         update_kernel,
         grid=(rows // CHUNK,),
         out_shape=jax.ShapeDtypeStruct(own.shape, F32),
-        in_specs=[SMEM, SMEM, whole, whole, part, part],
+        in_specs=[SMEM, SMEM, whole] + [piece] * ROWS + [part, part],
         out_specs=part,
         scratch_shapes=[pltpu.VMEM((W, W), BF16)] * 4 + [pltpu.VMEM((CHUNK, W), F32)],
         compiler_params=params(60),
         name="update",
-    )(ids, pattern, w, xc, xr, own)
+    )(ids, pattern, w, *xc, xr, own)
 
 
 def add_kernel(places, base, came, out, held, sems):
@@ -510,6 +521,22 @@
     return lax.optimization_barrier((value, first))[0]
 
 
+def along_x(piece):
+    half = ROWS // 2
+    pieces = [piece]
+    for d in range(1, half):
+        to = [(2 * x + k, 2 * ((x + d) % half) + k) for x in range(half) for k in range(2)]
+        pieces.append(lax.ppermute(piece, "prow", to))
+    return pieces
+
+
+def across(pieces):
+    both = []
+    for piece in pieces:
+        both += [piece, lax.ppermute(piece, "prow", [(k, k ^ 1) for k in range(ROWS)])]
+    return both
+
+
 def body(child, own, pattern, cmap):
     row, col = lax.axis_index("prow"), lax.axis_index("pcol")
     moves, sends, gets = scatter_plan()
@@ -528,26 +555,27 @@
     *pieces, start = pack_parent(sends, pattern, own)
     small = pack_small(ids, cmap, child)
     small = lax.all_to_all(small, "prow", 0, 0, tiled=True)
+    top = start
     for step, piece in enumerate(pieces):
         piece = lax.ppermute(piece, AXES, moves[step])
         start = jnp.where(mine[0] == step, piece, start)
-    parent = lax.all_to_all(start, "prow", 0, 0, tiled=True)
+        top = start if step == NB - 2 else top
+    parent = lax.all_to_all(top, "prow", 0, 0, tiled=True)
 
     owners, diag = relay(ids, cmap, small, parent)
     diag = lax.all_gather(diag, "pcol", axis=0)
-    owners = lax.all_to_all(owners, "pcol", 0, 0, tiled=True)
-    owned = owner_rows(ids, cmap, start, owners)
+    diag = diag_rows(ids, cmap, diag)
+    pivot = across(along_x(diag))
+    owners = lax.all_to_all(after(owners, diag), "pcol", 0, 0, tiled=True)
+    owned = owner_rows(ids, cmap, start, after(owners, pivot[2::2]))
+    xr = lax.all_gather(owned, "pcol", axis=0, tiled=True)
     to = [(at(r, c), at(c % 8, 2 * r + c // 8)) for r in range(ROWS) for c in range(COLS)]
     xc = lax.ppermute(owned, AXES, to)
-
-    bulk = after(pack(ids, cmap, child), owners)
+    bulk = after(pack(ids, cmap, child), (xc, pivot))
     bulk = lax.all_to_all(bulk, AXES, 0, 0, tiled=True)
-
-    pivot = diag_rows(ids, cmap, after(diag, xc))
-    pivot = lax.all_gather(pivot, "prow", axis=0, tiled=True)
-    xr = lax.all_gather(owned, "pcol", axis=0, tiled=True)
-    xc = lax.all_gather(xc, "prow", axis=0, tiled=True)
-    w = factor(pivot)
+    xc = along_x(xc)
+    w = factor(ids, pivot)
+    xc = across(after(xc, w))
     base = update(ids, pattern, w, xc, xr, own)
     return add(places, base, bulk)
 

time: 443 us -> 421 us (0.950); the launches traced: 441 us -> 414 us
  blocking collectives: 61.4 us -> 19.8 us
  starting transfers between devices: 28.6 us -> 47.4 us
  waiting for transfers between devices: 184 us -> 178 us
    ppermute x0 -> x14, waiting for transfers between devices: none -> 79.6 us  [the longest x6 77 us: along_x(): pieces.append(lax.ppermute(piece, 'prow', to))]
    all_gather x1, waiting for transfers between devices: 75.1 us -> 4.54 us  [body(): xr = lax.all_gather(owned, 'pcol', axis=0, tiled=True)]
    all_gather x2 -> x0, waiting for transfers between devices: 51.8 us -> none  [the longest x1 36.9 us: body(): pivot = lax.all_gather(pivot, 'prow', axis=0, tiled=True)]
    all_gather x1, waiting for transfers between devices: 10.6 us -> 53.1 us  [body(): diag = lax.all_gather(diag, 'pcol', axis=0)]
    all_to_all x2 -> x1, blocking collectives: 61.4 us -> 19.8 us  [body(): parent = lax.all_to_all(top, 'prow', 0, 0, tiled=True)]
    ppermute x0 -> x14, starting transfers between devices: none -> 10.2 us  [the longest x6 8.06 us: along_x(): pieces.append(lax.ppermute(piece, 'prow', to))]
    ppermute x1, waiting for transfers between devices: 23.8 us -> 17.1 us  [body(): xc = lax.ppermute(owned, AXES, to)]
    all_to_all x0 -> x1, starting transfers between devices: none -> 5.7 us  [body(): owners = lax.all_to_all(after(owners, diag), 'pcol', 0, 0, tiled=True)]
  transfers between devices with their start and end apart: 17 -> 28, of which waited for: 6 -> 11; matrix products, arithmetic and copies ran while one was open for 1% -> 1% of each run, Pallas kernels for 23% -> 24%
where the time goes in v4:
time: 421 us; the launch traced here: 414 us
  waiting for transfers between devices  178 us (42%)
  Pallas kernels  132 us (31%)
  starting transfers between devices  47.4 us (11%)
  blocking collectives  19.8 us (5%)
  between operations  18.1 us (4%)
  local copies, waits for them, and re-layouts  16 us (4%)
    ppermute x6, waiting for transfers between devices, along_x(): pieces.append(lax.ppermute(piece, 'prow', to))  77 us
    pallas_call x1, Pallas kernels, factor(): pl.pallas_call(factor_kernel, out_shape=jax.ShapeDtypeStruct((W, W), F32)...  56.6 us
    all_gather x1, waiting for transfers between devices, body(): diag = lax.all_gather(diag, 'pcol', axis=0)  53.1 us
    pallas_call x1, Pallas kernels, update(): pl.pallas_call(update_kernel, grid=(rows // CHUNK,), out_shape=jax.ShapeD...  35.6 us
    ppermute x8, waiting for transfers between devices, body(): piece = lax.ppermute(piece, AXES, moves[step])  23.6 us
    all_to_all x1, blocking collectives, body(): parent = lax.all_to_all(top, 'prow', 0, 0, tiled=True)  19.8 us
    pallas_call x1, Pallas kernels, add(): pl.pallas_call(add_kernel, grid=(base.shape[0] // CHUNK,), out_shape=jax....  18 us
    ppermute x1, waiting for transfers between devices, body(): xc = lax.ppermute(owned, AXES, to)  17.1 us
  transfers between devices with their start and end apart: 28, of which 11 were waited for; matrix products, arithmetic and copies ran while one was open for 1% of the time, Pallas kernels for 24%

profile of v4, /device:TPU:14, one launch (start us, length us, event | category | flops | bytes accessed | tf_op | source)
XLA Modules:
  0.0 414.1 jit_solution(11340076180990565945)
XLA Ops:
  7.9 1.4 copy.15.pattern
  9.3 6.1 %pack_parent.1 = (f32[8,128,128]{2,1,0:T(8,128)}, f32[8,128,128]{2,1,0:T(8,128)}, f32[8,128,128]{2,1,0:T(8,128)}, f32[8,128,128]{2,1,0:T(8,128)}, f32[8,128,128]...) custom-call(s32[8,2]{1,0:T(8,128)} %copy.13.sends, ...), custom_call_target="tpu_custom_call" | custom-call | tf_op jit(solution)/shard_map/pack_parent/pallas_call | solution.py:82
  15.4 0.8 collective-permute-start
  16.2 0.7 collective-permute-start.1
  16.9 0.7 collective-permute-start.2
  17.6 0.7 constant_dynamic-slice_fusion
  18.9 0.7 pad_add_fusion.1.ids
  19.6 2.2 copy-done
  21.8 1.5 pack_small.1
  23.3 4.8 %all-to-all-start = ((f32[8,2,128,128]{3,2,1,0:T(8,128)}), f32[8,2,128,128]{3,2,1,0:T(8,128)S(1)}, u32[]{:S(2)}, u32[]{:S(2)}) async-start(f32[8,2,128,128]{3,2,1,0:T(8,128)} %pack_small.1), calls=%async_computation | async-start | bytes 2097152 | tf_op jit(solution)/shard_map/all_to_all | solution.py:557
  28.8 0.7 collective-permute-start.4
  29.5 1.3 collective-permute-start.5
  31.6 0.7 collective-permute-start.14
  36.7 23.6 %collective-permute-done.5 = f32[8,128,128]{2,1,0:T(8,128)S(1)} collective-permute-done((f32[8,128,128]{2,1,0:T(8,128)}, f32[8,128,128]{2,1,0:T(8,128)S(1)}, u32[]{:S(2)}, u32[]{:S(2)}) %collective-permute-start.5) | collective-permute-done | bytes 524320 | tf_op jit(solution)/shard_map/ppermute | solution.py:560
  60.3 1.4 broadcast_select_fusion
  61.7 19.8 %all_to_all.20.parent = f32[8,128,128]{2,1,0:T(8,128)} all-to-all(f32[8,128,128]{2,1,0:T(8,128)S(1)} %get-tuple-element.44), channel_id=1, replica_groups=mesh['prow'=8,'pcol'=16] {'prow'}, dimensions={0} | all-to-all | bytes 1048576 | tf_op jit(solution)/shard_map/all_to_all | solution.py:563
  81.4 2.5 relay.1
  84.0 53.1 %all-gather.6.cloned.1.call-done = f32[48,128,128]{2,1,0:T(8,128)} async-done(((f32[3,128,128]{2,1,0:T(8,128)}), f32[48,128,128]{2,1,0:T(8,128)}) %all-gather.6.cloned.1.call-update) | async-done | bytes 3145744 | tf_op jit(solution)/shard_map/all_gather | solution.py:566
  137.1 1.9 copy-done.2
  139.7 3.1 diag_rows.1.refs_0_
  142.7 5.7 %all-to-all-start.2 = ((f32[16,2,128,128]{3,2,1,0:T(8,128)}), f32[16,2,128,128]{3,2,1,0:T(8,128)S(1)}, u32[]{:S(2)}, u32[]{:S(2)}) async-start(f32[16,2,128,128]{3,2,1,0:T(8,128)} %get-tuple-element.34), calls=%async_computation.2 | async-start | bytes 4194304 | tf_op jit(solution)/shard_map/all_to_all | solution.py:569
  148.5 0.9 collective-permute-start.12
  149.4 1.2 collective-permute-start.10
  150.6 1.8 collective-permute-start.8
  152.4 21.1 %collective-permute-done.12.refs_6_ = f32[128,1024]{1,0:T(8,128)S(1)} collective-permute-done((f32[128,1024]{1,0:T(8,128)S(1)}, f32[128,1024]{1,0:T(8,128)S(1)}, u32[]{:S(2)}, u32[]{:S(2)}) %collective-permute-start.12) | collective-permute-done | bytes 524320 | tf_op jit(solution)/shard_map/ppermute | solution.py:529
  173.5 0.8 copy-done.4
  174.3 0.8 copy-done.6
  175.8 3.2 owner_rows.1
  179.0 0.8 copy-done.3
  180.9 4.5 %collective-permute-start.15 = (f32[128,1024]{1,0:T(8,128)}, f32[128,1024]{1,0:T(8,128)}, u32[]{:S(2)}, u32[]{:S(2)}) collective-permute-start(f32[128,1024]{1,0:T(8,128)} %copy-done.3), channel_id=1, source_target_pairs={{0,0},{1,16},{2,32},{3,48},{4,64},{5,80},{6,96},{7,112},{8,1},{9,1... | collective-permute-start | bytes 1572872 | tf_op jit(solution)/shard_map/ppermute | solution.py:573
  185.4 5.3 %pack.1 = f32[128,128,128]{2,1,0:T(8,128)} custom-call(s32[3]{0:T(128)} %copy-done.13, s32[8,32]{1,0:T(8,128)} %cmap.9, f32[1024,1024]{1,0:T(8,128)} %child.3), custom_call_target="tpu_custom_call" | custom-call | tf_op jit(solution)/shard_map/pack/pallas_call | solution.py:136
  190.8 0.8 copy-done.8
  191.6 17.1 %collective-permute-done.15.refs_0_ = f32[128,1024]{1,0:T(8,128)} collective-permute-done((f32[128,1024]{1,0:T(8,128)}, f32[128,1024]{1,0:T(8,128)}, u32[]{:S(2)}, u32[]{:S(2)}) %collective-permute-start.15) | collective-permute-done | bytes 524320 | tf_op jit(solution)/shard_map/ppermute | solution.py:573
  208.7 16.0 %all-to-all-start.3 = ((f32[128,128,128]{2,1,0:T(8,128)}), f32[128,128,128]{2,1,0:T(8,128)}, u32[]{:S(2)}, u32[]{:S(2)}) async-start(f32[128,128,128]{2,1,0:T(8,128)} %pack.1), calls=%async_computation.3 | async-start | bytes 16777216 | tf_op jit(solution)/shard_map/all_to_all | solution.py:575
  224.7 0.9 collective-permute-start.18
  225.6 1.2 collective-permute-start.17
  226.8 2.1 collective-permute-start.16
  228.9 1.2 copy-done.9
  230.1 56.6 %factor.1.w_ref = f32[1024,1024]{1,0:T(8,128)S(1)} custom-call(s32[3]{0:T(128)S(1)} %copy-done.16, f32[128,1024]{1,0:T(8,128)S(1)} %diag_rows.1.refs_0_, f32[128,1024]{1,0:T(8,128)S(1)} %collective-permute-done.7.refs_1_, f32[128,1024]{1,0:T(8,128)} %collective-permute-done.8.refs_2_, f32[128,1024]{1,0:T(8,128)S(1)} %copy-done.9, f32[128,1024]{1,0:T(8,128)S(1)} %copy-done.7, ...), custom_call_target="tpu_custom_call" | custom-call | tf_op jit(solution)/shard_map/factor/pallas_call | solution.py:333
  286.7 2.1 copy-done.1
  288.8 41.1 %collective-permute-done.18.refs_6_ = f32[128,1024]{1,0:T(8,128)} collective-permute-done((f32[128,1024]{1,0:T(8,128)}, f32[128,1024]{1,0:T(8,128)}, u32[]{:S(2)}, u32[]{:S(2)}) %collective-permute-start.18) | collective-permute-done | bytes 524320 | tf_op jit(solution)/shard_map/ppermute | solution.py:529
  329.8 14.8 %collective-permute-done.17.refs_4_ = f32[128,1024]{1,0:T(8,128)} collective-permute-done((f32[128,1024]{1,0:T(8,128)}, f32[128,1024]{1,0:T(8,128)}, u32[]{:S(2)}, u32[]{:S(2)}) %collective-permute-start.17) | collective-permute-done | bytes 524320 | tf_op jit(solution)/shard_map/ppermute | solution.py:529
  346.8 0.7 collective-permute-done.20.refs_3_
  347.5 0.7 collective-permute-done.21.refs_5_
  348.3 0.7 collective-permute-done.22.refs_7_
  349.0 4.5 %all-gather.4.cloned.1.call-done.refs_8_ = f32[2048,1024]{1,0:T(8,128)} async-done(((f32[128,1024]{1,0:T(8,128)}), f32[2048,1024]{1,0:T(8,128)}) %all-gather.4.cloned.1.call-update) | async-done | bytes 8388624 | tf_op jit(solution)/shard_map/all_gather | solution.py:571
  353.6 35.6 %update.1.base = f32[2048,1024]{1,0:T(8,128)} custom-call(s32[3]{0:T(128)} %copy-done.13, s32[16,8]{1,0:T(8,128)} %copy.15.pattern, f32[1024,1024]{1,0:T(8,128)} %copy-done.1, f32[128,1024]{1,0:T(8,128)} %collective-permute-done.15.refs_0_, f32[128,1024]{1,0:T(8,128)} %copy-done.18, f32[128,1024]{1,0:T(8,128)} %collective-permute-done.16.refs_2_, ...), custom_call_target="tpu_custom_call" | custom-call | tf_op jit(solution)/shard_map/update/pallas_call | solution.py:440
  389.2 18.0 %add.41 = f32[2048,1024]{1,0:T(8,128)} custom-call(s32[2,32]{1,0:T(2,128)} %pad_add_fusion.places, f32[2048,1024]{1,0:T(8,128)} %update.1.base, f32[128,128,128]{2,1,0:T(8,128)} %all-to-all-done.3.came), custom_call_target="tpu_custom_call" | custom-call | tf_op jit(solution)/shard_map/add/pallas_call | solution.py:501
  (76 shorter events, 8.1 us)
Async XLA Ops:
  6.5 13.1 %copy-start.10 = (s32[8,32]{1,0:T(8,128)S(1)}, s32[8,32]{1,0:T(8,128)}, u32[]{:S(2)}) copy-start(s32[8,32]{1,0:T(8,128)} %cmap.9) | copy-start | bytes 3076
  15.4 121.7 %copy-start.11 = (s32[8,32]{1,0:T(8,128)S(1)}, s32[8,32]{1,0:T(8,128)}, u32[]{:S(2)}) copy-start(s32[8,32]{1,0:T(8,128)} %cmap.9) | copy-start | bytes 3076
  15.4 14.1 %collective-permute-start = (f32[8,128,128]{2,1,0:T(8,128)}, f32[8,128,128]{2,1,0:T(8,128)S(1)}, u32[]{:S(2)}, u32[]{:S(2)}) collective-permute-start(f32[8,128,128]{2,1,0:T(8,128)} %get-tuple-element.23), channel_id=1, source_target_pairs={{0,7},{1,14}} | collective-permute-start | bytes 1572872 | tf_op jit(solution)/shard_map/ppermute | solution.py:560
  16.2 14.6 %collective-permute-start.1 = (f32[8,128,128]{2,1,0:T(8,128)}, f32[8,128,128]{2,1,0:T(8,128)S(1)}, u32[]{:S(2)}, u32[]{:S(2)}) collective-permute-start(f32[8,128,128]{2,1,0:T(8,128)} %get-tuple-element.24), channel_id=1, source_target_pairs={{0,6},{1,13},{16,21},{32,38},{48,55},{64,77},{80,94},{96,111},{112... | collective-permute-start | bytes 1572872 | tf_op jit(solution)/shard_map/ppermute | solution.py:560
  16.9 14.6 %collective-permute-start.2 = (f32[8,128,128]{2,1,0:T(8,128)}, f32[8,128,128]{2,1,0:T(8,128)S(1)}, u32[]{:S(2)}, u32[]{:S(2)}) collective-permute-start(f32[8,128,128]{2,1,0:T(8,128)} %get-tuple-element.25), channel_id=1, source_target_pairs={{0,5},{1,12},{16,31},{3,24},{32,37},{5,41},{48,54},{7,58},{64,71},... | collective-permute-start | bytes 1572872 | tf_op jit(solution)/shard_map/ppermute | solution.py:560
  19.6 2.2 copy-start
  21.8 59.6 %copy-start.13 = (s32[3]{0:T(128)}, s32[3]{0:T(128)S(1)}, u32[]{:S(2)}) copy-start(s32[3]{0:T(128)S(1)} %pad_add_fusion.1.ids) | copy-start | bytes 40
  23.3 38.3 %all-to-all-start = ((f32[8,2,128,128]{3,2,1,0:T(8,128)}), f32[8,2,128,128]{3,2,1,0:T(8,128)S(1)}, u32[]{:S(2)}, u32[]{:S(2)}) async-start(f32[8,2,128,128]{3,2,1,0:T(8,128)} %pack_small.1), calls=%async_computation | async-start | bytes 2097152 | tf_op jit(solution)/shard_map/all_to_all | solution.py:557
  28.1 108.9 %all-gather.6.cloned.1.call-start = ((), (), s32[]{:S(2)}) async-start(), calls=%async_computation.5 | async-start | bytes 3342336 | tf_op jit(solution)/shard_map/all_gather | solution.py:566
  28.1 8.5 %collective-permute-start.3 = (f32[8,128,128]{2,1,0:T(8,128)}, f32[8,128,128]{2,1,0:T(8,128)S(1)}, u32[]{:S(2)}, u32[]{:S(2)}) collective-permute-start(f32[8,128,128]{2,1,0:T(8,128)} %get-tuple-element.26), channel_id=1, source_target_pairs={{0,4},{1,11},{2,17},{16,30},{3,28},{4,34},{32,47},{5,40},{6,51},{4... | collective-permute-start | bytes 1572872 | tf_op jit(solution)/shard_map/ppermute | solution.py:560
  28.8 7.8 %collective-permute-start.4 = (f32[8,128,128]{2,1,0:T(8,128)}, f32[8,128,128]{2,1,0:T(8,128)S(1)}, u32[]{:S(2)}, u32[]{:S(2)}) collective-permute-start(f32[8,128,128]{2,1,0:T(8,128)} %get-tuple-element.27), channel_id=1, source_target_pairs={{0,3},{1,10},{2,20},{16,29},{3,27},{4,33},{32,46},{5,44},{6,50},{4... | collective-permute-start | bytes 1572872 | tf_op jit(solution)/shard_map/ppermute | solution.py:560
  29.5 30.7 %collective-permute-start.5 = (f32[8,128,128]{2,1,0:T(8,128)}, f32[8,128,128]{2,1,0:T(8,128)S(1)}, u32[]{:S(2)}, u32[]{:S(2)}) collective-permute-start(f32[8,128,128]{2,1,0:T(8,128)} %get-tuple-element.28), channel_id=1, source_target_pairs={{0,2},{1,9},{2,19},{16,23},{3,26},{4,36},{32,45},{5,43},{6,49},{48... | collective-permute-start | bytes 1572872 | tf_op jit(solution)/shard_map/ppermute | solution.py:560
  30.9 29.4 %collective-permute-start.6 = (f32[8,128,128]{2,1,0:T(8,128)}, f32[8,128,128]{2,1,0:T(8,128)S(1)}, u32[]{:S(2)}, u32[]{:S(2)}) collective-permute-start(f32[8,128,128]{2,1,0:T(8,128)} %get-tuple-element.29), channel_id=1, source_target_pairs={{0,1},{1,8},{2,18},{16,22},{3,25},{4,35},{32,39},{5,42},{6,52},{48... | collective-permute-start | bytes 1572872 | tf_op jit(solution)/shard_map/ppermute | solution.py:560
  31.6 28.7 %copy-start.22 = (f32[8,128,128]{2,1,0:T(8,128)}, f32[8,128,128]{2,1,0:T(8,128)S(1)}, u32[]{:S(2)}) copy-start(f32[8,128,128]{2,1,0:T(8,128)S(1)} %collective-permute-done.2) | copy-start | bytes 1572868
  31.6 28.7 %collective-permute-start.14 = (f32[8,128,128]{2,1,0:T(8,128)}, f32[8,128,128]{2,1,0:T(8,128)S(1)}, u32[]{:S(2)}, u32[]{:S(2)}) collective-permute-start(f32[8,128,128]{2,1,0:T(8,128)} %get-tuple-element.32), channel_id=1, source_target_pairs={{1,15}} | collective-permute-start | bytes 1572872 | tf_op jit(solution)/shard_map/ppermute | solution.py:560
  61.7 19.8 %copy-start.17 = (f32[8,2,128,128]{3,2,1,0:T(8,128)}, f32[8,2,128,128]{3,2,1,0:T(8,128)S(1)}, u32[]{:S(2)}) copy-start(f32[8,2,128,128]{3,2,1,0:T(8,128)S(1)} %all-to-all-done.came) | copy-start | bytes 3145732
  137.1 1.9 copy-start.2
  142.7 32.3 %all-to-all-start.2 = ((f32[16,2,128,128]{3,2,1,0:T(8,128)}), f32[16,2,128,128]{3,2,1,0:T(8,128)S(1)}, u32[]{:S(2)}, u32[]{:S(2)}) async-start(f32[16,2,128,128]{3,2,1,0:T(8,128)} %get-tuple-element.34), calls=%async_computation.2 | async-start | bytes 4194304 | tf_op jit(solution)/shard_map/all_to_all | solution.py:569
  148.4 205.1 %all-gather.4.cloned.1.call-start = ((), (), s32[]{:S(2)}) async-start(), calls=%async_computation.4 | async-start | bytes 8912896 | tf_op jit(solution)/shard_map/all_gather | solution.py:571
  148.5 25.0 %collective-permute-start.12 = (f32[128,1024]{1,0:T(8,128)S(1)}, f32[128,1024]{1,0:T(8,128)S(1)}, u32[]{:S(2)}, u32[]{:S(2)}) collective-permute-start(f32[128,1024]{1,0:T(8,128)S(1)} %diag_rows.1.refs_0_), channel_id=1, source_target_pairs={{0,96},{16,112},{32,0},{48,16},{64,32},{80,48},{96,64},{112,80},{1... | collective-permute-start | bytes 1572872 | tf_op jit(solution)/shard_map/ppermute | solution.py:529
  149.4 24.1 %collective-permute-start.10 = (f32[128,1024]{1,0:T(8,128)S(1)}, f32[128,1024]{1,0:T(8,128)S(1)}, u32[]{:S(2)}, u32[]{:S(2)}) collective-permute-start(f32[128,1024]{1,0:T(8,128)S(1)} %diag_rows.1.refs_0_), channel_id=1, source_target_pairs={{0,64},{16,80},{32,96},{48,112},{64,0},{80,16},{96,32},{112,48},{1... | collective-permute-start | bytes 1572872 | tf_op jit(solution)/shard_map/ppermute | solution.py:529
  150.6 24.5 %collective-permute-start.8 = (f32[128,1024]{1,0:T(8,128)S(1)}, f32[128,1024]{1,0:T(8,128)}, u32[]{:S(2)}, u32[]{:S(2)}) collective-permute-start(f32[128,1024]{1,0:T(8,128)S(1)} %diag_rows.1.refs_0_), channel_id=1, source_target_pairs={{0,32},{16,48},{32,64},{48,80},{64,96},{80,112},{96,0},{112,16},{1... | collective-permute-start | bytes 1572872 | tf_op jit(solution)/shard_map/ppermute | solution.py:529
  173.5 0.8 copy-start.4
  174.3 0.8 copy-start.6
  179.0 0.8 copy-start.3
  179.8 10.9 %collective-permute-start.7 = (f32[128,1024]{1,0:T(8,128)S(1)}, f32[128,1024]{1,0:T(8,128)S(1)}, u32[]{:S(2)}, u32[]{:S(2)}) collective-permute-start(f32[128,1024]{1,0:T(8,128)S(1)} %diag_rows.1.refs_0_), channel_id=1, source_target_pairs={{0,16},{16,0},{32,48},{48,32},{64,80},{80,64},{96,112},{112,96},{1... | collective-permute-start | bytes 1572872 | tf_op jit(solution)/shard_map/ppermute | solution.py:536
  179.9 10.8 %collective-permute-start.13 = (f32[128,1024]{1,0:T(8,128)}, f32[128,1024]{1,0:T(8,128)S(1)}, u32[]{:S(2)}, u32[]{:S(2)}) collective-permute-start(f32[128,1024]{1,0:T(8,128)} %copy-done.4), channel_id=1, source_target_pairs={{0,16},{16,0},{32,48},{48,32},{64,80},{80,64},{96,112},{112,96},{1... | collective-permute-start | bytes 1572872 | tf_op jit(solution)/shard_map/ppermute | solution.py:536
  180.4 10.3 %collective-permute-start.11 = (f32[128,1024]{1,0:T(8,128)}, f32[128,1024]{1,0:T(8,128)S(1)}, u32[]{:S(2)}, u32[]{:S(2)}) collective-permute-start(f32[128,1024]{1,0:T(8,128)} %copy-done.6), channel_id=1, source_target_pairs={{0,16},{16,0},{32,48},{48,32},{64,80},{80,64},{96,112},{112,96},{1... | collective-permute-start | bytes 1572872 | tf_op jit(solution)/shard_map/ppermute | solution.py:536
  180.5 10.3 %collective-permute-start.9 = (f32[128,1024]{1,0:T(8,128)}, f32[128,1024]{1,0:T(8,128)S(1)}, u32[]{:S(2)}, u32[]{:S(2)}) collective-permute-start(f32[128,1024]{1,0:T(8,128)} %collective-permute-done.8.refs_2_), channel_id=1, source_target_pairs={{0,16},{16,0},{32,48},{48,32},{64,80},{80,64},{96,112},{112,96},{1... | collective-permute-start | bytes 1572872 | tf_op jit(solution)/shard_map/ppermute | solution.py:536
  180.9 27.8 %collective-permute-start.15 = (f32[128,1024]{1,0:T(8,128)}, f32[128,1024]{1,0:T(8,128)}, u32[]{:S(2)}, u32[]{:S(2)}) collective-permute-start(f32[128,1024]{1,0:T(8,128)} %copy-done.3), channel_id=1, source_target_pairs={{0,0},{1,16},{2,32},{3,48},{4,64},{5,80},{6,96},{7,112},{8,1},{9,1... | collective-permute-start | bytes 1572872 | tf_op jit(solution)/shard_map/ppermute | solution.py:573
  190.7 38.2 %copy-start.5 = (f32[128,1024]{1,0:T(8,128)S(1)}, f32[128,1024]{1,0:T(8,128)}, u32[]{:S(2)}) copy-start(f32[128,1024]{1,0:T(8,128)} %copy-done.4) | copy-start | bytes 1572868
  190.7 38.2 %copy-start.7 = (f32[128,1024]{1,0:T(8,128)S(1)}, f32[128,1024]{1,0:T(8,128)}, u32[]{:S(2)}) copy-start(f32[128,1024]{1,0:T(8,128)} %copy-done.6) | copy-start | bytes 1572868
  190.7 38.1 %copy-start.16 = (s32[3]{0:T(128)S(1)}, s32[3]{0:T(128)}, u32[]{:S(2)}) copy-start(s32[3]{0:T(128)} %copy-done.13) | copy-start | bytes 40
  208.7 137.0 %copy-start.12 = (s32[8,32]{1,0:T(8,128)S(1)}, s32[8,32]{1,0:T(8,128)}, u32[]{:S(2)}) copy-start(s32[8,32]{1,0:T(8,128)} %cmap.9) | copy-start | bytes 3076
  208.7 180.5 %all-to-all-start.3 = ((f32[128,128,128]{2,1,0:T(8,128)}), f32[128,128,128]{2,1,0:T(8,128)}, u32[]{:S(2)}, u32[]{:S(2)}) async-start(f32[128,128,128]{2,1,0:T(8,128)} %pack.1), calls=%async_computation.3 | async-start | bytes 16777216 | tf_op jit(solution)/shard_map/all_to_all | solution.py:575
  224.7 105.1 %collective-permute-start.18 = (f32[128,1024]{1,0:T(8,128)}, f32[128,1024]{1,0:T(8,128)}, u32[]{:S(2)}, u32[]{:S(2)}) collective-permute-start(f32[128,1024]{1,0:T(8,128)} %collective-permute-done.15.refs_0_), channel_id=1, source_target_pairs={{0,96},{16,112},{32,0},{48,16},{64,32},{80,48},{96,64},{112,80},{1... | collective-permute-start | bytes 1572872 | tf_op jit(solution)/shard_map/ppermute | solution.py:529
  225.6 119.0 %collective-permute-start.17 = (f32[128,1024]{1,0:T(8,128)}, f32[128,1024]{1,0:T(8,128)}, u32[]{:S(2)}, u32[]{:S(2)}) collective-permute-start(f32[128,1024]{1,0:T(8,128)} %collective-permute-done.15.refs_0_), channel_id=1, source_target_pairs={{0,64},{16,80},{32,96},{48,112},{64,0},{80,16},{96,32},{112,48},{1... | collective-permute-start | bytes 1572872 | tf_op jit(solution)/shard_map/ppermute | solution.py:529
  226.8 117.9 %collective-permute-start.16 = (f32[128,1024]{1,0:T(8,128)}, f32[128,1024]{1,0:T(8,128)}, u32[]{:S(2)}, u32[]{:S(2)}) collective-permute-start(f32[128,1024]{1,0:T(8,128)} %collective-permute-done.15.refs_0_), channel_id=1, source_target_pairs={{0,32},{16,48},{32,64},{48,80},{64,96},{80,112},{96,0},{112,16},{1... | collective-permute-start | bytes 1572872 | tf_op jit(solution)/shard_map/ppermute | solution.py:529
  228.9 1.2 copy-start.9
  286.7 2.1 copy-start.1
  344.7 2.1 collective-permute-start.19
  344.7 2.9 collective-permute-start.20
  345.2 3.1 collective-permute-start.21
  345.2 3.9 collective-permute-start.22
  346.8 6.8 %copy-start.18 = (f32[128,1024]{1,0:T(8,128)}, f32[128,1024]{1,0:T(8,128)S(1)}, u32[]{:S(2)}) copy-start(f32[128,1024]{1,0:T(8,128)S(1)} %collective-permute-done.19.refs_1_) | copy-start | bytes 1572868
  347.5 6.0 %copy-start.19 = (f32[128,1024]{1,0:T(8,128)}, f32[128,1024]{1,0:T(8,128)S(1)}, u32[]{:S(2)}) copy-start(f32[128,1024]{1,0:T(8,128)S(1)} %collective-permute-done.20.refs_3_) | copy-start | bytes 1572868
  348.3 5.3 %copy-start.20 = (f32[128,1024]{1,0:T(8,128)}, f32[128,1024]{1,0:T(8,128)S(1)}, u32[]{:S(2)}) copy-start(f32[128,1024]{1,0:T(8,128)S(1)} %collective-permute-done.21.refs_5_) | copy-start | bytes 1572868
  349.0 4.6 %copy-start.21 = (f32[128,1024]{1,0:T(8,128)}, f32[128,1024]{1,0:T(8,128)S(1)}, u32[]{:S(2)}) copy-start(f32[128,1024]{1,0:T(8,128)S(1)} %collective-permute-done.22.refs_7_) | copy-start | bytes 1572868
  (3 other events, 2.1 us)
Sparse Core Ops, SparseCore 0:
  84.1 52.9 all-gather.5
  180.0 173.5 all-gather.3

commit v5 on v4

--- a/solution.py
+++ b/solution.py
@@ -18,6 +18,8 @@
 SMEM = pl.BlockSpec(memory_space=pltpu.SMEM)
 VMEM = pl.BlockSpec(memory_space=pltpu.VMEM)
 MIB = 1024 * 1024
+PARTS = 2
+PART = B // PARTS
 
 
 def params(mib):
@@ -119,26 +121,40 @@
     )(ids, cmap, child)
 
 
-def pack_kernel(ids, cmap, child, bulk, sems):
+def pack_kernel(ids, cmap, child, *rest):
+    bulk, sems = rest[:PARTS], rest[PARTS]
     r, c = ids[0], ids[1]
     mine = r // 4 * 4 + c // 4
 
-    def copy(n):
+    def copies(n):
         a, b = n // 8, n % 8
         slot = cmap[mine, r % 4 * 8 + a] // 16 * COLS + cmap[mine, c % 4 * 8 + b] // 8
-        return pltpu.make_async_copy(child.at[block(a), block(b)], bulk.at[slot], sems.at[n])
-
-    lax.fori_loop(0, 64, lambda n, _: (copy(n).start(), 0)[1], 0)
-    lax.fori_loop(0, 64, lambda n, _: (copy(n).wait(), 0)[1], 0)
+        for part in range(PARTS):
+            rows = pl.ds(pl.multiple_of(a * B + part * PART, PART), PART)
+            src = child.at[rows, block(b)]
+            yield pltpu.make_async_copy(src, bulk[part].at[slot], sems.at[n, part])
+
+    def start(n, _):
+        for m in copies(n):
+            m.start()
+        return 0
+
+    def wait(n, _):
+        for m in copies(n):
+            m.wait()
+        return 0
+
+    lax.fori_loop(0, 64, start, 0)
+    lax.fori_loop(0, 64, wait, 0)
 
 
 def pack(ids, cmap, child):
     return pl.pallas_call(
         pack_kernel,
-        out_shape=jax.ShapeDtypeStruct((ROWS * COLS, B, B), F32),
+        out_shape=(jax.ShapeDtypeStruct((ROWS * COLS, PART, B), F32),) * PARTS,
         in_specs=[SMEM, SMEM, VMEM],
-        out_specs=HBM,
-        scratch_shapes=[pltpu.SemaphoreType.DMA((64,))],
+        out_specs=(HBM,) * PARTS,
+        scratch_shapes=[pltpu.SemaphoreType.DMA((64, PARTS))],
         compiler_params=params(60),
         name="pack",
     )(ids, cmap, child)
@@ -366,33 +382,97 @@
         out[:, rows] = dot3(xh[:, :upto], xl[:, :upto], eh[rows, :upto], el[rows, :upto])
 
 
-def update_kernel(ids, pattern, w_ref, *refs):
-    pieces, (xr_ref, own_ref, out_ref, eh, el, ch, cl, x) = refs[:ROWS], refs[ROWS:]
+def columns_kernel(ids, w_ref, *refs):
+    pieces, (eh, el, ch, cl, x) = refs[:ROWS], refs[ROWS:]
+    row = lax.broadcasted_iota(jnp.int32, (B, W), 0)
+    col = lax.broadcasted_iota(jnp.int32, (B, W), 1)
+
+    def split(i, _):
+        rows = block(i)
+        high, low = halves(jnp.where(row + i * B >= col, w_ref[rows, :], 0.0))
+        eh[rows, :] = high
+        el[rows, :] = low
+        return 0
+
+    lax.fori_loop(0, NB, split, 0)
+    at_row = piece_rows(ids[0])
+    for n in range(0, ROWS, 2):
+        pair = jnp.concatenate([pieces[n][...], pieces[n + 1][...]], axis=0)
+        solve_rows(pair, x, eh, el)
+        for m in range(2):
+            high, low = halves(x[m * B : (m + 1) * B, :])
+            ch[block(at_row[n + m]), :] = high
+            cl[block(at_row[n + m]), :] = low
+
+
+def columns(ids, w, pieces):
+    return pl.pallas_call(
+        columns_kernel,
+        out_shape=(jax.ShapeDtypeStruct((W, W), BF16),) * 4,
+        in_specs=[SMEM, VMEM] + [VMEM] * ROWS,
+        out_specs=(VMEM,) * 4,
+        scratch_shapes=[pltpu.VMEM((CHUNK, W), F32)],
+        compiler_params=params(32),
+        name="columns",
+    )(ids, w, *pieces)
+
+
+def update_kernel(ids, pattern, places, w_ref, eh, el, ch, cl, xr_ref, own_ref, *refs):
+    came, (out_ref, x, held, sems) = refs[:PARTS], refs[PARTS:]
     step = pl.program_id(0)
     r, c = ids[0], ids[1]
 
+    def visit(group, act):
+        def one(quarter, _):
+            child = group // 4
+            slot = (child // 4 * 4 + group % 4) * COLS + child % 4 * 4 + quarter
+            col = places[1, child * 4 + quarter]
+
+            @pl.when(col >= 0)
+            def _():
+                copies = [
+                    pltpu.make_async_copy(
+                        came[part].at[slot],
+                        held.at[slot, pl.ds(part * PART, PART)],
+                        sems.at[slot, part],
+                    )
+                    for part in range(PARTS)
+                ]
+                act(copies, slot, col)
+
+            return 0
+
+        lax.fori_loop(0, 4, one, 0)
+
+    def begin(group, _):
+        def act(copies, slot, col):
+            for m in copies:
+                m.start()
+
+        @pl.when(places[0, group] >= 0)
+        def _():
+            visit(group, act)
+
+        return 0
+
+    def finish(group, _):
+        row = places[0, group]
+
+        def act(copies, slot, col):
+            for m in copies:
+                m.wait()
+            here = block(row % (CHUNK // B)), block(col)
+            out_ref[here] = out_ref[here] + held[slot]
+
+        @pl.when((row >= 0) & (row // (CHUNK // B) == step))
+        def _():
+            visit(group, act)
+
+        return 0
+
     @pl.when(step == 0)
     def _():
-        row = lax.broadcasted_iota(jnp.int32, (B, W), 0)
-        col = lax.broadcasted_iota(jnp.int32, (B, W), 1)
-
-        def split(i, _):
-            rows = block(i)
-            high, low = halves(jnp.where(row + i * B >= col, w_ref[rows, :], 0.0))
-            eh[rows, :] = high
-            el[rows, :] = low
-            return 0
-
-        lax.fori_loop(0, NB, split, 0)
-
-        at_row = piece_rows(r)
-        for n in range(0, ROWS, 2):
-            pair = jnp.concatenate([pieces[n][...], pieces[n + 1][...]], axis=0)
-            solve_rows(pair, x, eh, el)
-            for m in range(2):
-                high, low = halves(x[m * B : (m + 1) * B, :])
-                ch[block(at_row[n + m]), :] = high
-                cl[block(at_row[n + m]), :] = low
+        lax.fori_loop(0, 32, begin, 0)
 
     solve_rows(xr_ref[...], x, eh, el)
     top = (r == 0) & (step < W // CHUNK)
@@ -432,85 +512,27 @@
             out_ref[:, cols] = jnp.where(gap > 0, above, jnp.where(gap == 0, 1.0 / here, 0.0))
 
 
-def update(ids, pattern, w, xc, xr, own):
+    lax.fori_loop(0, 32, finish, 0)
+
+
+def update(ids, pattern, places, w, solved, xr, own, came):
     rows = own.shape[0]
     whole = pl.BlockSpec((W, W), lambda i: (0, 0), pipeline_mode=pl.Buffered(1))
-    piece = pl.BlockSpec((B, W), lambda i: (0, 0), pipeline_mode=pl.Buffered(1))
     part = pl.BlockSpec((CHUNK, W), lambda i: (i, 0))
     return pl.pallas_call(
         update_kernel,
         grid=(rows // CHUNK,),
         out_shape=jax.ShapeDtypeStruct(own.shape, F32),
-        in_specs=[SMEM, SMEM, whole] + [piece] * ROWS + [part, part],
+        in_specs=[SMEM, SMEM, SMEM] + [whole] * 5 + [part, part] + [HBM] * PARTS,
         out_specs=part,
-        scratch_shapes=[pltpu.VMEM((W, W), BF16)] * 4 + [pltpu.VMEM((CHUNK, W), F32)],
+        scratch_shapes=[
+            pltpu.VMEM((CHUNK, W), F32),
+            pltpu.VMEM((ROWS * COLS, B, B), F32),
+            pltpu.SemaphoreType.DMA((ROWS * COLS, PARTS)),
+        ],
         compiler_params=params(60),
         name="update",
-    )(ids, pattern, w, *xc, xr, own)
-
-
-def add_kernel(places, base, came, out, held, sems):
-    step = pl.program_id(0)
-
-    def visit(group, act):
-        def one(quarter, _):
-            child = group // 4
-            slot = (child // 4 * 4 + group % 4) * COLS + child % 4 * 4 + quarter
-            col = places[1, child * 4 + quarter]
-
-            @pl.when(col >= 0)
-            def _():
-                act(pltpu.make_async_copy(came.at[slot], held.at[slot], sems.at[slot]), slot, col)
-
-            return 0
-
-        lax.fori_loop(0, 4, one, 0)
-
-    @pl.when(step == 0)
-    def _():
-        def begin(group, _):
-            @pl.when(places[0, group] >= 0)
-            def _():
-                visit(group, lambda m, slot, col: m.start())
-
-            return 0
-
-        lax.fori_loop(0, 32, begin, 0)
-
-    out[...] = base[...]
-
-    def finish(group, _):
-        row = places[0, group]
-
-        def act(m, slot, col):
-            m.wait()
-            here = block(row % (CHUNK // B)), block(col)
-            out[here] = out[here] + held[slot]
-
-        @pl.when((row >= 0) & (row // (CHUNK // B) == step))
-        def _():
-            visit(group, act)
-
-        return 0
-
-    lax.fori_loop(0, 32, finish, 0)
-
-
-def add(places, base, came):
-    part = pl.BlockSpec((CHUNK, W), lambda i: (i, 0))
-    return pl.pallas_call(
-        add_kernel,
-        grid=(base.shape[0] // CHUNK,),
-        out_shape=jax.ShapeDtypeStruct(base.shape, F32),
-        in_specs=[SMEM, part, HBM],
-        out_specs=part,
-        scratch_shapes=[
-            pltpu.VMEM((ROWS * COLS, B, B), F32),
-            pltpu.SemaphoreType.DMA((ROWS * COLS,)),
-        ],
-        compiler_params=params(60),
-        name="add",
-    )(places, base, came)
+    )(ids, pattern, places, w, *solved, xr, own, *came)
 
 
 def at(r, c):
@@ -553,14 +575,17 @@
     )
 
     *pieces, start = pack_parent(sends, pattern, own)
-    small = pack_small(ids, cmap, child)
+    small = pack_small(after(ids, start), cmap, child)
     small = lax.all_to_all(small, "prow", 0, 0, tiled=True)
+    pieces = [lax.ppermute(p, AXES, m) for p, m in zip(pieces, moves)]
+    bulk = list(pack(ids, cmap, child))
+    first = after(bulk[0], (small, pieces[:3]))
+    bulk[0] = lax.all_to_all(first, AXES, 0, 0, tiled=True)
     top = start
     for step, piece in enumerate(pieces):
-        piece = lax.ppermute(piece, AXES, moves[step])
         start = jnp.where(mine[0] == step, piece, start)
         top = start if step == NB - 2 else top
-    parent = lax.all_to_all(top, "prow", 0, 0, tiled=True)
+    parent = lax.all_to_all(after(top, bulk[0]), "prow", 0, 0, tiled=True)
 
     owners, diag = relay(ids, cmap, small, parent)
     diag = lax.all_gather(diag, "pcol", axis=0)
@@ -571,13 +596,11 @@
     xr = lax.all_gather(owned, "pcol", axis=0, tiled=True)
     to = [(at(r, c), at(c % 8, 2 * r + c // 8)) for r in range(ROWS) for c in range(COLS)]
     xc = lax.ppermute(owned, AXES, to)
-    bulk = after(pack(ids, cmap, child), (xc, pivot))
-    bulk = lax.all_to_all(bulk, AXES, 0, 0, tiled=True)
+    bulk[1] = lax.all_to_all(after(bulk[1], (xc, pivot)), AXES, 0, 0, tiled=True)
     xc = along_x(xc)
     w = factor(ids, pivot)
-    xc = across(after(xc, w))
-    base = update(ids, pattern, w, xc, xr, own)
-    return add(places, base, bulk)
+    solved = columns(ids, w, across(after(xc, w)))
+    return update(ids, pattern, places, w, solved, xr, own, bulk)
 
 
 def solution(mesh):

time: 421 us -> 440 us (1.045)
  waiting for transfers between devices: 178 us -> 153 us
  starting transfers between devices: 47.4 us -> 66.9 us
  blocking collectives: 19.8 us -> 33.9 us
  local copies, waits for them, and re-layouts: 16 us -> 29.5 us
    ppermute x6, waiting for transfers between devices: 77 us -> 22.9 us  [along_x(): pieces.append(lax.ppermute(piece, 'prow', to))]
    all_to_all x1 -> x2, waiting for transfers between devices: 0.01 us -> 41.5 us  [the longest x1 41.5 us: body(): bulk[0] = lax.all_to_all(first, AXES, 0, 0, tiled=True)]
    all_to_all x1 -> x2, starting transfers between devices: 16 us -> 34.6 us  [the longest x1 17.4 us: body(): lax.all_to_all(after(bulk[1], (xc, pivot)), AXES, 0, 0, tiled=True)]
    all_to_all x1, blocking collectives: 19.8 us -> 33.9 us  [body(): parent = lax.all_to_all(after(top, bulk[0]), 'prow', 0, 0, tiled=True)]
    unnamed x47 -> x65, local copies, waits for them, and re-layouts: 13.2 us -> 26.8 us
    pallas_call x1, Pallas kernels: 35.6 us -> 46.5 us  [update(): pl.pallas_call(update_kernel, grid=(rows // CHUNK,), out_shape=jax.ShapeD...]
    pallas_call x2, Pallas kernels: 23.2 us -> 12.7 us  [the longest x1 6.75 us: columns(): pl.pallas_call(columns_kernel, out_shape=(jax.ShapeDtypeStruct((W, W), BF...]
    ppermute x8, waiting for transfers between devices: 23.6 us -> 16.3 us  [body(): pieces = [lax.ppermute(p, AXES, m) for p, m in zip(pieces, moves)]]
  transfers between devices with their start and end apart: 28 -> 29, of which waited for: 11 -> 10; matrix products, arithmetic and copies ran while one was open for 1% -> 1% of each run, Pallas kernels for 24% -> 16%
where the time goes in v5:
time: 440 us; the launch traced here: 437 us
  waiting for transfers between devices  153 us (35%)
  Pallas kernels  132 us (30%)
  starting transfers between devices  66.9 us (15%)
  blocking collectives  33.9 us (8%)
  local copies, waits for them, and re-layouts  29.5 us (7%)
  between operations  18.9 us (4%)
    pallas_call x1, Pallas kernels, factor(): pl.pallas_call(factor_kernel, out_shape=jax.ShapeDtypeStruct((W, W), F32)...  56.3 us
    all_gather x1, waiting for transfers between devices, body(): diag = lax.all_gather(diag, 'pcol', axis=0)  51 us
    pallas_call x1, Pallas kernels, update(): pl.pallas_call(update_kernel, grid=(rows // CHUNK,), out_shape=jax.ShapeD...  46.5 us
    all_to_all x1, waiting for transfers between devices, body(): bulk[0] = lax.all_to_all(first, AXES, 0, 0, tiled=True)  41.5 us
    all_to_all x1, blocking collectives, body(): parent = lax.all_to_all(after(top, bulk[0]), 'prow', 0, 0, tiled=True)  33.9 us
    unnamed x65, local copies, waits for them, and re-layouts  26.8 us
    ppermute x6, waiting for transfers between devices, along_x(): pieces.append(lax.ppermute(piece, 'prow', to))  22.9 us
    ppermute x1, waiting for transfers between devices, body(): xc = lax.ppermute(owned, AXES, to)  18.6 us
  transfers between devices with their start and end apart: 29, of which 10 were waited for; matrix products, arithmetic and copies ran while one was open for 1% of the time, Pallas kernels for 16%

profile of v5, /device:TPU:14, one launch (start us, length us, event | category | flops | bytes accessed | tf_op | source)
XLA Modules:
  0.0 436.9 jit_solution(1804222788936490849)
XLA Ops:
  9.2 1.3 copy.15.pattern
  11.2 6.1 %pack_parent.1 = (f32[8,128,128]{2,1,0:T(8,128)}, f32[8,128,128]{2,1,0:T(8,128)}, f32[8,128,128]{2,1,0:T(8,128)}, f32[8,128,128]{2,1,0:T(8,128)}, f32[8,128,128]...) custom-call(s32[8,2]{1,0:T(8,128)} %copy.13.sends, ...), custom_call_target="tpu_custom_call" | custom-call | tf_op jit(solution)/shard_map/pack_parent/pallas_call | solution.py:84
  17.4 2.2 copy-done.2
  19.6 1.6 pack_small.1
  21.1 4.8 %all-to-all-start = ((f32[8,2,128,128]{3,2,1,0:T(8,128)}), f32[8,2,128,128]{3,2,1,0:T(8,128)S(1)}, u32[]{:S(2)}, u32[]{:S(2)}) async-start(f32[8,2,128,128]{3,2,1,0:T(8,128)} %pack_small.1), calls=%async_computation | async-start | bytes 2097152 | tf_op jit(solution)/shard_map/all_to_all | solution.py:579
  26.6 1.3 collective-permute-start.5
  27.9 1.5 collective-permute-start.6
  29.4 6.0 %pack.1 = (f32[128,64,128]{2,1,0:T(8,128)}, f32[128,64,128]{2,1,0:T(8,128)}) custom-call(s32[3]{0:T(128)} %copy-done.23, s32[8,32]{1,0:T(8,128)} %cmap.9, f32[1024,1024]{1,0:T(8,128)} %child.3), custom_call_target="tpu_custom_call" | custom-call | tf_op jit(solution)/shard_map/pack/pallas_call | solution.py:152
  35.4 16.3 %collective-permute-done.5 = f32[8,128,128]{2,1,0:T(8,128)S(1)} collective-permute-done((f32[8,128,128]{2,1,0:T(8,128)S(1)}, f32[8,128,128]{2,1,0:T(8,128)S(1)}, u32[]{:S(2)}, u32[]{:S(2)}) %collective-permute-start.5) | collective-permute-done | bytes 524320 | tf_op jit(solution)/shard_map/ppermute | solution.py:580
  52.5 1.0 copy-done.25
  53.5 17.2 %all-to-all-start.1 = ((f32[128,64,128]{2,1,0:T(8,128)}), f32[128,64,128]{2,1,0:T(8,128)}, u32[]{:S(2)}, u32[]{:S(2)}) async-start(f32[128,64,128]{2,1,0:T(8,128)} %get-tuple-element.42), calls=%async_computation.1 | async-start | bytes 8388608 | tf_op jit(solution)/shard_map/all_to_all | solution.py:583
  79.5 1.4 broadcast_select_fusion
  80.9 41.5 %all-to-all-done.1.refs_0_ = f32[128,64,128]{2,1,0:T(8,128)} async-done(((f32[128,64,128]{2,1,0:T(8,128)}), f32[128,64,128]{2,1,0:T(8,128)}, u32[]{:S(2)}, u32[]{:S(2)}) %all-to-all-start.1) | async-done | bytes 4194336 | tf_op jit(solution)/shard_map/all_to_all | solution.py:583
  122.4 33.9 %all_to_all.25.parent = f32[8,128,128]{2,1,0:T(8,128)} all-to-all(f32[8,128,128]{2,1,0:T(8,128)S(1)} %get-tuple-element.43), channel_id=1, replica_groups=mesh['prow'=8,'pcol'=16] {'prow'}, dimensions={0} | all-to-all | bytes 1048576 | tf_op jit(solution)/shard_map/all_to_all | solution.py:588
  156.4 2.5 relay.1
  158.9 51.0 %all-gather.6.cloned.1.call-done = f32[48,128,128]{2,1,0:T(8,128)} async-done(((f32[3,128,128]{2,1,0:T(8,128)}), f32[48,128,128]{2,1,0:T(8,128)}) %all-gather.6.cloned.1.call-update) | async-done | bytes 3145744 | tf_op jit(solution)/shard_map/all_gather | solution.py:591
  209.9 1.9 copy-done.3
  211.8 3.1 diag_rows.1.refs_0_
  214.9 5.7 %all-to-all-start.3 = ((f32[16,2,128,128]{3,2,1,0:T(8,128)}), f32[16,2,128,128]{3,2,1,0:T(8,128)S(1)}, u32[]{:S(2)}, u32[]{:S(2)}) async-start(f32[16,2,128,128]{3,2,1,0:T(8,128)} %get-tuple-element.47), calls=%async_computation.3 | async-start | bytes 4194304 | tf_op jit(solution)/shard_map/all_to_all | solution.py:594
  221.4 1.2 collective-permute-start.10
  222.6 2.1 collective-permute-start.8
  224.7 21.0 %collective-permute-done.12.refs_6_ = f32[128,1024]{1,0:T(8,128)S(1)} collective-permute-done((f32[128,1024]{1,0:T(8,128)S(1)}, f32[128,1024]{1,0:T(8,128)S(1)}, u32[]{:S(2)}, u32[]{:S(2)}) %collective-permute-start.12) | collective-permute-done | bytes 524320 | tf_op jit(solution)/shard_map/ppermute | solution.py:551
  245.7 0.8 copy-done.9
  246.5 0.8 copy-done.11
  247.4 3.0 owner_rows.1
  250.4 0.8 copy-done.8
  252.3 4.5 %collective-permute-start.15 = (f32[128,1024]{1,0:T(8,128)}, f32[128,1024]{1,0:T(8,128)S(1)}, u32[]{:S(2)}, u32[]{:S(2)}) collective-permute-start(f32[128,1024]{1,0:T(8,128)} %copy-done.8), channel_id=1, source_target_pairs={{0,0},{1,16},{2,32},{3,48},{4,64},{5,80},{6,96},{7,112},{8,1},{9,1... | collective-permute-start | bytes 1572872 | tf_op jit(solution)/shard_map/ppermute | solution.py:598
  257.7 0.8 copy-done.15
  260.1 18.6 %collective-permute-done.15.refs_0_ = f32[128,1024]{1,0:T(8,128)S(1)} collective-permute-done((f32[128,1024]{1,0:T(8,128)}, f32[128,1024]{1,0:T(8,128)S(1)}, u32[]{:S(2)}, u32[]{:S(2)}) %collective-permute-start.15) | collective-permute-done | bytes 524320 | tf_op jit(solution)/shard_map/ppermute | solution.py:598
  278.8 17.4 %all-to-all-start.4 = ((f32[128,64,128]{2,1,0:T(8,128)}), f32[128,64,128]{2,1,0:T(8,128)}, u32[]{:S(2)}, u32[]{:S(2)}) async-start(f32[128,64,128]{2,1,0:T(8,128)} %get-tuple-element.58), calls=%async_computation.4 | async-start | bytes 8388608 | tf_op jit(solution)/shard_map/all_to_all | solution.py:599
  296.2 0.9 collective-permute-start.18
  297.1 1.2 collective-permute-start.17
  298.3 2.1 collective-permute-start.16
  300.4 1.2 copy-done.14
  301.6 1.1 copy-done.16
  302.7 1.0 copy-done.18
  303.7 1.0 copy-done.20
  304.7 56.3 %factor.1.w_ref = f32[1024,1024]{1,0:T(8,128)S(1)} custom-call(s32[3]{0:T(128)S(1)} %copy-done.24, f32[128,1024]{1,0:T(8,128)S(1)} %diag_rows.1.refs_0_, f32[128,1024]{1,0:T(8,128)S(1)} %copy-done.14, f32[128,1024]{1,0:T(8,128)} %collective-permute-done.8.refs_2_, f32[128,1024]{1,0:T(8,128)S(1)} %copy-done.20, f32[128,1024]{1,0:T(8,128)S(1)} %copy-done.12, ...), custom_call_target="tpu_custom_call" | custom-call | tf_op jit(solution)/shard_map/factor/pallas_call | solution.py:349
  361.0 2.0 copy-done
  363.0 1.9 collective-permute-done.17.refs_4_
  368.2 0.9 collective-permute-done.21.refs_5_
  369.2 2.2 copy-done.1
  371.4 6.8 %columns.1 = (bf16[1024,1024]{1,0:T(8,128)(2,1)S(1)}, bf16[1024,1024]{1,0:T(8,128)(2,1)S(1)}, bf16[1024,1024]{1,0:T(8,128)(2,1)S(1)}, bf16[1024,1024]{1,0:T(8,128)(2,1)S(1)}) custom-call(s32[3]{0:T(128)S(1)} %copy-done.24, f32[1024,1024]{1,0:T(8,128)S(1)} %copy-done.1, f32[128,1024]{1,0:T(8,128)S(1)} %collective-permute-done.15.refs_0_, ...), custom_call_target="tpu_custom_call" | custom-call | tf_op jit(solution)/shard_map/columns/pallas_call | solution.py:409
  378.2 1.3 copy-done.4
  379.5 1.4 copy-done.5
  380.9 1.3 copy-done.6
  382.2 1.3 copy-done.7
  383.5 46.5 %update.1 = f32[2048,1024]{1,0:T(8,128)} custom-call(s32[3]{0:T(128)} %copy-done.23, s32[16,8]{1,0:T(8,128)} %copy.15.pattern, s32[2,32]{1,0:T(2,128)} %pad_add_fusion.places, f32[1024,1024]{1,0:T(8,128)} %copy-done, bf16[1024,1024]{1,0:T(8,128)(2,1)} %copy-done.4, bf16[1024,1024]{1,0:T(8,128)(2,1)} %copy-done.5, bf16[1024,1024]{1,0:T(8,128)(2,1)} %copy-done.6, ...), custom_call_target="tpu_custom_call" | custom-call | tf_op jit(solution)/shard_map/update/pallas_call | solution.py:522
  (96 shorter events, 16.1 us)
Async XLA Ops:
  11.2 6.1 %copy-start.23 = (s32[3]{0:T(128)}, s32[3]{0:T(128)S(1)}, u32[]{:S(2)}) copy-start(s32[3]{0:T(128)S(1)} %pad_add_fusion.1.ids) | copy-start | bytes 40
  11.2 6.2 %copy-start.21 = (s32[8,32]{1,0:T(8,128)S(1)}, s32[8,32]{1,0:T(8,128)}, u32[]{:S(2)}) copy-start(s32[8,32]{1,0:T(8,128)} %cmap.9) | copy-start | bytes 3076
  17.4 2.2 copy-start.2
  19.6 7.0 %copy-start.31 = (f32[8,128,128]{2,1,0:T(8,128)S(1)}, f32[8,128,128]{2,1,0:T(8,128)}, u32[]{:S(2)}) copy-start(f32[8,128,128]{2,1,0:T(8,128)} %get-tuple-element.39) | copy-start | bytes 1572868
  19.6 8.3 %copy-start.30 = (f32[8,128,128]{2,1,0:T(8,128)S(1)}, f32[8,128,128]{2,1,0:T(8,128)}, u32[]{:S(2)}) copy-start(f32[8,128,128]{2,1,0:T(8,128)} %get-tuple-element.40) | copy-start | bytes 1572868
  21.1 30.6 %all-to-all-start = ((f32[8,2,128,128]{3,2,1,0:T(8,128)}), f32[8,2,128,128]{3,2,1,0:T(8,128)S(1)}, u32[]{:S(2)}, u32[]{:S(2)}) async-start(f32[8,2,128,128]{3,2,1,0:T(8,128)} %pack_small.1), calls=%async_computation | async-start | bytes 2097152 | tf_op jit(solution)/shard_map/all_to_all | solution.py:579
  25.9 9.5 %collective-permute-start.4 = (f32[8,128,128]{2,1,0:T(8,128)}, f32[8,128,128]{2,1,0:T(8,128)S(1)}, u32[]{:S(2)}, u32[]{:S(2)}) collective-permute-start(f32[8,128,128]{2,1,0:T(8,128)} %get-tuple-element.38), channel_id=1, source_target_pairs={{0,3},{1,10},{2,20},{16,29},{3,27},{4,33},{32,46},{5,44},{6,50},{4... | collective-permute-start | bytes 1572872 | tf_op jit(solution)/shard_map/ppermute | solution.py:580
  26.6 25.1 %collective-permute-start.5 = (f32[8,128,128]{2,1,0:T(8,128)S(1)}, f32[8,128,128]{2,1,0:T(8,128)S(1)}, u32[]{:S(2)}, u32[]{:S(2)}) collective-permute-start(f32[8,128,128]{2,1,0:T(8,128)S(1)} %copy-done.31), channel_id=1, source_target_pairs={{0,2},{1,9},{2,19},{16,23},{3,26},{4,36},{32,45},{5,43},{6,49},{48... | collective-permute-start | bytes 1572872 | tf_op jit(solution)/shard_map/ppermute | solution.py:580
  27.9 23.8 %collective-permute-start.6 = (f32[8,128,128]{2,1,0:T(8,128)S(1)}, f32[8,128,128]{2,1,0:T(8,128)}, u32[]{:S(2)}, u32[]{:S(2)}) collective-permute-start(f32[8,128,128]{2,1,0:T(8,128)S(1)} %copy-done.30), channel_id=1, source_target_pairs={{0,1},{1,8},{2,18},{16,22},{3,25},{4,35},{32,39},{5,42},{6,52},{48... | collective-permute-start | bytes 1572872 | tf_op jit(solution)/shard_map/ppermute | solution.py:580
  52.5 20.4 %copy-start.29 = (f32[8,128,128]{2,1,0:T(8,128)S(1)}, f32[8,128,128]{2,1,0:T(8,128)}, u32[]{:S(2)}) copy-start(f32[8,128,128]{2,1,0:T(8,128)} %get-tuple-element.37) | copy-start | bytes 1572868
  52.5 21.1 %copy-start.28 = (f32[8,128,128]{2,1,0:T(8,128)S(1)}, f32[8,128,128]{2,1,0:T(8,128)}, u32[]{:S(2)}) copy-start(f32[8,128,128]{2,1,0:T(8,128)} %get-tuple-element.45) | copy-start | bytes 1572868
  52.5 26.9 %copy-start.26 = (f32[8,128,128]{2,1,0:T(8,128)S(1)}, f32[8,128,128]{2,1,0:T(8,128)}, u32[]{:S(2)}) copy-start(f32[8,128,128]{2,1,0:T(8,128)} %get-tuple-element.32) | copy-start | bytes 1572868
  53.5 68.9 %all-to-all-start.1 = ((f32[128,64,128]{2,1,0:T(8,128)}), f32[128,64,128]{2,1,0:T(8,128)}, u32[]{:S(2)}, u32[]{:S(2)}) async-start(f32[128,64,128]{2,1,0:T(8,128)} %get-tuple-element.42), calls=%async_computation.1 | async-start | bytes 8388608 | tf_op jit(solution)/shard_map/all_to_all | solution.py:583
  70.7 139.2 %all-gather.6.cloned.1.call-start = ((), (), s32[]{:S(2)}) async-start(), calls=%async_computation.6 | async-start | bytes 3342336 | tf_op jit(solution)/shard_map/all_gather | solution.py:591
  70.8 8.6 %collective-permute-start = (f32[8,128,128]{2,1,0:T(8,128)}, f32[8,128,128]{2,1,0:T(8,128)S(1)}, u32[]{:S(2)}, u32[]{:S(2)}) collective-permute-start(f32[8,128,128]{2,1,0:T(8,128)} %get-tuple-element.34), channel_id=1, source_target_pairs={{0,7},{1,14}} | collective-permute-start | bytes 1572872 | tf_op jit(solution)/shard_map/ppermute | solution.py:580
  71.5 7.9 %collective-permute-start.1 = (f32[8,128,128]{2,1,0:T(8,128)}, f32[8,128,128]{2,1,0:T(8,128)S(1)}, u32[]{:S(2)}, u32[]{:S(2)}) collective-permute-start(f32[8,128,128]{2,1,0:T(8,128)} %get-tuple-element.35), channel_id=1, source_target_pairs={{0,6},{1,13},{16,21},{32,38},{48,55},{64,77},{80,94},{96,111},{112... | collective-permute-start | bytes 1572872 | tf_op jit(solution)/shard_map/ppermute | solution.py:580
  72.2 7.2 %collective-permute-start.2 = (f32[8,128,128]{2,1,0:T(8,128)}, f32[8,128,128]{2,1,0:T(8,128)S(1)}, u32[]{:S(2)}, u32[]{:S(2)}) collective-permute-start(f32[8,128,128]{2,1,0:T(8,128)} %get-tuple-element.36), channel_id=1, source_target_pairs={{0,5},{1,12},{16,31},{3,24},{32,37},{5,41},{48,54},{7,58},{64,71},... | collective-permute-start | bytes 1572872 | tf_op jit(solution)/shard_map/ppermute | solution.py:580
  72.9 6.5 %collective-permute-start.3 = (f32[8,128,128]{2,1,0:T(8,128)S(1)}, f32[8,128,128]{2,1,0:T(8,128)S(1)}, u32[]{:S(2)}, u32[]{:S(2)}) collective-permute-start(f32[8,128,128]{2,1,0:T(8,128)S(1)} %copy-done.29), channel_id=1, source_target_pairs={{0,4},{1,11},{2,17},{16,30},{3,28},{4,34},{32,47},{5,40},{6,51},{4... | collective-permute-start | bytes 1572872 | tf_op jit(solution)/shard_map/ppermute | solution.py:580
  73.6 5.8 %collective-permute-start.14 = (f32[8,128,128]{2,1,0:T(8,128)S(1)}, f32[8,128,128]{2,1,0:T(8,128)S(1)}, u32[]{:S(2)}, u32[]{:S(2)}) collective-permute-start(f32[8,128,128]{2,1,0:T(8,128)S(1)} %copy-done.28), channel_id=1, source_target_pairs={{1,15}} | collective-permute-start | bytes 1572872 | tf_op jit(solution)/shard_map/ppermute | solution.py:580
  79.4 130.5 %copy-start.22 = (s32[8,32]{1,0:T(8,128)S(1)}, s32[8,32]{1,0:T(8,128)}, u32[]{:S(2)}) copy-start(s32[8,32]{1,0:T(8,128)} %cmap.9) | copy-start | bytes 3076
  79.4 130.5 %copy-start.24 = (s32[3]{0:T(128)S(1)}, s32[3]{0:T(128)}, u32[]{:S(2)}) copy-start(s32[3]{0:T(128)} %copy-done.23) | copy-start | bytes 40
  209.9 1.9 copy-start.3
  214.9 32.5 %all-to-all-start.3 = ((f32[16,2,128,128]{3,2,1,0:T(8,128)}), f32[16,2,128,128]{3,2,1,0:T(8,128)S(1)}, u32[]{:S(2)}, u32[]{:S(2)}) async-start(f32[16,2,128,128]{3,2,1,0:T(8,128)} %get-tuple-element.47), calls=%async_computation.3 | async-start | bytes 4194304 | tf_op jit(solution)/shard_map/all_to_all | solution.py:594
  220.6 162.9 %all-gather.4.cloned.1.call-start = ((), (), s32[]{:S(2)}) async-start(), calls=%async_computation.5 | async-start | bytes 8912896 | tf_op jit(solution)/shard_map/all_gather | solution.py:596
  220.6 25.1 %collective-permute-start.12 = (f32[128,1024]{1,0:T(8,128)S(1)}, f32[128,1024]{1,0:T(8,128)S(1)}, u32[]{:S(2)}, u32[]{:S(2)}) collective-permute-start(f32[128,1024]{1,0:T(8,128)S(1)} %diag_rows.1.refs_0_), channel_id=1, source_target_pairs={{0,96},{16,112},{32,0},{48,16},{64,32},{80,48},{96,64},{112,80},{1... | collective-permute-start | bytes 1572872 | tf_op jit(solution)/shard_map/ppermute | solution.py:551
  221.4 24.3 %collective-permute-start.10 = (f32[128,1024]{1,0:T(8,128)S(1)}, f32[128,1024]{1,0:T(8,128)S(1)}, u32[]{:S(2)}, u32[]{:S(2)}) collective-permute-start(f32[128,1024]{1,0:T(8,128)S(1)} %diag_rows.1.refs_0_), channel_id=1, source_target_pairs={{0,64},{16,80},{32,96},{48,112},{64,0},{80,16},{96,32},{112,48},{1... | collective-permute-start | bytes 1572872 | tf_op jit(solution)/shard_map/ppermute | solution.py:551
  222.6 24.7 %collective-permute-start.8 = (f32[128,1024]{1,0:T(8,128)S(1)}, f32[128,1024]{1,0:T(8,128)}, u32[]{:S(2)}, u32[]{:S(2)}) collective-permute-start(f32[128,1024]{1,0:T(8,128)S(1)} %diag_rows.1.refs_0_), channel_id=1, source_target_pairs={{0,32},{16,48},{32,64},{48,80},{64,96},{80,112},{96,0},{112,16},{1... | collective-permute-start | bytes 1572872 | tf_op jit(solution)/shard_map/ppermute | solution.py:551
  251.2 5.6 %collective-permute-start.7 = (f32[128,1024]{1,0:T(8,128)S(1)}, f32[128,1024]{1,0:T(8,128)S(1)}, u32[]{:S(2)}, u32[]{:S(2)}) collective-permute-start(f32[128,1024]{1,0:T(8,128)S(1)} %diag_rows.1.refs_0_), channel_id=1, source_target_pairs={{0,16},{16,0},{32,48},{48,32},{64,80},{80,64},{96,112},{112,96},{1... | collective-permute-start | bytes 1572872 | tf_op jit(solution)/shard_map/ppermute | solution.py:558
  251.3 6.4 %collective-permute-start.13 = (f32[128,1024]{1,0:T(8,128)}, f32[128,1024]{1,0:T(8,128)S(1)}, u32[]{:S(2)}, u32[]{:S(2)}) collective-permute-start(f32[128,1024]{1,0:T(8,128)} %copy-done.9), channel_id=1, source_target_pairs={{0,16},{16,0},{32,48},{48,32},{64,80},{80,64},{96,112},{112,96},{1... | collective-permute-start | bytes 1572872 | tf_op jit(solution)/shard_map/ppermute | solution.py:558
  251.8 6.7 %collective-permute-start.11 = (f32[128,1024]{1,0:T(8,128)}, f32[128,1024]{1,0:T(8,128)S(1)}, u32[]{:S(2)}, u32[]{:S(2)}) collective-permute-start(f32[128,1024]{1,0:T(8,128)} %copy-done.11), channel_id=1, source_target_pairs={{0,16},{16,0},{32,48},{48,32},{64,80},{80,64},{96,112},{112,96},{1... | collective-permute-start | bytes 1572872 | tf_op jit(solution)/shard_map/ppermute | solution.py:558
  251.9 7.4 %collective-permute-start.9 = (f32[128,1024]{1,0:T(8,128)}, f32[128,1024]{1,0:T(8,128)S(1)}, u32[]{:S(2)}, u32[]{:S(2)}) collective-permute-start(f32[128,1024]{1,0:T(8,128)} %collective-permute-done.8.refs_2_), channel_id=1, source_target_pairs={{0,16},{16,0},{32,48},{48,32},{64,80},{80,64},{96,112},{112,96},{1... | collective-permute-start | bytes 1572872 | tf_op jit(solution)/shard_map/ppermute | solution.py:558
  252.3 26.4 %collective-permute-start.15 = (f32[128,1024]{1,0:T(8,128)}, f32[128,1024]{1,0:T(8,128)S(1)}, u32[]{:S(2)}, u32[]{:S(2)}) collective-permute-start(f32[128,1024]{1,0:T(8,128)} %copy-done.8), channel_id=1, source_target_pairs={{0,0},{1,16},{2,32},{3,48},{4,64},{5,80},{6,96},{7,112},{8,1},{9,1... | collective-permute-start | bytes 1572872 | tf_op jit(solution)/shard_map/ppermute | solution.py:598
  278.8 21.6 %copy-start.10 = (f32[128,1024]{1,0:T(8,128)S(1)}, f32[128,1024]{1,0:T(8,128)}, u32[]{:S(2)}) copy-start(f32[128,1024]{1,0:T(8,128)} %copy-done.9) | copy-start | bytes 1572868
  278.8 21.6 %copy-start.12 = (f32[128,1024]{1,0:T(8,128)S(1)}, f32[128,1024]{1,0:T(8,128)}, u32[]{:S(2)}) copy-start(f32[128,1024]{1,0:T(8,128)} %copy-done.11) | copy-start | bytes 1572868
  278.8 104.8 %all-to-all-start.4 = ((f32[128,64,128]{2,1,0:T(8,128)}), f32[128,64,128]{2,1,0:T(8,128)}, u32[]{:S(2)}, u32[]{:S(2)}) async-start(f32[128,64,128]{2,1,0:T(8,128)} %get-tuple-element.58), calls=%async_computation.4 | async-start | bytes 8388608 | tf_op jit(solution)/shard_map/all_to_all | solution.py:599
  296.2 66.8 %collective-permute-start.18 = (f32[128,1024]{1,0:T(8,128)S(1)}, f32[128,1024]{1,0:T(8,128)S(1)}, u32[]{:S(2)}, u32[]{:S(2)}) collective-permute-start(f32[128,1024]{1,0:T(8,128)S(1)} %collective-permute-done.15.refs_0_), channel_id=1, source_target_pairs={{0,96},{16,112},{32,0},{48,16},{64,32},{80,48},{96,64},{112,80},{1... | collective-permute-start | bytes 1572872 | tf_op jit(solution)/shard_map/ppermute | solution.py:551
  297.1 67.8 %collective-permute-start.17 = (f32[128,1024]{1,0:T(8,128)S(1)}, f32[128,1024]{1,0:T(8,128)S(1)}, u32[]{:S(2)}, u32[]{:S(2)}) collective-permute-start(f32[128,1024]{1,0:T(8,128)S(1)} %collective-permute-done.15.refs_0_), channel_id=1, source_target_pairs={{0,64},{16,80},{32,96},{48,112},{64,0},{80,16},{96,32},{112,48},{1... | collective-permute-start | bytes 1572872 | tf_op jit(solution)/shard_map/ppermute | solution.py:551
  298.3 66.7 %collective-permute-start.16 = (f32[128,1024]{1,0:T(8,128)S(1)}, f32[128,1024]{1,0:T(8,128)}, u32[]{:S(2)}, u32[]{:S(2)}) collective-permute-start(f32[128,1024]{1,0:T(8,128)S(1)} %collective-permute-done.15.refs_0_), channel_id=1, source_target_pairs={{0,32},{16,48},{32,64},{48,80},{64,96},{80,112},{96,0},{112,16},{1... | collective-permute-start | bytes 1572872 | tf_op jit(solution)/shard_map/ppermute | solution.py:551
  361.0 2.0 copy-start
  364.9 2.6 collective-permute-start.19
  364.9 3.2 collective-permute-start.20
  365.5 3.6 collective-permute-start.21
  365.5 3.8 collective-permute-start.22
  369.2 2.2 copy-start.1
  378.2 1.3 copy-start.4
  379.5 1.4 copy-start.5
  380.9 1.3 copy-start.6
  382.2 1.3 copy-start.7
  (13 other events, 11.9 us)
Sparse Core Ops, SparseCore 0:
  159.1 50.8 all-gather.5
  251.4 127.2 all-gather.3

commit v6 on v4

--- a/solution.py
+++ b/solution.py
@@ -366,34 +366,44 @@
         out[:, rows] = dot3(xh[:, :upto], xl[:, :upto], eh[rows, :upto], el[rows, :upto])
 
 
-def update_kernel(ids, pattern, w_ref, *refs):
-    pieces, (xr_ref, own_ref, out_ref, eh, el, ch, cl, x) = refs[:ROWS], refs[ROWS:]
+def columns_kernel(ids, w_ref, *refs):
+    pieces, (eh, el, ch, cl, x) = refs[:ROWS], refs[ROWS:]
+    row = lax.broadcasted_iota(jnp.int32, (B, W), 0)
+    col = lax.broadcasted_iota(jnp.int32, (B, W), 1)
+
+    def split(i, _):
+        rows = block(i)
+        high, low = halves(jnp.where(row + i * B >= col, w_ref[rows, :], 0.0))
+        eh[rows, :] = high
+        el[rows, :] = low
+        return 0
+
+    lax.fori_loop(0, NB, split, 0)
+    at_row = piece_rows(ids[0])
+    for n in range(0, ROWS, 2):
+        pair = jnp.concatenate([pieces[n][...], pieces[n + 1][...]], axis=0)
+        solve_rows(pair, x, eh, el)
+        for m in range(2):
+            high, low = halves(x[m * B : (m + 1) * B, :])
+            ch[block(at_row[n + m]), :] = high
+            cl[block(at_row[n + m]), :] = low
+
+
+def columns(ids, w, pieces):
+    return pl.pallas_call(
+        columns_kernel,
+        out_shape=(jax.ShapeDtypeStruct((W, W), BF16),) * 4,
+        in_specs=[SMEM, VMEM] + [VMEM] * ROWS,
+        out_specs=(VMEM,) * 4,
+        scratch_shapes=[pltpu.VMEM((CHUNK, W), F32)],
+        compiler_params=params(32),
+        name="columns",
+    )(ids, w, *pieces)
+
+
+def update_kernel(ids, pattern, w_ref, eh, el, ch, cl, xr_ref, own_ref, out_ref, x):
     step = pl.program_id(0)
     r, c = ids[0], ids[1]
-
-    @pl.when(step == 0)
-    def _():
-        row = lax.broadcasted_iota(jnp.int32, (B, W), 0)
-        col = lax.broadcasted_iota(jnp.int32, (B, W), 1)
-
-        def split(i, _):
-            rows = block(i)
-            high, low = halves(jnp.where(row + i * B >= col, w_ref[rows, :], 0.0))
-            eh[rows, :] = high
-            el[rows, :] = low
-            return 0
-
-        lax.fori_loop(0, NB, split, 0)
-
-        at_row = piece_rows(r)
-        for n in range(0, ROWS, 2):
-            pair = jnp.concatenate([pieces[n][...], pieces[n + 1][...]], axis=0)
-            solve_rows(pair, x, eh, el)
-            for m in range(2):
-                high, low = halves(x[m * B : (m + 1) * B, :])
-                ch[block(at_row[n + m]), :] = high
-                cl[block(at_row[n + m]), :] = low
-
     solve_rows(xr_ref[...], x, eh, el)
     top = (r == 0) & (step < W // CHUNK)
 
@@ -432,68 +442,54 @@
             out_ref[:, cols] = jnp.where(gap > 0, above, jnp.where(gap == 0, 1.0 / here, 0.0))
 
 
-def update(ids, pattern, w, xc, xr, own):
+def update(ids, pattern, w, solved, xr, own):
     rows = own.shape[0]
     whole = pl.BlockSpec((W, W), lambda i: (0, 0), pipeline_mode=pl.Buffered(1))
-    piece = pl.BlockSpec((B, W), lambda i: (0, 0), pipeline_mode=pl.Buffered(1))
     part = pl.BlockSpec((CHUNK, W), lambda i: (i, 0))
     return pl.pallas_call(
         update_kernel,
         grid=(rows // CHUNK,),
         out_shape=jax.ShapeDtypeStruct(own.shape, F32),
-        in_specs=[SMEM, SMEM, whole] + [piece] * ROWS + [part, part],
+        in_specs=[SMEM, SMEM] + [whole] * 5 + [part, part],
         out_specs=part,
-        scratch_shapes=[pltpu.VMEM((W, W), BF16)] * 4 + [pltpu.VMEM((CHUNK, W), F32)],
+        scratch_shapes=[pltpu.VMEM((CHUNK, W), F32)],
         compiler_params=params(60),
         name="update",
-    )(ids, pattern, w, *xc, xr, own)
-
-
-def add_kernel(places, base, came, out, held, sems):
+    )(ids, pattern, w, *solved, xr, own)
+
+
+def add_kernel(places, base, came, out, held, sem):
     step = pl.program_id(0)
-
-    def visit(group, act):
-        def one(quarter, _):
-            child = group // 4
-            slot = (child // 4 * 4 + group % 4) * COLS + child % 4 * 4 + quarter
-            col = places[1, child * 4 + quarter]
-
-            @pl.when(col >= 0)
-            def _():
-                act(pltpu.make_async_copy(came.at[slot], held.at[slot], sems.at[slot]), slot, col)
-
-            return 0
-
-        lax.fori_loop(0, 4, one, 0)
+    load = pltpu.make_async_copy(came, held, sem)
 
     @pl.when(step == 0)
     def _():
-        def begin(group, _):
-            @pl.when(places[0, group] >= 0)
-            def _():
-                visit(group, lambda m, slot, col: m.start())
-
-            return 0
-
-        lax.fori_loop(0, 32, begin, 0)
+        load.start()
 
     out[...] = base[...]
 
-    def finish(group, _):
+    @pl.when(step == 0)
+    def _():
+        load.wait()
+
+    def group_blocks(group, _):
         row = places[0, group]
-
-        def act(m, slot, col):
-            m.wait()
-            here = block(row % (CHUNK // B)), block(col)
-            out[here] = out[here] + held[slot]
 
         @pl.when((row >= 0) & (row // (CHUNK // B) == step))
         def _():
-            visit(group, act)
+            child = group // 4
+            for quarter in range(4):
+                slot = (child // 4 * 4 + group % 4) * COLS + child % 4 * 4 + quarter
+                col = places[1, child * 4 + quarter]
+
+                @pl.when(col >= 0)
+                def _():
+                    here = block(row % (CHUNK // B)), block(col)
+                    out[here] = out[here] + held[slot]
 
         return 0
 
-    lax.fori_loop(0, 32, finish, 0)
+    lax.fori_loop(0, 32, group_blocks, 0)
 
 
 def add(places, base, came):
@@ -504,10 +500,7 @@
         out_shape=jax.ShapeDtypeStruct(base.shape, F32),
         in_specs=[SMEM, part, HBM],
         out_specs=part,
-        scratch_shapes=[
-            pltpu.VMEM((ROWS * COLS, B, B), F32),
-            pltpu.SemaphoreType.DMA((ROWS * COLS,)),
-        ],
+        scratch_shapes=[pltpu.VMEM((ROWS * COLS, B, B), F32), pltpu.SemaphoreType.DMA(())],
         compiler_params=params(60),
         name="add",
     )(places, base, came)
@@ -571,12 +564,13 @@
     xr = lax.all_gather(owned, "pcol", axis=0, tiled=True)
     to = [(at(r, c), at(c % 8, 2 * r + c // 8)) for r in range(ROWS) for c in range(COLS)]
     xc = lax.ppermute(owned, AXES, to)
-    bulk = after(pack(ids, cmap, child), (xc, pivot))
-    bulk = lax.all_to_all(bulk, AXES, 0, 0, tiled=True)
+    bulk = after(pack(ids, cmap, child), pivot)
     xc = along_x(xc)
-    w = factor(ids, pivot)
-    xc = across(after(xc, w))
-    base = update(ids, pattern, w, xc, xr, own)
+    w = factor(ids, after(pivot, xc[0]))
+    xc, _ = lax.optimization_barrier((xc, w))
+    bulk = lax.all_to_all(after(bulk, (w, xc)), AXES, 0, 0, tiled=True)
+    solved = columns(ids, w, across(xc))
+    base = update(ids, pattern, w, solved, xr, own)
     return add(places, base, bulk)
 
 

time: 421 us -> 427 us (1.014); the launches traced: 414 us -> 425 us
  local copies, waits for them, and re-layouts: 16 us -> 24.5 us
    all_to_all x1, waiting for transfers between devices: 0.01 us -> 59 us  [body(): bulk = lax.all_to_all(after(bulk, (w, xc)), AXES, 0, 0, tiled=True)]
    ppermute x6, waiting for transfers between devices: 77 us -> 20.9 us  [along_x(): pieces.append(lax.ppermute(piece, 'prow', to))]
    unnamed x47 -> x59, local copies, waits for them, and re-layouts: 13.2 us -> 21.8 us
    pallas_call x0 -> x1, Pallas kernels: none -> 6.73 us  [columns(): pl.pallas_call(columns_kernel, out_shape=(jax.ShapeDtypeStruct((W, W), BF...]
    ppermute x6, starting transfers between devices: 8.06 us -> 14.2 us  [along_x(): pieces.append(lax.ppermute(piece, 'prow', to))]
    all_to_all x1, starting transfers between devices: 16 us -> 10 us  [body(): bulk = lax.all_to_all(after(bulk, (w, xc)), AXES, 0, 0, tiled=True)]
    all_gather x1, waiting for transfers between devices: 4.54 us -> 0.01 us  [body(): xr = lax.all_gather(owned, 'pcol', axis=0, tiled=True)]
    pallas_call x1, Pallas kernels: 35.6 us -> 31.2 us  [update(): pl.pallas_call(update_kernel, grid=(rows // CHUNK,), out_shape=jax.ShapeD...]
  transfers between devices with their start and end apart: 28 -> 28, of which waited for: 11 -> 9; matrix products, arithmetic and copies ran while one was open for 1% -> 1% of each run, Pallas kernels for 24% -> 24%
where the time goes in v6:
time: 427 us; the launch traced here: 425 us
  waiting for transfers between devices  178 us (42%)
  Pallas kernels  132 us (31%)
  starting transfers between devices  48.6 us (11%)
  local copies, waits for them, and re-layouts  24.5 us (6%)
  blocking collectives  20.8 us (5%)
  between operations  19.4 us (5%)
    all_to_all x1, waiting for transfers between devices, body(): bulk = lax.all_to_all(after(bulk, (w, xc)), AXES, 0, 0, tiled=True)  59 us
    pallas_call x1, Pallas kernels, factor(): pl.pallas_call(factor_kernel, out_shape=jax.ShapeDtypeStruct((W, W), F32)...  56.6 us
    all_gather x1, waiting for transfers between devices, body(): diag = lax.all_gather(diag, 'pcol', axis=0)  52 us
    pallas_call x1, Pallas kernels, update(): pl.pallas_call(update_kernel, grid=(rows // CHUNK,), out_shape=jax.ShapeD...  31.2 us
    ppermute x8, waiting for transfers between devices, body(): piece = lax.ppermute(piece, AXES, moves[step])  22.4 us
    unnamed x59, local copies, waits for them, and re-layouts  21.8 us
    ppermute x1, waiting for transfers between devices, body(): xc = lax.ppermute(owned, AXES, to)  21.2 us
    ppermute x6, waiting for transfers between devices, along_x(): pieces.append(lax.ppermute(piece, 'prow', to))  20.9 us
  transfers between devices with their start and end apart: 28, of which 9 were waited for; matrix products, arithmetic and copies ran while one was open for 1% of the time, Pallas kernels for 24%

profile of v6, /device:TPU:14, one launch (start us, length us, event | category | flops | bytes accessed | tf_op | source)
XLA Modules:
  0.0 424.8 jit_solution(3182718428100016367)
XLA Ops:
  7.9 1.4 copy.15.pattern
  9.2 6.2 %pack_parent.1 = (f32[8,128,128]{2,1,0:T(8,128)}, f32[8,128,128]{2,1,0:T(8,128)}, f32[8,128,128]{2,1,0:T(8,128)}, f32[8,128,128]{2,1,0:T(8,128)}, f32[8,128,128]...) custom-call(s32[8,2]{1,0:T(8,128)} %copy.13.sends, ...), custom_call_target="tpu_custom_call" | custom-call | tf_op jit(solution)/shard_map/pack_parent/pallas_call | solution.py:82
  17.5 0.7 constant_dynamic-slice_fusion
  18.8 0.7 pad_add_fusion.1.ids
  19.5 2.2 copy-done.2
  21.7 1.5 pack_small.1
  23.2 4.8 %all-to-all-start = ((f32[8,2,128,128]{3,2,1,0:T(8,128)}), f32[8,2,128,128]{3,2,1,0:T(8,128)S(1)}, u32[]{:S(2)}, u32[]{:S(2)}) async-start(f32[8,2,128,128]{3,2,1,0:T(8,128)} %pack_small.1), calls=%async_computation | async-start | bytes 2097152 | tf_op jit(solution)/shard_map/all_to_all | solution.py:550
  29.4 1.3 collective-permute-start.5
  30.8 0.7 collective-permute-start.6
  37.7 22.4 %collective-permute-done.5 = f32[8,128,128]{2,1,0:T(8,128)S(1)} collective-permute-done((f32[8,128,128]{2,1,0:T(8,128)}, f32[8,128,128]{2,1,0:T(8,128)S(1)}, u32[]{:S(2)}, u32[]{:S(2)}) %collective-permute-start.5) | collective-permute-done | bytes 524320 | tf_op jit(solution)/shard_map/ppermute | solution.py:553
  60.7 20.8 %all_to_all.20.parent = f32[8,128,128]{2,1,0:T(8,128)} all-to-all(f32[8,128,128]{2,1,0:T(8,128)S(1)} %get-tuple-element.70), channel_id=1, replica_groups=mesh['prow'=8,'pcol'=16] {'prow'}, dimensions={0} | all-to-all | bytes 1048576 | tf_op jit(solution)/shard_map/all_to_all | solution.py:556
  81.5 2.5 relay.1
  84.0 52.0 %all-gather.6.cloned.1.call-done = f32[48,128,128]{2,1,0:T(8,128)} async-done(((f32[3,128,128]{2,1,0:T(8,128)}), f32[48,128,128]{2,1,0:T(8,128)}) %all-gather.6.cloned.1.call-update) | async-done | bytes 3145744 | tf_op jit(solution)/shard_map/all_gather | solution.py:559
  136.1 1.9 copy-done.3
  138.6 3.1 diag_rows.1.refs_0_
  141.7 5.7 %all-to-all-start.2 = ((f32[16,2,128,128]{3,2,1,0:T(8,128)}), f32[16,2,128,128]{3,2,1,0:T(8,128)S(1)}, u32[]{:S(2)}, u32[]{:S(2)}) async-start(f32[16,2,128,128]{3,2,1,0:T(8,128)} %get-tuple-element.47), calls=%async_computation.2 | async-start | bytes 4194304 | tf_op jit(solution)/shard_map/all_to_all | solution.py:562
  147.5 0.9 collective-permute-start.12
  148.3 1.1 collective-permute-start.10
  149.4 2.1 collective-permute-start.8
  151.5 20.9 %collective-permute-done.12.refs_6_ = f32[128,1024]{1,0:T(8,128)S(1)} collective-permute-done((f32[128,1024]{1,0:T(8,128)S(1)}, f32[128,1024]{1,0:T(8,128)S(1)}, u32[]{:S(2)}, u32[]{:S(2)}) %collective-permute-start.12) | collective-permute-done | bytes 524320 | tf_op jit(solution)/shard_map/ppermute | solution.py:522
  172.5 0.8 copy-done.9
  173.2 0.8 copy-done.11
  174.1 3.1 owner_rows.1
  177.2 0.8 copy-done.8
  178.0 4.9 %collective-permute-start.15 = (f32[128,1024]{1,0:T(8,128)}, f32[128,1024]{1,0:T(8,128)S(1)}, u32[]{:S(2)}, u32[]{:S(2)}) collective-permute-start(f32[128,1024]{1,0:T(8,128)} %copy-done.8), channel_id=1, source_target_pairs={{0,0},{1,16},{2,32},{3,48},{4,64},{5,80},{6,96},{7,112},{8,1},{9,1... | collective-permute-start | bytes 1572872 | tf_op jit(solution)/shard_map/ppermute | solution.py:566
  182.9 1.1 collective-permute-start.7
  184.6 21.2 %collective-permute-done.15.refs_0_ = f32[128,1024]{1,0:T(8,128)S(1)} collective-permute-done((f32[128,1024]{1,0:T(8,128)}, f32[128,1024]{1,0:T(8,128)S(1)}, u32[]{:S(2)}, u32[]{:S(2)}) %collective-permute-start.15) | collective-permute-done | bytes 524320 | tf_op jit(solution)/shard_map/ppermute | solution.py:566
  205.8 0.8 copy-done.13
  206.6 7.5 %collective-permute-start.17 = (f32[128,1024]{1,0:T(8,128)S(1)}, f32[128,1024]{1,0:T(8,128)S(1)}, u32[]{:S(2)}, u32[]{:S(2)}) collective-permute-start(f32[128,1024]{1,0:T(8,128)S(1)} %collective-permute-done.15.refs_0_), channel_id=1, source_target_pairs={{0,64},{16,80},{32,96},{48,112},{64,0},{80,16},{96,32},{112,48},{1... | collective-permute-start | bytes 1572872 | tf_op jit(solution)/shard_map/ppermute | solution.py:522
  214.2 0.8 copy-done.15
  215.0 2.6 collective-permute-start.16
  217.6 5.3 %pack.1 = f32[128,128,128]{2,1,0:T(8,128)} custom-call(s32[3]{0:T(128)} %copy-done.20, s32[8,32]{1,0:T(8,128)} %cmap.9, f32[1024,1024]{1,0:T(8,128)} %child.3), custom_call_target="tpu_custom_call" | custom-call | tf_op jit(solution)/shard_map/pack/pallas_call | solution.py:136
  223.0 1.0 copy-done.14
  224.0 1.0 copy-done.16
  225.0 56.6 %factor.1.w_ref = f32[1024,1024]{1,0:T(8,128)S(1)} custom-call(s32[3]{0:T(128)S(1)} %copy-done.23, f32[128,1024]{1,0:T(8,128)S(1)} %diag_rows.1.refs_0_, f32[128,1024]{1,0:T(8,128)S(1)} %copy-done.14, f32[128,1024]{1,0:T(8,128)} %collective-permute-done.8.refs_2_, f32[128,1024]{1,0:T(8,128)} %collective-permute-done.9.refs_3_, f32[128,1024]{1,0:T(8,128)S(1)} %copy-done.12, ...), custom_call_target="tpu_custom_call" | custom-call | tf_op jit(solution)/shard_map/factor/pallas_call | solution.py:333
  281.6 2.1 copy-done
  283.7 10.0 %all-to-all-start.3 = ((f32[128,128,128]{2,1,0:T(8,128)}), f32[128,128,128]{2,1,0:T(8,128)}, u32[]{:S(2)}, u32[]{:S(2)}) async-start(f32[128,128,128]{2,1,0:T(8,128)} %pack.1), calls=%async_computation.3 | async-start | bytes 16777216 | tf_op jit(solution)/shard_map/all_to_all | solution.py:571
  295.7 1.5 collective-permute-done.20.refs_3_
  297.4 0.8 collective-permute-done.22.refs_7_
  298.1 2.2 copy-done.1
  300.3 6.7 %columns.1 = (bf16[1024,1024]{1,0:T(8,128)(2,1)S(1)}, bf16[1024,1024]{1,0:T(8,128)(2,1)S(1)}, bf16[1024,1024]{1,0:T(8,128)(2,1)S(1)}, bf16[1024,1024]{1,0:T(8,128)(2,1)S(1)}) custom-call(s32[3]{0:T(128)S(1)} %copy-done.23, f32[1024,1024]{1,0:T(8,128)S(1)} %copy-done.1, f32[128,1024]{1,0:T(8,128)S(1)} %collective-permute-done.15.refs_0_, ...), custom_call_target="tpu_custom_call" | custom-call | tf_op jit(solution)/shard_map/columns/pallas_call | solution.py:393
  307.1 1.3 copy-done.4
  308.3 1.3 copy-done.5
  309.7 1.3 copy-done.6
  311.0 1.4 copy-done.7
  312.3 31.2 %update.1.base = f32[2048,1024]{1,0:T(8,128)} custom-call(s32[3]{0:T(128)} %copy-done.20, s32[16,8]{1,0:T(8,128)} %copy.15.pattern, f32[1024,1024]{1,0:T(8,128)} %copy-done, bf16[1024,1024]{1,0:T(8,128)(2,1)} %copy-done.4, bf16[1024,1024]{1,0:T(8,128)(2,1)} %copy-done.5, bf16[1024,1024]{1,0:T(8,128)(2,1)} %copy-done.6, bf16[1024,1024]{1,0:T(8,128)(2,1)} %copy-done.7, ...), custom_call_target="tpu_custom_call" | custom-call | tf_op jit(solution)/shard_map/update/pallas_call | solution.py:449
  343.6 59.0 %all-to-all-done.3.came = f32[128,128,128]{2,1,0:T(8,128)} async-done(((f32[128,128,128]{2,1,0:T(8,128)}), f32[128,128,128]{2,1,0:T(8,128)}, u32[]{:S(2)}, u32[]{:S(2)}) %all-to-all-start.3) | async-done | bytes 8388640 | tf_op jit(solution)/shard_map/all_to_all | solution.py:571
  402.6 15.3 %add.41 = f32[2048,1024]{1,0:T(8,128)} custom-call(s32[2,32]{1,0:T(2,128)} %pad_add_fusion.places, f32[2048,1024]{1,0:T(8,128)} %update.1.base, f32[128,128,128]{2,1,0:T(8,128)} %all-to-all-done.3.came), custom_call_target="tpu_custom_call" | custom-call | tf_op jit(solution)/shard_map/add/pallas_call | solution.py:497
  (89 shorter events, 10.1 us)
Async XLA Ops:
  9.2 10.3 %copy-start.17 = (s32[8,32]{1,0:T(8,128)S(1)}, s32[8,32]{1,0:T(8,128)}, u32[]{:S(2)}) copy-start(s32[8,32]{1,0:T(8,128)} %cmap.9) | copy-start | bytes 3076
  15.4 14.0 %collective-permute-start = (f32[8,128,128]{2,1,0:T(8,128)}, f32[8,128,128]{2,1,0:T(8,128)S(1)}, u32[]{:S(2)}, u32[]{:S(2)}) collective-permute-start(f32[8,128,128]{2,1,0:T(8,128)} %get-tuple-element.36), channel_id=1, source_target_pairs={{0,7},{1,14}} | collective-permute-start | bytes 1572872 | tf_op jit(solution)/shard_map/ppermute | solution.py:553
  16.1 14.7 %collective-permute-start.1 = (f32[8,128,128]{2,1,0:T(8,128)}, f32[8,128,128]{2,1,0:T(8,128)S(1)}, u32[]{:S(2)}, u32[]{:S(2)}) collective-permute-start(f32[8,128,128]{2,1,0:T(8,128)} %get-tuple-element.37), channel_id=1, source_target_pairs={{0,6},{1,13},{16,21},{32,38},{48,55},{64,77},{80,94},{96,111},{112... | collective-permute-start | bytes 1572872 | tf_op jit(solution)/shard_map/ppermute | solution.py:553
  16.8 14.7 %collective-permute-start.2 = (f32[8,128,128]{2,1,0:T(8,128)}, f32[8,128,128]{2,1,0:T(8,128)S(1)}, u32[]{:S(2)}, u32[]{:S(2)}) collective-permute-start(f32[8,128,128]{2,1,0:T(8,128)} %get-tuple-element.38), channel_id=1, source_target_pairs={{0,5},{1,12},{16,31},{3,24},{32,37},{5,41},{48,54},{7,58},{64,71},... | collective-permute-start | bytes 1572872 | tf_op jit(solution)/shard_map/ppermute | solution.py:553
  19.5 2.2 copy-start.2
  21.7 38.9 %copy-start.20 = (s32[3]{0:T(128)}, s32[3]{0:T(128)S(1)}, u32[]{:S(2)}) copy-start(s32[3]{0:T(128)S(1)} %pad_add_fusion.1.ids) | copy-start | bytes 40
  21.7 38.5 %copy-start.25 = (f32[8,128,128]{2,1,0:T(8,128)S(1)}, f32[8,128,128]{2,1,0:T(8,128)}, u32[]{:S(2)}) copy-start(f32[8,128,128]{2,1,0:T(8,128)} %get-tuple-element.43) | copy-start | bytes 1572868
  23.2 37.4 %all-to-all-start = ((f32[8,2,128,128]{3,2,1,0:T(8,128)}), f32[8,2,128,128]{3,2,1,0:T(8,128)S(1)}, u32[]{:S(2)}, u32[]{:S(2)}) async-start(f32[8,2,128,128]{3,2,1,0:T(8,128)} %pack_small.1), calls=%async_computation | async-start | bytes 2097152 | tf_op jit(solution)/shard_map/all_to_all | solution.py:550
  28.0 108.0 %all-gather.6.cloned.1.call-start = ((), (), s32[]{:S(2)}) async-start(), calls=%async_computation.5 | async-start | bytes 3342336 | tf_op jit(solution)/shard_map/all_gather | solution.py:559
  28.0 9.7 %collective-permute-start.3 = (f32[8,128,128]{2,1,0:T(8,128)}, f32[8,128,128]{2,1,0:T(8,128)S(1)}, u32[]{:S(2)}, u32[]{:S(2)}) collective-permute-start(f32[8,128,128]{2,1,0:T(8,128)} %get-tuple-element.39), channel_id=1, source_target_pairs={{0,4},{1,11},{2,17},{16,30},{3,28},{4,34},{32,47},{5,40},{6,51},{4... | collective-permute-start | bytes 1572872 | tf_op jit(solution)/shard_map/ppermute | solution.py:553
  28.7 9.0 %collective-permute-start.4 = (f32[8,128,128]{2,1,0:T(8,128)}, f32[8,128,128]{2,1,0:T(8,128)S(1)}, u32[]{:S(2)}, u32[]{:S(2)}) collective-permute-start(f32[8,128,128]{2,1,0:T(8,128)} %get-tuple-element.40), channel_id=1, source_target_pairs={{0,3},{1,10},{2,20},{16,29},{3,27},{4,33},{32,46},{5,44},{6,50},{4... | collective-permute-start | bytes 1572872 | tf_op jit(solution)/shard_map/ppermute | solution.py:553
  29.4 30.7 %copy-start.26 = (f32[8,128,128]{2,1,0:T(8,128)}, f32[8,128,128]{2,1,0:T(8,128)S(1)}, u32[]{:S(2)}) copy-start(f32[8,128,128]{2,1,0:T(8,128)S(1)} %collective-permute-done) | copy-start | bytes 1572868
  29.4 30.7 %collective-permute-start.5 = (f32[8,128,128]{2,1,0:T(8,128)}, f32[8,128,128]{2,1,0:T(8,128)S(1)}, u32[]{:S(2)}, u32[]{:S(2)}) collective-permute-start(f32[8,128,128]{2,1,0:T(8,128)} %get-tuple-element.41), channel_id=1, source_target_pairs={{0,2},{1,9},{2,19},{16,23},{3,26},{4,36},{32,45},{5,43},{6,49},{48... | collective-permute-start | bytes 1572872 | tf_op jit(solution)/shard_map/ppermute | solution.py:553
  30.8 29.4 %copy-start.27 = (f32[8,128,128]{2,1,0:T(8,128)}, f32[8,128,128]{2,1,0:T(8,128)S(1)}, u32[]{:S(2)}) copy-start(f32[8,128,128]{2,1,0:T(8,128)S(1)} %collective-permute-done.1) | copy-start | bytes 1572868
  30.8 29.4 %collective-permute-start.6 = (f32[8,128,128]{2,1,0:T(8,128)}, f32[8,128,128]{2,1,0:T(8,128)S(1)}, u32[]{:S(2)}, u32[]{:S(2)}) collective-permute-start(f32[8,128,128]{2,1,0:T(8,128)} %get-tuple-element.42), channel_id=1, source_target_pairs={{0,1},{1,8},{2,18},{16,22},{3,25},{4,35},{32,39},{5,42},{6,52},{48... | collective-permute-start | bytes 1572872 | tf_op jit(solution)/shard_map/ppermute | solution.py:553
  31.5 28.7 %copy-start.28 = (f32[8,128,128]{2,1,0:T(8,128)}, f32[8,128,128]{2,1,0:T(8,128)S(1)}, u32[]{:S(2)}) copy-start(f32[8,128,128]{2,1,0:T(8,128)S(1)} %collective-permute-done.2) | copy-start | bytes 1572868
  31.5 28.7 %collective-permute-start.14 = (f32[8,128,128]{2,1,0:T(8,128)}, f32[8,128,128]{2,1,0:T(8,128)S(1)}, u32[]{:S(2)}, u32[]{:S(2)}) collective-permute-start(f32[8,128,128]{2,1,0:T(8,128)} %get-tuple-element.45), channel_id=1, source_target_pairs={{1,15}} | collective-permute-start | bytes 1572872 | tf_op jit(solution)/shard_map/ppermute | solution.py:553
  60.2 75.9 %copy-start.18 = (s32[8,32]{1,0:T(8,128)S(1)}, s32[8,32]{1,0:T(8,128)}, u32[]{:S(2)}) copy-start(s32[8,32]{1,0:T(8,128)} %cmap.9) | copy-start | bytes 3076
  60.6 20.8 %copy-start.24 = (f32[8,2,128,128]{3,2,1,0:T(8,128)}, f32[8,2,128,128]{3,2,1,0:T(8,128)S(1)}, u32[]{:S(2)}) copy-start(f32[8,2,128,128]{3,2,1,0:T(8,128)S(1)} %all-to-all-done.came) | copy-start | bytes 3145732
  84.0 90.0 %copy-start.22 = (s32[3]{0:T(128)S(1)}, s32[3]{0:T(128)}, u32[]{:S(2)}) copy-start(s32[3]{0:T(128)} %copy-done.20) | copy-start | bytes 40
  136.1 1.9 copy-start.3
  141.7 32.4 %all-to-all-start.2 = ((f32[16,2,128,128]{3,2,1,0:T(8,128)}), f32[16,2,128,128]{3,2,1,0:T(8,128)S(1)}, u32[]{:S(2)}, u32[]{:S(2)}) async-start(f32[16,2,128,128]{3,2,1,0:T(8,128)} %get-tuple-element.47), calls=%async_computation.2 | async-start | bytes 4194304 | tf_op jit(solution)/shard_map/all_to_all | solution.py:562
  147.4 164.9 %all-gather.4.cloned.1.call-start = ((), (), s32[]{:S(2)}) async-start(), calls=%async_computation.4 | async-start | bytes 8912896 | tf_op jit(solution)/shard_map/all_gather | solution.py:564
  147.5 25.0 %collective-permute-start.12 = (f32[128,1024]{1,0:T(8,128)S(1)}, f32[128,1024]{1,0:T(8,128)S(1)}, u32[]{:S(2)}, u32[]{:S(2)}) collective-permute-start(f32[128,1024]{1,0:T(8,128)S(1)} %diag_rows.1.refs_0_), channel_id=1, source_target_pairs={{0,96},{16,112},{32,0},{48,16},{64,32},{80,48},{96,64},{112,80},{1... | collective-permute-start | bytes 1572872 | tf_op jit(solution)/shard_map/ppermute | solution.py:522
  148.3 24.2 %collective-permute-start.10 = (f32[128,1024]{1,0:T(8,128)S(1)}, f32[128,1024]{1,0:T(8,128)S(1)}, u32[]{:S(2)}, u32[]{:S(2)}) collective-permute-start(f32[128,1024]{1,0:T(8,128)S(1)} %diag_rows.1.refs_0_), channel_id=1, source_target_pairs={{0,64},{16,80},{32,96},{48,112},{64,0},{80,16},{96,32},{112,48},{1... | collective-permute-start | bytes 1572872 | tf_op jit(solution)/shard_map/ppermute | solution.py:522
  149.4 24.7 %collective-permute-start.8 = (f32[128,1024]{1,0:T(8,128)S(1)}, f32[128,1024]{1,0:T(8,128)}, u32[]{:S(2)}, u32[]{:S(2)}) collective-permute-start(f32[128,1024]{1,0:T(8,128)S(1)} %diag_rows.1.refs_0_), channel_id=1, source_target_pairs={{0,32},{16,48},{32,64},{48,80},{64,96},{80,112},{96,0},{112,16},{1... | collective-permute-start | bytes 1572872 | tf_op jit(solution)/shard_map/ppermute | solution.py:522
  178.0 44.9 %copy-start.10 = (f32[128,1024]{1,0:T(8,128)S(1)}, f32[128,1024]{1,0:T(8,128)}, u32[]{:S(2)}) copy-start(f32[128,1024]{1,0:T(8,128)} %copy-done.9) | copy-start | bytes 1572868
  178.0 44.9 %copy-start.12 = (f32[128,1024]{1,0:T(8,128)S(1)}, f32[128,1024]{1,0:T(8,128)}, u32[]{:S(2)}) copy-start(f32[128,1024]{1,0:T(8,128)} %copy-done.11) | copy-start | bytes 1572868
  178.0 44.9 %copy-start.23 = (s32[3]{0:T(128)S(1)}, s32[3]{0:T(128)}, u32[]{:S(2)}) copy-start(s32[3]{0:T(128)} %copy-done.20) | copy-start | bytes 40
  178.0 27.7 %collective-permute-start.15 = (f32[128,1024]{1,0:T(8,128)}, f32[128,1024]{1,0:T(8,128)S(1)}, u32[]{:S(2)}, u32[]{:S(2)}) collective-permute-start(f32[128,1024]{1,0:T(8,128)} %copy-done.8), channel_id=1, source_target_pairs={{0,0},{1,16},{2,32},{3,48},{4,64},{5,80},{6,96},{7,112},{8,1},{9,1... | collective-permute-start | bytes 1572872 | tf_op jit(solution)/shard_map/ppermute | solution.py:566
  182.9 22.9 %collective-permute-start.7 = (f32[128,1024]{1,0:T(8,128)S(1)}, f32[128,1024]{1,0:T(8,128)S(1)}, u32[]{:S(2)}, u32[]{:S(2)}) collective-permute-start(f32[128,1024]{1,0:T(8,128)S(1)} %diag_rows.1.refs_0_), channel_id=1, source_target_pairs={{0,16},{16,0},{32,48},{48,32},{64,80},{80,64},{96,112},{112,96},{1... | collective-permute-start | bytes 1572872 | tf_op jit(solution)/shard_map/ppermute | solution.py:529
  184.0 30.1 %collective-permute-start.13 = (f32[128,1024]{1,0:T(8,128)}, f32[128,1024]{1,0:T(8,128)S(1)}, u32[]{:S(2)}, u32[]{:S(2)}) collective-permute-start(f32[128,1024]{1,0:T(8,128)} %copy-done.9), channel_id=1, source_target_pairs={{0,16},{16,0},{32,48},{48,32},{64,80},{80,64},{96,112},{112,96},{1... | collective-permute-start | bytes 1572872 | tf_op jit(solution)/shard_map/ppermute | solution.py:529
  184.1 38.8 %collective-permute-start.11 = (f32[128,1024]{1,0:T(8,128)}, f32[128,1024]{1,0:T(8,128)}, u32[]{:S(2)}, u32[]{:S(2)}) collective-permute-start(f32[128,1024]{1,0:T(8,128)} %copy-done.11), channel_id=1, source_target_pairs={{0,16},{16,0},{32,48},{48,32},{64,80},{80,64},{96,112},{112,96},{1... | collective-permute-start | bytes 1572872 | tf_op jit(solution)/shard_map/ppermute | solution.py:529
  184.5 38.4 %collective-permute-start.9 = (f32[128,1024]{1,0:T(8,128)}, f32[128,1024]{1,0:T(8,128)}, u32[]{:S(2)}, u32[]{:S(2)}) collective-permute-start(f32[128,1024]{1,0:T(8,128)} %collective-permute-done.8.refs_2_), channel_id=1, source_target_pairs={{0,16},{16,0},{32,48},{48,32},{64,80},{80,64},{96,112},{112,96},{1... | collective-permute-start | bytes 1572872 | tf_op jit(solution)/shard_map/ppermute | solution.py:529
  205.8 77.9 %collective-permute-start.18 = (f32[128,1024]{1,0:T(8,128)S(1)}, f32[128,1024]{1,0:T(8,128)S(1)}, u32[]{:S(2)}, u32[]{:S(2)}) collective-permute-start(f32[128,1024]{1,0:T(8,128)S(1)} %collective-permute-done.15.refs_0_), channel_id=1, source_target_pairs={{0,96},{16,112},{32,0},{48,16},{64,32},{80,48},{96,64},{112,80},{1... | collective-permute-start | bytes 1572872 | tf_op jit(solution)/shard_map/ppermute | solution.py:522
  206.6 77.1 %collective-permute-start.17 = (f32[128,1024]{1,0:T(8,128)S(1)}, f32[128,1024]{1,0:T(8,128)S(1)}, u32[]{:S(2)}, u32[]{:S(2)}) collective-permute-start(f32[128,1024]{1,0:T(8,128)S(1)} %collective-permute-done.15.refs_0_), channel_id=1, source_target_pairs={{0,64},{16,80},{32,96},{48,112},{64,0},{80,16},{96,32},{112,48},{1... | collective-permute-start | bytes 1572872 | tf_op jit(solution)/shard_map/ppermute | solution.py:522
  215.0 68.7 %collective-permute-start.16 = (f32[128,1024]{1,0:T(8,128)S(1)}, f32[128,1024]{1,0:T(8,128)S(1)}, u32[]{:S(2)}, u32[]{:S(2)}) collective-permute-start(f32[128,1024]{1,0:T(8,128)S(1)} %collective-permute-done.15.refs_0_), channel_id=1, source_target_pairs={{0,32},{16,48},{32,64},{48,80},{64,96},{80,112},{96,0},{112,16},{1... | collective-permute-start | bytes 1572872 | tf_op jit(solution)/shard_map/ppermute | solution.py:522
  281.6 2.1 copy-start
  283.7 11.2 %copy-start.19 = (s32[8,32]{1,0:T(8,128)S(1)}, s32[8,32]{1,0:T(8,128)}, u32[]{:S(2)}) copy-start(s32[8,32]{1,0:T(8,128)} %cmap.9) | copy-start | bytes 3076
  283.7 118.9 %all-to-all-start.3 = ((f32[128,128,128]{2,1,0:T(8,128)}), f32[128,128,128]{2,1,0:T(8,128)}, u32[]{:S(2)}, u32[]{:S(2)}) async-start(f32[128,128,128]{2,1,0:T(8,128)} %pack.1), calls=%async_computation.3 | async-start | bytes 16777216 | tf_op jit(solution)/shard_map/all_to_all | solution.py:571
  293.7 2.0 collective-permute-start.19
  294.0 3.3 collective-permute-start.20
  294.3 3.0 collective-permute-start.21
  294.5 3.6 collective-permute-start.22
  298.1 2.2 copy-start.1
  307.0 1.3 copy-start.4
  309.6 1.3 copy-start.6
  311.0 1.4 copy-start.7
  (9 other events, 8.1 us)
Sparse Core Ops, SparseCore 0:
  84.2 51.8 all-gather.5
  178.1 86.2 all-gather.3

commit v7 on v6

--- a/solution.py
+++ b/solution.py
@@ -556,20 +556,20 @@
     parent = lax.all_to_all(top, "prow", 0, 0, tiled=True)
 
     owners, diag = relay(ids, cmap, small, parent)
+    bulk = pack(after(ids, diag), cmap, child)
     diag = lax.all_gather(diag, "pcol", axis=0)
-    diag = diag_rows(ids, cmap, diag)
+    diag = diag_rows(ids, cmap, after(diag, bulk))
     pivot = across(along_x(diag))
     owners = lax.all_to_all(after(owners, diag), "pcol", 0, 0, tiled=True)
     owned = owner_rows(ids, cmap, start, after(owners, pivot[2::2]))
     xr = lax.all_gather(owned, "pcol", axis=0, tiled=True)
     to = [(at(r, c), at(c % 8, 2 * r + c // 8)) for r in range(ROWS) for c in range(COLS)]
     xc = lax.ppermute(owned, AXES, to)
-    bulk = after(pack(ids, cmap, child), pivot)
-    xc = along_x(xc)
-    w = factor(ids, after(pivot, xc[0]))
-    xc, _ = lax.optimization_barrier((xc, w))
+
+    w = factor(ids, pivot)
+    xc = after(xc, w)
     bulk = lax.all_to_all(after(bulk, (w, xc)), AXES, 0, 0, tiled=True)
-    solved = columns(ids, w, across(xc))
+    solved = columns(ids, w, across(along_x(xc)))
     base = update(ids, pattern, w, solved, xr, own)
     return add(places, base, bulk)
 

time: 427 us -> 450 us (1.054); the launches traced: 425 us -> 442 us
  waiting for transfers between devices: 178 us -> 208 us
  starting transfers between devices: 48.6 us -> 39.9 us
    ppermute x6, waiting for transfers between devices: 20.9 us -> 136 us  [along_x(): pieces.append(lax.ppermute(piece, 'prow', to))]
    all_to_all x1, waiting for transfers between devices: 59 us -> 0.01 us  [body(): bulk = lax.all_to_all(after(bulk, (w, xc)), AXES, 0, 0, tiled=True)]
    ppermute x1, waiting for transfers between devices: 21.2 us -> 0.01 us  [body(): xc = lax.ppermute(owned, AXES, to)]
    ppermute x6, starting transfers between devices: 14.2 us -> 8.15 us  [along_x(): pieces.append(lax.ppermute(piece, 'prow', to))]
    all_gather x1, waiting for transfers between devices: 52 us -> 46.7 us  [body(): diag = lax.all_gather(diag, 'pcol', axis=0)]
    unnamed x59 -> x43, local copies, waits for them, and re-layouts: 21.8 us -> 19.5 us
  transfers between devices with their start and end apart: 28 -> 28, of which waited for: 9 -> 7; matrix products, arithmetic and copies ran while one was open for 1% -> 1% of each run, Pallas kernels for 24% -> 23%
where the time goes in v7:
time: 450 us; the launch traced here: 442 us
  waiting for transfers between devices  208 us (46%)
  Pallas kernels  131 us (29%)
  starting transfers between devices  39.9 us (9%)
  local copies, waits for them, and re-layouts  22.2 us (5%)
  blocking collectives  20.8 us (5%)
  between operations  18.3 us (4%)
    ppermute x6, waiting for transfers between devices, along_x(): pieces.append(lax.ppermute(piece, 'prow', to))  136 us
    pallas_call x1, Pallas kernels, factor(): pl.pallas_call(factor_kernel, out_shape=jax.ShapeDtypeStruct((W, W), F32)...  56.5 us
    all_gather x1, waiting for transfers between devices, body(): diag = lax.all_gather(diag, 'pcol', axis=0)  46.7 us
    pallas_call x1, Pallas kernels, update(): pl.pallas_call(update_kernel, grid=(rows // CHUNK,), out_shape=jax.ShapeD...  31.2 us
    ppermute x8, waiting for transfers between devices, body(): piece = lax.ppermute(piece, AXES, moves[step])  23.4 us
    all_to_all x1, blocking collectives, body(): parent = lax.all_to_all(top, 'prow', 0, 0, tiled=True)  20.8 us
    unnamed x43, local copies, waits for them, and re-layouts  19.5 us
    pallas_call x1, Pallas kernels, add(): pl.pallas_call(add_kernel, grid=(base.shape[0] // CHUNK,), out_shape=jax....  15.4 us
  transfers between devices with their start and end apart: 28, of which 7 were waited for; matrix products, arithmetic and copies ran while one was open for 1% of the time, Pallas kernels for 23%

profile of v7, /device:TPU:14, one launch (start us, length us, event | category | flops | bytes accessed | tf_op | source)
XLA Modules:
  0.0 442.4 jit_solution(2735271998487684236)
XLA Ops:
  7.9 1.3 copy.15.pattern
  9.2 6.2 %pack_parent.1 = (f32[8,128,128]{2,1,0:T(8,128)}, f32[8,128,128]{2,1,0:T(8,128)}, f32[8,128,128]{2,1,0:T(8,128)}, f32[8,128,128]{2,1,0:T(8,128)}, f32[8,128,128]...) custom-call(s32[8,2]{1,0:T(8,128)} %copy.13.sends, ...), custom_call_target="tpu_custom_call" | custom-call | tf_op jit(solution)/shard_map/pack_parent/pallas_call | solution.py:82
  16.1 0.7 collective-permute-start.1
  16.8 0.7 collective-permute-start.2
  17.5 0.7 constant_dynamic-slice_fusion
  18.8 0.7 pad_add_fusion.1.ids
  19.5 2.2 copy-done.2
  21.7 1.5 pack_small.1
  23.2 4.8 %all-to-all-start = ((f32[8,2,128,128]{3,2,1,0:T(8,128)}), f32[8,2,128,128]{3,2,1,0:T(8,128)S(1)}, u32[]{:S(2)}, u32[]{:S(2)}) async-start(f32[8,2,128,128]{3,2,1,0:T(8,128)} %pack_small.1), calls=%async_computation | async-start | bytes 2097152 | tf_op jit(solution)/shard_map/all_to_all | solution.py:550
  29.4 1.3 collective-permute-start.5
  31.5 0.7 collective-permute-start.14
  36.7 23.4 %collective-permute-done.5 = f32[8,128,128]{2,1,0:T(8,128)S(1)} collective-permute-done((f32[8,128,128]{2,1,0:T(8,128)}, f32[8,128,128]{2,1,0:T(8,128)S(1)}, u32[]{:S(2)}, u32[]{:S(2)}) %collective-permute-start.5) | collective-permute-done | bytes 524320 | tf_op jit(solution)/shard_map/ppermute | solution.py:553
  60.6 20.8 %all_to_all.20.parent = f32[8,128,128]{2,1,0:T(8,128)} all-to-all(f32[8,128,128]{2,1,0:T(8,128)S(1)} %get-tuple-element.50), channel_id=1, replica_groups=mesh['prow'=8,'pcol'=16] {'prow'}, dimensions={0} | all-to-all | bytes 1048576 | tf_op jit(solution)/shard_map/all_to_all | solution.py:556
  81.4 2.6 relay.1
  84.0 5.3 %pack.1 = f32[128,128,128]{2,1,0:T(8,128)} custom-call(s32[3]{0:T(128)} %copy-done.15, s32[8,32]{1,0:T(8,128)} %cmap.9, f32[1024,1024]{1,0:T(8,128)} %child.3), custom_call_target="tpu_custom_call" | custom-call | tf_op jit(solution)/shard_map/pack/pallas_call | solution.py:136
  89.3 46.7 %all-gather.6.cloned.1.call-done = f32[48,128,128]{2,1,0:T(8,128)} async-done(((f32[3,128,128]{2,1,0:T(8,128)}), f32[48,128,128]{2,1,0:T(8,128)}) %all-gather.6.cloned.1.call-update) | async-done | bytes 3145744 | tf_op jit(solution)/shard_map/all_gather | solution.py:560
  136.0 1.9 copy-done.3
  137.9 3.0 diag_rows.1.refs_0_
  140.9 5.7 %all-to-all-start.2 = ((f32[16,2,128,128]{3,2,1,0:T(8,128)}), f32[16,2,128,128]{3,2,1,0:T(8,128)S(1)}, u32[]{:S(2)}, u32[]{:S(2)}) async-start(f32[16,2,128,128]{3,2,1,0:T(8,128)} %get-tuple-element.39), calls=%async_computation.2 | async-start | bytes 4194304 | tf_op jit(solution)/shard_map/all_to_all | solution.py:563
  146.6 0.9 collective-permute-start.12
  147.5 1.1 collective-permute-start.10
  148.6 2.0 collective-permute-start.8
  150.6 21.2 %collective-permute-done.12.refs_6_ = f32[128,1024]{1,0:T(8,128)S(1)} collective-permute-done((f32[128,1024]{1,0:T(8,128)S(1)}, f32[128,1024]{1,0:T(8,128)S(1)}, u32[]{:S(2)}, u32[]{:S(2)}) %collective-permute-start.12) | collective-permute-done | bytes 524320 | tf_op jit(solution)/shard_map/ppermute | solution.py:522
  171.8 0.8 copy-done.9
  172.6 0.8 copy-done.11
  173.4 3.0 owner_rows.1
  176.5 0.8 copy-done.8
  178.4 4.8 %collective-permute-start.15 = (f32[128,1024]{1,0:T(8,128)}, f32[128,1024]{1,0:T(8,128)S(1)}, u32[]{:S(2)}, u32[]{:S(2)}) collective-permute-start(f32[128,1024]{1,0:T(8,128)} %copy-done.8), channel_id=1, source_target_pairs={{0,0},{1,16},{2,32},{3,48},{4,64},{5,80},{6,96},{7,112},{8,1},{9,1... | collective-permute-start | bytes 1572872 | tf_op jit(solution)/shard_map/ppermute | solution.py:567
  183.3 1.0 copy-done.10
  184.3 1.0 copy-done.12
  185.4 56.5 %factor.1.w_ref = f32[1024,1024]{1,0:T(8,128)S(1)} custom-call(s32[3]{0:T(128)S(1)} %copy-done.16, f32[128,1024]{1,0:T(8,128)S(1)} %diag_rows.1.refs_0_, f32[128,1024]{1,0:T(8,128)S(1)} %collective-permute-done.7.refs_1_, f32[128,1024]{1,0:T(8,128)} %collective-permute-done.8.refs_2_, f32[128,1024]{1,0:T(8,128)S(1)} %collective-permute-done.9.refs_3_, ...), custom_call_target="tpu_custom_call" | custom-call | tf_op jit(solution)/shard_map/factor/pallas_call | solution.py:333
  241.9 2.1 copy-done
  244.0 8.7 %all-to-all-start.3 = ((f32[128,128,128]{2,1,0:T(8,128)}), f32[128,128,128]{2,1,0:T(8,128)}, u32[]{:S(2)}, u32[]{:S(2)}) async-start(f32[128,128,128]{2,1,0:T(8,128)} %pack.1), calls=%async_computation.3 | async-start | bytes 16777216 | tf_op jit(solution)/shard_map/all_to_all | solution.py:571
  252.6 0.9 collective-permute-start.21
  253.6 1.2 collective-permute-start.19
  254.7 2.1 collective-permute-start.17
  256.8 100.6 %collective-permute-done.21.refs_6_ = f32[128,1024]{1,0:T(8,128)S(1)} collective-permute-done((f32[128,1024]{1,0:T(8,128)S(1)}, f32[128,1024]{1,0:T(8,128)S(1)}, u32[]{:S(2)}, u32[]{:S(2)}) %collective-permute-start.21) | collective-permute-done | bytes 524320 | tf_op jit(solution)/shard_map/ppermute | solution.py:522
  357.5 14.4 %collective-permute-done.19.refs_4_ = f32[128,1024]{1,0:T(8,128)S(1)} collective-permute-done((f32[128,1024]{1,0:T(8,128)S(1)}, f32[128,1024]{1,0:T(8,128)S(1)}, u32[]{:S(2)}, u32[]{:S(2)}) %collective-permute-start.19) | collective-permute-done | bytes 524320 | tf_op jit(solution)/shard_map/ppermute | solution.py:522
  373.1 0.7 collective-permute-done.20.refs_5_
  373.9 0.7 collective-permute-done.18.refs_3_
  374.6 2.2 copy-done.1
  376.8 6.8 %columns.1 = (bf16[1024,1024]{1,0:T(8,128)(2,1)S(1)}, bf16[1024,1024]{1,0:T(8,128)(2,1)S(1)}, bf16[1024,1024]{1,0:T(8,128)(2,1)S(1)}, bf16[1024,1024]{1,0:T(8,128)(2,1)S(1)}) custom-call(s32[3]{0:T(128)S(1)} %copy-done.16, f32[1024,1024]{1,0:T(8,128)S(1)} %copy-done.1, f32[128,1024]{1,0:T(8,128)S(1)} %collective-permute-done.15.refs_0_, ...), custom_call_target="tpu_custom_call" | custom-call | tf_op jit(solution)/shard_map/columns/pallas_call | solution.py:393
  383.6 1.3 copy-done.4
  384.9 1.3 copy-done.5
  386.2 1.3 copy-done.6
  387.5 1.4 copy-done.7
  388.9 31.2 %update.1.base = f32[2048,1024]{1,0:T(8,128)} custom-call(s32[3]{0:T(128)} %copy-done.15, s32[16,8]{1,0:T(8,128)} %copy.15.pattern, f32[1024,1024]{1,0:T(8,128)} %copy-done, bf16[1024,1024]{1,0:T(8,128)(2,1)} %copy-done.4, bf16[1024,1024]{1,0:T(8,128)(2,1)} %copy-done.5, bf16[1024,1024]{1,0:T(8,128)(2,1)} %copy-done.6, bf16[1024,1024]{1,0:T(8,128)(2,1)} %copy-done.7, ...), custom_call_target="tpu_custom_call" | custom-call | tf_op jit(solution)/shard_map/update/pallas_call | solution.py:449
  420.1 15.4 %add.41 = f32[2048,1024]{1,0:T(8,128)} custom-call(s32[2,32]{1,0:T(2,128)} %pad_add_fusion.places, f32[2048,1024]{1,0:T(8,128)} %update.1.base, f32[128,128,128]{2,1,0:T(8,128)} %all-to-all-done.3.came), custom_call_target="tpu_custom_call" | custom-call | tf_op jit(solution)/shard_map/add/pallas_call | solution.py:497
  (73 shorter events, 7.6 us)
Async XLA Ops:
  9.2 10.3 %copy-start.13 = (s32[8,32]{1,0:T(8,128)S(1)}, s32[8,32]{1,0:T(8,128)}, u32[]{:S(2)}) copy-start(s32[8,32]{1,0:T(8,128)} %cmap.9) | copy-start | bytes 3076
  15.4 14.0 %collective-permute-start = (f32[8,128,128]{2,1,0:T(8,128)}, f32[8,128,128]{2,1,0:T(8,128)S(1)}, u32[]{:S(2)}, u32[]{:S(2)}) collective-permute-start(f32[8,128,128]{2,1,0:T(8,128)} %get-tuple-element.26), channel_id=1, source_target_pairs={{0,7},{1,14}} | collective-permute-start | bytes 1572872 | tf_op jit(solution)/shard_map/ppermute | solution.py:553
  16.1 14.6 %collective-permute-start.1 = (f32[8,128,128]{2,1,0:T(8,128)}, f32[8,128,128]{2,1,0:T(8,128)S(1)}, u32[]{:S(2)}, u32[]{:S(2)}) collective-permute-start(f32[8,128,128]{2,1,0:T(8,128)} %get-tuple-element.27), channel_id=1, source_target_pairs={{0,6},{1,13},{16,21},{32,38},{48,55},{64,77},{80,94},{96,111},{112... | collective-permute-start | bytes 1572872 | tf_op jit(solution)/shard_map/ppermute | solution.py:553
  16.8 14.7 %collective-permute-start.2 = (f32[8,128,128]{2,1,0:T(8,128)}, f32[8,128,128]{2,1,0:T(8,128)S(1)}, u32[]{:S(2)}, u32[]{:S(2)}) collective-permute-start(f32[8,128,128]{2,1,0:T(8,128)} %get-tuple-element.28), channel_id=1, source_target_pairs={{0,5},{1,12},{16,31},{3,24},{32,37},{5,41},{48,54},{7,58},{64,71},... | collective-permute-start | bytes 1572872 | tf_op jit(solution)/shard_map/ppermute | solution.py:553
  19.5 2.2 copy-start.2
  21.7 38.8 %copy-start.15 = (s32[3]{0:T(128)}, s32[3]{0:T(128)S(1)}, u32[]{:S(2)}) copy-start(s32[3]{0:T(128)S(1)} %pad_add_fusion.1.ids) | copy-start | bytes 40
  21.7 38.5 %copy-start.18 = (f32[8,128,128]{2,1,0:T(8,128)S(1)}, f32[8,128,128]{2,1,0:T(8,128)}, u32[]{:S(2)}) copy-start(f32[8,128,128]{2,1,0:T(8,128)} %get-tuple-element.33) | copy-start | bytes 1572868
  23.2 37.3 %all-to-all-start = ((f32[8,2,128,128]{3,2,1,0:T(8,128)}), f32[8,2,128,128]{3,2,1,0:T(8,128)S(1)}, u32[]{:S(2)}, u32[]{:S(2)}) async-start(f32[8,2,128,128]{3,2,1,0:T(8,128)} %pack_small.1), calls=%async_computation | async-start | bytes 2097152 | tf_op jit(solution)/shard_map/all_to_all | solution.py:550
  28.0 108.0 %all-gather.6.cloned.1.call-start = ((), (), s32[]{:S(2)}) async-start(), calls=%async_computation.5 | async-start | bytes 3342336 | tf_op jit(solution)/shard_map/all_gather | solution.py:560
  28.0 8.7 %collective-permute-start.3 = (f32[8,128,128]{2,1,0:T(8,128)}, f32[8,128,128]{2,1,0:T(8,128)S(1)}, u32[]{:S(2)}, u32[]{:S(2)}) collective-permute-start(f32[8,128,128]{2,1,0:T(8,128)} %get-tuple-element.29), channel_id=1, source_target_pairs={{0,4},{1,11},{2,17},{16,30},{3,28},{4,34},{32,47},{5,40},{6,51},{4... | collective-permute-start | bytes 1572872 | tf_op jit(solution)/shard_map/ppermute | solution.py:553
  28.7 8.0 %collective-permute-start.4 = (f32[8,128,128]{2,1,0:T(8,128)}, f32[8,128,128]{2,1,0:T(8,128)S(1)}, u32[]{:S(2)}, u32[]{:S(2)}) collective-permute-start(f32[8,128,128]{2,1,0:T(8,128)} %get-tuple-element.30), channel_id=1, source_target_pairs={{0,3},{1,10},{2,20},{16,29},{3,27},{4,33},{32,46},{5,44},{6,50},{4... | collective-permute-start | bytes 1572872 | tf_op jit(solution)/shard_map/ppermute | solution.py:553
  29.4 30.7 %collective-permute-start.5 = (f32[8,128,128]{2,1,0:T(8,128)}, f32[8,128,128]{2,1,0:T(8,128)S(1)}, u32[]{:S(2)}, u32[]{:S(2)}) collective-permute-start(f32[8,128,128]{2,1,0:T(8,128)} %get-tuple-element.31), channel_id=1, source_target_pairs={{0,2},{1,9},{2,19},{16,23},{3,26},{4,36},{32,45},{5,43},{6,49},{48... | collective-permute-start | bytes 1572872 | tf_op jit(solution)/shard_map/ppermute | solution.py:553
  30.7 29.4 %copy-start.19 = (f32[8,128,128]{2,1,0:T(8,128)}, f32[8,128,128]{2,1,0:T(8,128)S(1)}, u32[]{:S(2)}) copy-start(f32[8,128,128]{2,1,0:T(8,128)S(1)} %collective-permute-done.1) | copy-start | bytes 1572868
  30.7 29.4 %collective-permute-start.6 = (f32[8,128,128]{2,1,0:T(8,128)}, f32[8,128,128]{2,1,0:T(8,128)S(1)}, u32[]{:S(2)}, u32[]{:S(2)}) collective-permute-start(f32[8,128,128]{2,1,0:T(8,128)} %get-tuple-element.32), channel_id=1, source_target_pairs={{0,1},{1,8},{2,18},{16,22},{3,25},{4,35},{32,39},{5,42},{6,52},{48... | collective-permute-start | bytes 1572872 | tf_op jit(solution)/shard_map/ppermute | solution.py:553
  31.5 28.7 %copy-start.20 = (f32[8,128,128]{2,1,0:T(8,128)}, f32[8,128,128]{2,1,0:T(8,128)S(1)}, u32[]{:S(2)}) copy-start(f32[8,128,128]{2,1,0:T(8,128)S(1)} %collective-permute-done.2) | copy-start | bytes 1572868
  31.5 28.7 %collective-permute-start.14 = (f32[8,128,128]{2,1,0:T(8,128)}, f32[8,128,128]{2,1,0:T(8,128)S(1)}, u32[]{:S(2)}, u32[]{:S(2)}) collective-permute-start(f32[8,128,128]{2,1,0:T(8,128)} %get-tuple-element.37), channel_id=1, source_target_pairs={{1,15}} | collective-permute-start | bytes 1572872 | tf_op jit(solution)/shard_map/ppermute | solution.py:553
  60.5 20.8 %copy-start.17 = (f32[8,2,128,128]{3,2,1,0:T(8,128)}, f32[8,2,128,128]{3,2,1,0:T(8,128)S(1)}, u32[]{:S(2)}) copy-start(f32[8,2,128,128]{3,2,1,0:T(8,128)S(1)} %all-to-all-done.came) | copy-start | bytes 3145732
  84.0 52.0 %copy-start.14 = (s32[8,32]{1,0:T(8,128)S(1)}, s32[8,32]{1,0:T(8,128)}, u32[]{:S(2)}) copy-start(s32[8,32]{1,0:T(8,128)} %cmap.9) | copy-start | bytes 3076
  84.0 52.0 %copy-start.16 = (s32[3]{0:T(128)S(1)}, s32[3]{0:T(128)}, u32[]{:S(2)}) copy-start(s32[3]{0:T(128)} %copy-done.15) | copy-start | bytes 40
  136.0 1.9 copy-start.3
  140.9 32.6 %all-to-all-start.2 = ((f32[16,2,128,128]{3,2,1,0:T(8,128)}), f32[16,2,128,128]{3,2,1,0:T(8,128)S(1)}, u32[]{:S(2)}, u32[]{:S(2)}) async-start(f32[16,2,128,128]{3,2,1,0:T(8,128)} %get-tuple-element.39), calls=%async_computation.2 | async-start | bytes 4194304 | tf_op jit(solution)/shard_map/all_to_all | solution.py:563
  146.6 242.3 %all-gather.4.cloned.1.call-start = ((), (), s32[]{:S(2)}) async-start(), calls=%async_computation.4 | async-start | bytes 8912896 | tf_op jit(solution)/shard_map/all_gather | solution.py:565
  146.6 25.2 %collective-permute-start.12 = (f32[128,1024]{1,0:T(8,128)S(1)}, f32[128,1024]{1,0:T(8,128)S(1)}, u32[]{:S(2)}, u32[]{:S(2)}) collective-permute-start(f32[128,1024]{1,0:T(8,128)S(1)} %diag_rows.1.refs_0_), channel_id=1, source_target_pairs={{0,96},{16,112},{32,0},{48,16},{64,32},{80,48},{96,64},{112,80},{1... | collective-permute-start | bytes 1572872 | tf_op jit(solution)/shard_map/ppermute | solution.py:522
  147.5 24.3 %collective-permute-start.10 = (f32[128,1024]{1,0:T(8,128)S(1)}, f32[128,1024]{1,0:T(8,128)S(1)}, u32[]{:S(2)}, u32[]{:S(2)}) collective-permute-start(f32[128,1024]{1,0:T(8,128)S(1)} %diag_rows.1.refs_0_), channel_id=1, source_target_pairs={{0,64},{16,80},{32,96},{48,112},{64,0},{80,16},{96,32},{112,48},{1... | collective-permute-start | bytes 1572872 | tf_op jit(solution)/shard_map/ppermute | solution.py:522
  148.6 24.8 %collective-permute-start.8 = (f32[128,1024]{1,0:T(8,128)S(1)}, f32[128,1024]{1,0:T(8,128)}, u32[]{:S(2)}, u32[]{:S(2)}) collective-permute-start(f32[128,1024]{1,0:T(8,128)S(1)} %diag_rows.1.refs_0_), channel_id=1, source_target_pairs={{0,32},{16,48},{32,64},{48,80},{64,96},{80,112},{96,0},{112,16},{1... | collective-permute-start | bytes 1572872 | tf_op jit(solution)/shard_map/ppermute | solution.py:522
  171.8 0.8 copy-start.9
  176.5 0.8 copy-start.8
  177.3 5.9 %collective-permute-start.7 = (f32[128,1024]{1,0:T(8,128)S(1)}, f32[128,1024]{1,0:T(8,128)S(1)}, u32[]{:S(2)}, u32[]{:S(2)}) collective-permute-start(f32[128,1024]{1,0:T(8,128)S(1)} %diag_rows.1.refs_0_), channel_id=1, source_target_pairs={{0,16},{16,0},{32,48},{48,32},{64,80},{80,64},{96,112},{112,96},{1... | collective-permute-start | bytes 1572872 | tf_op jit(solution)/shard_map/ppermute | solution.py:529
  177.4 5.9 %collective-permute-start.13 = (f32[128,1024]{1,0:T(8,128)}, f32[128,1024]{1,0:T(8,128)S(1)}, u32[]{:S(2)}, u32[]{:S(2)}) collective-permute-start(f32[128,1024]{1,0:T(8,128)} %copy-done.9), channel_id=1, source_target_pairs={{0,16},{16,0},{32,48},{48,32},{64,80},{80,64},{96,112},{112,96},{1... | collective-permute-start | bytes 1572872 | tf_op jit(solution)/shard_map/ppermute | solution.py:529
  177.9 5.4 %collective-permute-start.11 = (f32[128,1024]{1,0:T(8,128)}, f32[128,1024]{1,0:T(8,128)S(1)}, u32[]{:S(2)}, u32[]{:S(2)}) collective-permute-start(f32[128,1024]{1,0:T(8,128)} %copy-done.11), channel_id=1, source_target_pairs={{0,16},{16,0},{32,48},{48,32},{64,80},{80,64},{96,112},{112,96},{1... | collective-permute-start | bytes 1572872 | tf_op jit(solution)/shard_map/ppermute | solution.py:529
  178.0 5.3 %collective-permute-start.9 = (f32[128,1024]{1,0:T(8,128)}, f32[128,1024]{1,0:T(8,128)S(1)}, u32[]{:S(2)}, u32[]{:S(2)}) collective-permute-start(f32[128,1024]{1,0:T(8,128)} %collective-permute-done.8.refs_2_), channel_id=1, source_target_pairs={{0,16},{16,0},{32,48},{48,32},{64,80},{80,64},{96,112},{112,96},{1... | collective-permute-start | bytes 1572872 | tf_op jit(solution)/shard_map/ppermute | solution.py:529
  178.4 65.6 %collective-permute-start.15 = (f32[128,1024]{1,0:T(8,128)}, f32[128,1024]{1,0:T(8,128)S(1)}, u32[]{:S(2)}, u32[]{:S(2)}) collective-permute-start(f32[128,1024]{1,0:T(8,128)} %copy-done.8), channel_id=1, source_target_pairs={{0,0},{1,16},{2,32},{3,48},{4,64},{5,80},{6,96},{7,112},{8,1},{9,1... | collective-permute-start | bytes 1572872 | tf_op jit(solution)/shard_map/ppermute | solution.py:567
  183.3 1.0 copy-start.10
  184.3 1.0 copy-start.12
  241.9 2.1 copy-start
  244.0 176.1 %all-to-all-start.3 = ((f32[128,128,128]{2,1,0:T(8,128)}), f32[128,128,128]{2,1,0:T(8,128)}, u32[]{:S(2)}, u32[]{:S(2)}) async-start(f32[128,128,128]{2,1,0:T(8,128)} %pack.1), calls=%async_computation.3 | async-start | bytes 16777216 | tf_op jit(solution)/shard_map/all_to_all | solution.py:571
  252.6 104.8 %collective-permute-start.21 = (f32[128,1024]{1,0:T(8,128)S(1)}, f32[128,1024]{1,0:T(8,128)S(1)}, u32[]{:S(2)}, u32[]{:S(2)}) collective-permute-start(f32[128,1024]{1,0:T(8,128)S(1)} %collective-permute-done.15.refs_0_), channel_id=1, source_target_pairs={{0,96},{16,112},{32,0},{48,16},{64,32},{80,48},{96,64},{112,80},{1... | collective-permute-start | bytes 1572872 | tf_op jit(solution)/shard_map/ppermute | solution.py:522
  253.6 118.2 %collective-permute-start.19 = (f32[128,1024]{1,0:T(8,128)S(1)}, f32[128,1024]{1,0:T(8,128)S(1)}, u32[]{:S(2)}, u32[]{:S(2)}) collective-permute-start(f32[128,1024]{1,0:T(8,128)S(1)} %collective-permute-done.15.refs_0_), channel_id=1, source_target_pairs={{0,64},{16,80},{32,96},{48,112},{64,0},{80,16},{96,32},{112,48},{1... | collective-permute-start | bytes 1572872 | tf_op jit(solution)/shard_map/ppermute | solution.py:522
  254.7 117.1 %collective-permute-start.17 = (f32[128,1024]{1,0:T(8,128)S(1)}, f32[128,1024]{1,0:T(8,128)S(1)}, u32[]{:S(2)}, u32[]{:S(2)}) collective-permute-start(f32[128,1024]{1,0:T(8,128)S(1)} %collective-permute-done.15.refs_0_), channel_id=1, source_target_pairs={{0,32},{16,48},{32,64},{48,80},{64,96},{80,112},{96,0},{112,16},{1... | collective-permute-start | bytes 1572872 | tf_op jit(solution)/shard_map/ppermute | solution.py:522
  256.8 116.3 %collective-permute-start.16 = (f32[128,1024]{1,0:T(8,128)S(1)}, f32[128,1024]{1,0:T(8,128)S(1)}, u32[]{:S(2)}, u32[]{:S(2)}) collective-permute-start(f32[128,1024]{1,0:T(8,128)S(1)} %collective-permute-done.15.refs_0_), channel_id=1, source_target_pairs={{0,16},{16,0},{32,48},{48,32},{64,80},{80,64},{96,112},{112,96},{1... | collective-permute-start | bytes 1572872 | tf_op jit(solution)/shard_map/ppermute | solution.py:529
  357.5 15.7 %collective-permute-start.22 = (f32[128,1024]{1,0:T(8,128)S(1)}, f32[128,1024]{1,0:T(8,128)S(1)}, u32[]{:S(2)}, u32[]{:S(2)}) collective-permute-start(f32[128,1024]{1,0:T(8,128)S(1)} %collective-permute-done.21.refs_6_), channel_id=1, source_target_pairs={{0,16},{16,0},{32,48},{48,32},{64,80},{80,64},{96,112},{112,96},{1... | collective-permute-start | bytes 1572872 | tf_op jit(solution)/shard_map/ppermute | solution.py:529
  371.8 2.0 collective-permute-start.20
  371.8 2.8 collective-permute-start.18
  374.6 2.2 copy-start.1
  383.6 1.3 copy-start.4
  384.9 1.3 copy-start.5
  386.2 1.3 copy-start.6
  387.5 1.4 copy-start.7
  (1 other events, 0.8 us)
Sparse Core Ops, SparseCore 0:
  84.1 51.8 all-gather.5
  177.4 179.7 all-gather.3

commit v8 on v7

--- a/solution.py
+++ b/solution.py
@@ -562,14 +562,14 @@
     pivot = across(along_x(diag))
     owners = lax.all_to_all(after(owners, diag), "pcol", 0, 0, tiled=True)
     owned = owner_rows(ids, cmap, start, after(owners, pivot[2::2]))
-    xr = lax.all_gather(owned, "pcol", axis=0, tiled=True)
     to = [(at(r, c), at(c % 8, 2 * r + c // 8)) for r in range(ROWS) for c in range(COLS)]
     xc = lax.ppermute(owned, AXES, to)
-
-    w = factor(ids, pivot)
-    xc = after(xc, w)
+    xr = lax.all_gather(after(owned, xc), "pcol", axis=0, tiled=True)
+
+    w = factor(ids, after(pivot, xc))
+    xc, _ = lax.optimization_barrier((along_x(xc), w))
     bulk = lax.all_to_all(after(bulk, (w, xc)), AXES, 0, 0, tiled=True)
-    solved = columns(ids, w, across(along_x(xc)))
+    solved = columns(ids, w, across(xc))
     base = update(ids, pattern, w, solved, xr, own)
     return add(places, base, bulk)
 

time: 450 us -> 418 us (0.929); the launches traced: 442 us -> 416 us
  waiting for transfers between devices: 208 us -> 176 us
  starting transfers between devices: 39.9 us -> 45.1 us
    ppermute x6, waiting for transfers between devices: 136 us -> 21.1 us  [along_x(): pieces.append(lax.ppermute(piece, 'prow', to))]
    all_to_all x1, waiting for transfers between devices: 0.01 us -> 59 us  [body(): bulk = lax.all_to_all(after(bulk, (w, xc)), AXES, 0, 0, tiled=True)]
    ppermute x1, waiting for transfers between devices: 0.01 us -> 22.6 us  [body(): xc = lax.ppermute(owned, AXES, to)]
  transfers between devices with their start and end apart: 28 -> 28, of which waited for: 7 -> 10; matrix products, arithmetic and copies ran while one was open for 1% -> 1% of each run, Pallas kernels for 23% -> 24%
where the time goes in v8:
time: 418 us; the launch traced here: 416 us
  waiting for transfers between devices  176 us (42%)
  Pallas kernels  132 us (32%)
  starting transfers between devices  45.1 us (11%)
  local copies, waits for them, and re-layouts  22.2 us (5%)
  blocking collectives  20.8 us (5%)
  between operations  18.3 us (4%)
    all_to_all x1, waiting for transfers between devices, body(): bulk = lax.all_to_all(after(bulk, (w, xc)), AXES, 0, 0, tiled=True)  59 us
    pallas_call x1, Pallas kernels, factor(): pl.pallas_call(factor_kernel, out_shape=jax.ShapeDtypeStruct((W, W), F32)...  56.5 us
    all_gather x1, waiting for transfers between devices, body(): diag = lax.all_gather(diag, 'pcol', axis=0)  46.7 us
    pallas_call x1, Pallas kernels, update(): pl.pallas_call(update_kernel, grid=(rows // CHUNK,), out_shape=jax.ShapeD...  31.2 us
    ppermute x8, waiting for transfers between devices, body(): piece = lax.ppermute(piece, AXES, moves[step])  23.4 us
    ppermute x1, waiting for transfers between devices, body(): xc = lax.ppermute(owned, AXES, to)  22.6 us
    ppermute x6, waiting for transfers between devices, along_x(): pieces.append(lax.ppermute(piece, 'prow', to))  21.1 us
    all_to_all x1, blocking collectives, body(): parent = lax.all_to_all(top, 'prow', 0, 0, tiled=True)  20.8 us
  transfers between devices with their start and end apart: 28, of which 10 were waited for; matrix products, arithmetic and copies ran while one was open for 1% of the time, Pallas kernels for 24%

profile of v8, /device:TPU:14, one launch (start us, length us, event | category | flops | bytes accessed | tf_op | source)
XLA Modules:
  0.0 416.4 jit_solution(9374196617446852607)
XLA Ops:
  7.9 1.3 copy.15.pattern
  9.2 6.2 %pack_parent.1 = (f32[8,128,128]{2,1,0:T(8,128)}, f32[8,128,128]{2,1,0:T(8,128)}, f32[8,128,128]{2,1,0:T(8,128)}, f32[8,128,128]{2,1,0:T(8,128)}, f32[8,128,128]...) custom-call(s32[8,2]{1,0:T(8,128)} %copy.13.sends, ...), custom_call_target="tpu_custom_call" | custom-call | tf_op jit(solution)/shard_map/pack_parent/pallas_call | solution.py:82
  16.1 0.7 collective-permute-start.1
  16.8 0.7 collective-permute-start.2
  17.5 0.7 constant_dynamic-slice_fusion
  18.8 0.7 pad_add_fusion.1.ids
  19.5 2.2 copy-done.2
  21.7 1.5 pack_small.1
  23.2 4.8 %all-to-all-start = ((f32[8,2,128,128]{3,2,1,0:T(8,128)}), f32[8,2,128,128]{3,2,1,0:T(8,128)S(1)}, u32[]{:S(2)}, u32[]{:S(2)}) async-start(f32[8,2,128,128]{3,2,1,0:T(8,128)} %pack_small.1), calls=%async_computation | async-start | bytes 2097152 | tf_op jit(solution)/shard_map/all_to_all | solution.py:550
  28.7 0.7 collective-permute-start.4
  29.4 1.3 collective-permute-start.5
  36.7 23.4 %collective-permute-done.5 = f32[8,128,128]{2,1,0:T(8,128)S(1)} collective-permute-done((f32[8,128,128]{2,1,0:T(8,128)}, f32[8,128,128]{2,1,0:T(8,128)S(1)}, u32[]{:S(2)}, u32[]{:S(2)}) %collective-permute-start.5) | collective-permute-done | bytes 524320 | tf_op jit(solution)/shard_map/ppermute | solution.py:553
  60.6 20.8 %all_to_all.20.parent = f32[8,128,128]{2,1,0:T(8,128)} all-to-all(f32[8,128,128]{2,1,0:T(8,128)S(1)} %get-tuple-element.74), channel_id=1, replica_groups=mesh['prow'=8,'pcol'=16] {'prow'}, dimensions={0} | all-to-all | bytes 1048576 | tf_op jit(solution)/shard_map/all_to_all | solution.py:556
  81.4 2.5 relay.1
  84.0 5.3 %pack.1 = f32[128,128,128]{2,1,0:T(8,128)} custom-call(s32[3]{0:T(128)} %copy-done.15, s32[8,32]{1,0:T(8,128)} %cmap.9, f32[1024,1024]{1,0:T(8,128)} %child.3), custom_call_target="tpu_custom_call" | custom-call | tf_op jit(solution)/shard_map/pack/pallas_call | solution.py:136
  89.2 46.7 %all-gather.6.cloned.1.call-done = f32[48,128,128]{2,1,0:T(8,128)} async-done(((f32[3,128,128]{2,1,0:T(8,128)}), f32[48,128,128]{2,1,0:T(8,128)}) %all-gather.6.cloned.1.call-update) | async-done | bytes 3145744 | tf_op jit(solution)/shard_map/all_gather | solution.py:560
  136.0 1.9 copy-done.3
  137.9 2.9 diag_rows.1.refs_0_
  140.8 5.7 %all-to-all-start.2 = ((f32[16,2,128,128]{3,2,1,0:T(8,128)}), f32[16,2,128,128]{3,2,1,0:T(8,128)S(1)}, u32[]{:S(2)}, u32[]{:S(2)}) async-start(f32[16,2,128,128]{3,2,1,0:T(8,128)} %get-tuple-element.51), calls=%async_computation.2 | async-start | bytes 4194304 | tf_op jit(solution)/shard_map/all_to_all | solution.py:563
  146.6 0.8 collective-permute-start.12
  147.4 1.3 collective-permute-start.10
  148.7 2.0 collective-permute-start.8
  150.7 21.1 %collective-permute-done.12.refs_6_ = f32[128,1024]{1,0:T(8,128)S(1)} collective-permute-done((f32[128,1024]{1,0:T(8,128)S(1)}, f32[128,1024]{1,0:T(8,128)S(1)}, u32[]{:S(2)}, u32[]{:S(2)}) %collective-permute-start.12) | collective-permute-done | bytes 524320 | tf_op jit(solution)/shard_map/ppermute | solution.py:522
  171.8 0.8 copy-done.9
  172.6 0.8 copy-done.11
  173.4 3.2 owner_rows.1
  176.6 0.8 copy-done.8
  177.4 4.4 %collective-permute-start.15 = (f32[128,1024]{1,0:T(8,128)}, f32[128,1024]{1,0:T(8,128)S(1)}, u32[]{:S(2)}, u32[]{:S(2)}) collective-permute-start(f32[128,1024]{1,0:T(8,128)} %copy-done.8), channel_id=1, source_target_pairs={{0,0},{1,16},{2,32},{3,48},{4,64},{5,80},{6,96},{7,112},{8,1},{9,1... | collective-permute-start | bytes 1572872 | tf_op jit(solution)/shard_map/ppermute | solution.py:566
  181.9 22.6 %collective-permute-done.15.refs_0_ = f32[128,1024]{1,0:T(8,128)S(1)} collective-permute-done((f32[128,1024]{1,0:T(8,128)}, f32[128,1024]{1,0:T(8,128)S(1)}, u32[]{:S(2)}, u32[]{:S(2)}) %collective-permute-start.15) | collective-permute-done | bytes 524320 | tf_op jit(solution)/shard_map/ppermute | solution.py:566
  204.5 0.9 collective-permute-start.7
  206.1 0.8 collective-permute-done.7.refs_1_
  206.9 3.8 collective-permute-start.17
  211.2 1.0 copy-done.10
  212.2 1.0 copy-done.12
  213.3 56.5 %factor.1.w_ref = f32[1024,1024]{1,0:T(8,128)S(1)} custom-call(s32[3]{0:T(128)S(1)} %copy-done.16, f32[128,1024]{1,0:T(8,128)S(1)} %diag_rows.1.refs_0_, f32[128,1024]{1,0:T(8,128)S(1)} %collective-permute-done.7.refs_1_, f32[128,1024]{1,0:T(8,128)} %collective-permute-done.8.refs_2_, f32[128,1024]{1,0:T(8,128)S(1)} %collective-permute-done.9.refs_3_, ...), custom_call_target="tpu_custom_call" | custom-call | tf_op jit(solution)/shard_map/factor/pallas_call | solution.py:333
  269.8 2.1 copy-done
  271.9 12.9 %all-to-all-start.3 = ((f32[128,128,128]{2,1,0:T(8,128)}), f32[128,128,128]{2,1,0:T(8,128)}, u32[]{:S(2)}, u32[]{:S(2)}) async-start(f32[128,128,128]{2,1,0:T(8,128)} %pack.1), calls=%async_computation.3 | async-start | bytes 16777216 | tf_op jit(solution)/shard_map/all_to_all | solution.py:571
  286.8 1.5 collective-permute-done.20.refs_3_
  288.4 0.8 collective-permute-done.22.refs_7_
  289.1 2.2 copy-done.1
  291.3 6.8 %columns.1 = (bf16[1024,1024]{1,0:T(8,128)(2,1)S(1)}, bf16[1024,1024]{1,0:T(8,128)(2,1)S(1)}, bf16[1024,1024]{1,0:T(8,128)(2,1)S(1)}, bf16[1024,1024]{1,0:T(8,128)(2,1)S(1)}) custom-call(s32[3]{0:T(128)S(1)} %copy-done.16, f32[1024,1024]{1,0:T(8,128)S(1)} %copy-done.1, f32[128,1024]{1,0:T(8,128)S(1)} %collective-permute-done.15.refs_0_, ...), custom_call_target="tpu_custom_call" | custom-call | tf_op jit(solution)/shard_map/columns/pallas_call | solution.py:393
  298.1 1.3 copy-done.4
  299.4 1.3 copy-done.5
  300.7 1.3 copy-done.6
  302.0 1.4 copy-done.7
  303.4 31.2 %update.1.base = f32[2048,1024]{1,0:T(8,128)} custom-call(s32[3]{0:T(128)} %copy-done.15, s32[16,8]{1,0:T(8,128)} %copy.15.pattern, f32[1024,1024]{1,0:T(8,128)} %copy-done, bf16[1024,1024]{1,0:T(8,128)(2,1)} %copy-done.4, bf16[1024,1024]{1,0:T(8,128)(2,1)} %copy-done.5, bf16[1024,1024]{1,0:T(8,128)(2,1)} %copy-done.6, bf16[1024,1024]{1,0:T(8,128)(2,1)} %copy-done.7, ...), custom_call_target="tpu_custom_call" | custom-call | tf_op jit(solution)/shard_map/update/pallas_call | solution.py:449
  334.7 59.0 %all-to-all-done.3.came = f32[128,128,128]{2,1,0:T(8,128)} async-done(((f32[128,128,128]{2,1,0:T(8,128)}), f32[128,128,128]{2,1,0:T(8,128)}, u32[]{:S(2)}, u32[]{:S(2)}) %all-to-all-start.3) | async-done | bytes 8388640 | tf_op jit(solution)/shard_map/all_to_all | solution.py:571
  393.6 15.9 %add.41 = f32[2048,1024]{1,0:T(8,128)} custom-call(s32[2,32]{1,0:T(2,128)} %pad_add_fusion.places, f32[2048,1024]{1,0:T(8,128)} %update.1.base, f32[128,128,128]{2,1,0:T(8,128)} %all-to-all-done.3.came), custom_call_target="tpu_custom_call" | custom-call | tf_op jit(solution)/shard_map/add/pallas_call | solution.py:497
  (73 shorter events, 8.5 us)
Async XLA Ops:
  9.2 10.3 %copy-start.13 = (s32[8,32]{1,0:T(8,128)S(1)}, s32[8,32]{1,0:T(8,128)}, u32[]{:S(2)}) copy-start(s32[8,32]{1,0:T(8,128)} %cmap.9) | copy-start | bytes 3076
  15.4 14.0 %collective-permute-start = (f32[8,128,128]{2,1,0:T(8,128)}, f32[8,128,128]{2,1,0:T(8,128)S(1)}, u32[]{:S(2)}, u32[]{:S(2)}) collective-permute-start(f32[8,128,128]{2,1,0:T(8,128)} %get-tuple-element.38), channel_id=1, source_target_pairs={{0,7},{1,14}} | collective-permute-start | bytes 1572872 | tf_op jit(solution)/shard_map/ppermute | solution.py:553
  16.1 14.6 %collective-permute-start.1 = (f32[8,128,128]{2,1,0:T(8,128)}, f32[8,128,128]{2,1,0:T(8,128)S(1)}, u32[]{:S(2)}, u32[]{:S(2)}) collective-permute-start(f32[8,128,128]{2,1,0:T(8,128)} %get-tuple-element.39), channel_id=1, source_target_pairs={{0,6},{1,13},{16,21},{32,38},{48,55},{64,77},{80,94},{96,111},{112... | collective-permute-start | bytes 1572872 | tf_op jit(solution)/shard_map/ppermute | solution.py:553
  16.8 14.7 %collective-permute-start.2 = (f32[8,128,128]{2,1,0:T(8,128)}, f32[8,128,128]{2,1,0:T(8,128)S(1)}, u32[]{:S(2)}, u32[]{:S(2)}) collective-permute-start(f32[8,128,128]{2,1,0:T(8,128)} %get-tuple-element.40), channel_id=1, source_target_pairs={{0,5},{1,12},{16,31},{3,24},{32,37},{5,41},{48,54},{7,58},{64,71},... | collective-permute-start | bytes 1572872 | tf_op jit(solution)/shard_map/ppermute | solution.py:553
  19.5 2.2 copy-start.2
  21.7 38.8 %copy-start.15 = (s32[3]{0:T(128)}, s32[3]{0:T(128)S(1)}, u32[]{:S(2)}) copy-start(s32[3]{0:T(128)S(1)} %pad_add_fusion.1.ids) | copy-start | bytes 40
  21.7 38.5 %copy-start.18 = (f32[8,128,128]{2,1,0:T(8,128)S(1)}, f32[8,128,128]{2,1,0:T(8,128)}, u32[]{:S(2)}) copy-start(f32[8,128,128]{2,1,0:T(8,128)} %get-tuple-element.45) | copy-start | bytes 1572868
  23.2 37.3 %all-to-all-start = ((f32[8,2,128,128]{3,2,1,0:T(8,128)}), f32[8,2,128,128]{3,2,1,0:T(8,128)S(1)}, u32[]{:S(2)}, u32[]{:S(2)}) async-start(f32[8,2,128,128]{3,2,1,0:T(8,128)} %pack_small.1), calls=%async_computation | async-start | bytes 2097152 | tf_op jit(solution)/shard_map/all_to_all | solution.py:550
  28.0 108.0 %all-gather.6.cloned.1.call-start = ((), (), s32[]{:S(2)}) async-start(), calls=%async_computation.5 | async-start | bytes 3342336 | tf_op jit(solution)/shard_map/all_gather | solution.py:560
  28.0 8.7 %collective-permute-start.3 = (f32[8,128,128]{2,1,0:T(8,128)}, f32[8,128,128]{2,1,0:T(8,128)S(1)}, u32[]{:S(2)}, u32[]{:S(2)}) collective-permute-start(f32[8,128,128]{2,1,0:T(8,128)} %get-tuple-element.41), channel_id=1, source_target_pairs={{0,4},{1,11},{2,17},{16,30},{3,28},{4,34},{32,47},{5,40},{6,51},{4... | collective-permute-start | bytes 1572872 | tf_op jit(solution)/shard_map/ppermute | solution.py:553
  28.7 8.0 %collective-permute-start.4 = (f32[8,128,128]{2,1,0:T(8,128)}, f32[8,128,128]{2,1,0:T(8,128)S(1)}, u32[]{:S(2)}, u32[]{:S(2)}) collective-permute-start(f32[8,128,128]{2,1,0:T(8,128)} %get-tuple-element.42), channel_id=1, source_target_pairs={{0,3},{1,10},{2,20},{16,29},{3,27},{4,33},{32,46},{5,44},{6,50},{4... | collective-permute-start | bytes 1572872 | tf_op jit(solution)/shard_map/ppermute | solution.py:553
  29.4 30.7 %collective-permute-start.5 = (f32[8,128,128]{2,1,0:T(8,128)}, f32[8,128,128]{2,1,0:T(8,128)S(1)}, u32[]{:S(2)}, u32[]{:S(2)}) collective-permute-start(f32[8,128,128]{2,1,0:T(8,128)} %get-tuple-element.43), channel_id=1, source_target_pairs={{0,2},{1,9},{2,19},{16,23},{3,26},{4,36},{32,45},{5,43},{6,49},{48... | collective-permute-start | bytes 1572872 | tf_op jit(solution)/shard_map/ppermute | solution.py:553
  30.7 29.4 %copy-start.19 = (f32[8,128,128]{2,1,0:T(8,128)}, f32[8,128,128]{2,1,0:T(8,128)S(1)}, u32[]{:S(2)}) copy-start(f32[8,128,128]{2,1,0:T(8,128)S(1)} %collective-permute-done.1) | copy-start | bytes 1572868
  30.7 29.4 %collective-permute-start.6 = (f32[8,128,128]{2,1,0:T(8,128)}, f32[8,128,128]{2,1,0:T(8,128)S(1)}, u32[]{:S(2)}, u32[]{:S(2)}) collective-permute-start(f32[8,128,128]{2,1,0:T(8,128)} %get-tuple-element.44), channel_id=1, source_target_pairs={{0,1},{1,8},{2,18},{16,22},{3,25},{4,35},{32,39},{5,42},{6,52},{48... | collective-permute-start | bytes 1572872 | tf_op jit(solution)/shard_map/ppermute | solution.py:553
  31.5 28.7 %copy-start.20 = (f32[8,128,128]{2,1,0:T(8,128)}, f32[8,128,128]{2,1,0:T(8,128)S(1)}, u32[]{:S(2)}) copy-start(f32[8,128,128]{2,1,0:T(8,128)S(1)} %collective-permute-done.2) | copy-start | bytes 1572868
  31.5 28.7 %collective-permute-start.14 = (f32[8,128,128]{2,1,0:T(8,128)}, f32[8,128,128]{2,1,0:T(8,128)S(1)}, u32[]{:S(2)}, u32[]{:S(2)}) collective-permute-start(f32[8,128,128]{2,1,0:T(8,128)} %get-tuple-element.49), channel_id=1, source_target_pairs={{1,15}} | collective-permute-start | bytes 1572872 | tf_op jit(solution)/shard_map/ppermute | solution.py:553
  60.5 20.8 %copy-start.17 = (f32[8,2,128,128]{3,2,1,0:T(8,128)}, f32[8,2,128,128]{3,2,1,0:T(8,128)S(1)}, u32[]{:S(2)}) copy-start(f32[8,2,128,128]{3,2,1,0:T(8,128)S(1)} %all-to-all-done.came) | copy-start | bytes 3145732
  83.9 52.0 %copy-start.14 = (s32[8,32]{1,0:T(8,128)S(1)}, s32[8,32]{1,0:T(8,128)}, u32[]{:S(2)}) copy-start(s32[8,32]{1,0:T(8,128)} %cmap.9) | copy-start | bytes 3076
  84.0 52.0 %copy-start.16 = (s32[3]{0:T(128)S(1)}, s32[3]{0:T(128)}, u32[]{:S(2)}) copy-start(s32[3]{0:T(128)} %copy-done.15) | copy-start | bytes 40
  136.0 1.9 copy-start.3
  140.8 32.6 %all-to-all-start.2 = ((f32[16,2,128,128]{3,2,1,0:T(8,128)}), f32[16,2,128,128]{3,2,1,0:T(8,128)S(1)}, u32[]{:S(2)}, u32[]{:S(2)}) async-start(f32[16,2,128,128]{3,2,1,0:T(8,128)} %get-tuple-element.51), calls=%async_computation.2 | async-start | bytes 4194304 | tf_op jit(solution)/shard_map/all_to_all | solution.py:563
  146.5 156.9 %all-gather.4.cloned.1.call-start = ((), (), s32[]{:S(2)}) async-start(), calls=%async_computation.4 | async-start | bytes 8912896 | tf_op jit(solution)/shard_map/all_gather | solution.py:567
  146.6 25.3 %collective-permute-start.12 = (f32[128,1024]{1,0:T(8,128)S(1)}, f32[128,1024]{1,0:T(8,128)S(1)}, u32[]{:S(2)}, u32[]{:S(2)}) collective-permute-start(f32[128,1024]{1,0:T(8,128)S(1)} %diag_rows.1.refs_0_), channel_id=1, source_target_pairs={{0,96},{16,112},{32,0},{48,16},{64,32},{80,48},{96,64},{112,80},{1... | collective-permute-start | bytes 1572872 | tf_op jit(solution)/shard_map/ppermute | solution.py:522
  147.4 24.5 %collective-permute-start.10 = (f32[128,1024]{1,0:T(8,128)S(1)}, f32[128,1024]{1,0:T(8,128)S(1)}, u32[]{:S(2)}, u32[]{:S(2)}) collective-permute-start(f32[128,1024]{1,0:T(8,128)S(1)} %diag_rows.1.refs_0_), channel_id=1, source_target_pairs={{0,64},{16,80},{32,96},{48,112},{64,0},{80,16},{96,32},{112,48},{1... | collective-permute-start | bytes 1572872 | tf_op jit(solution)/shard_map/ppermute | solution.py:522
  148.7 24.7 %collective-permute-start.8 = (f32[128,1024]{1,0:T(8,128)S(1)}, f32[128,1024]{1,0:T(8,128)}, u32[]{:S(2)}, u32[]{:S(2)}) collective-permute-start(f32[128,1024]{1,0:T(8,128)S(1)} %diag_rows.1.refs_0_), channel_id=1, source_target_pairs={{0,32},{16,48},{32,64},{48,80},{64,96},{80,112},{96,0},{112,16},{1... | collective-permute-start | bytes 1572872 | tf_op jit(solution)/shard_map/ppermute | solution.py:522
  171.8 0.8 copy-start.9
  176.6 0.8 copy-start.8
  177.4 27.1 %collective-permute-start.15 = (f32[128,1024]{1,0:T(8,128)}, f32[128,1024]{1,0:T(8,128)S(1)}, u32[]{:S(2)}, u32[]{:S(2)}) collective-permute-start(f32[128,1024]{1,0:T(8,128)} %copy-done.8), channel_id=1, source_target_pairs={{0,0},{1,16},{2,32},{3,48},{4,64},{5,80},{6,96},{7,112},{8,1},{9,1... | collective-permute-start | bytes 1572872 | tf_op jit(solution)/shard_map/ppermute | solution.py:566
  204.5 2.4 collective-permute-start.7
  205.4 5.3 %collective-permute-start.13 = (f32[128,1024]{1,0:T(8,128)}, f32[128,1024]{1,0:T(8,128)S(1)}, u32[]{:S(2)}, u32[]{:S(2)}) collective-permute-start(f32[128,1024]{1,0:T(8,128)} %copy-done.9), channel_id=1, source_target_pairs={{0,16},{16,0},{32,48},{48,32},{64,80},{80,64},{96,112},{112,96},{1... | collective-permute-start | bytes 1572872 | tf_op jit(solution)/shard_map/ppermute | solution.py:529
  205.5 5.7 %collective-permute-start.11 = (f32[128,1024]{1,0:T(8,128)}, f32[128,1024]{1,0:T(8,128)S(1)}, u32[]{:S(2)}, u32[]{:S(2)}) collective-permute-start(f32[128,1024]{1,0:T(8,128)} %copy-done.11), channel_id=1, source_target_pairs={{0,16},{16,0},{32,48},{48,32},{64,80},{80,64},{96,112},{112,96},{1... | collective-permute-start | bytes 1572872 | tf_op jit(solution)/shard_map/ppermute | solution.py:529
  205.9 5.3 %collective-permute-start.9 = (f32[128,1024]{1,0:T(8,128)}, f32[128,1024]{1,0:T(8,128)S(1)}, u32[]{:S(2)}, u32[]{:S(2)}) collective-permute-start(f32[128,1024]{1,0:T(8,128)} %collective-permute-done.8.refs_2_), channel_id=1, source_target_pairs={{0,16},{16,0},{32,48},{48,32},{64,80},{80,64},{96,112},{112,96},{1... | collective-permute-start | bytes 1572872 | tf_op jit(solution)/shard_map/ppermute | solution.py:529
  206.0 65.9 %collective-permute-start.18 = (f32[128,1024]{1,0:T(8,128)S(1)}, f32[128,1024]{1,0:T(8,128)S(1)}, u32[]{:S(2)}, u32[]{:S(2)}) collective-permute-start(f32[128,1024]{1,0:T(8,128)S(1)} %collective-permute-done.15.refs_0_), channel_id=1, source_target_pairs={{0,96},{16,112},{32,0},{48,16},{64,32},{80,48},{96,64},{112,80},{1... | collective-permute-start | bytes 1572872 | tf_op jit(solution)/shard_map/ppermute | solution.py:522
  206.9 65.0 %collective-permute-start.17 = (f32[128,1024]{1,0:T(8,128)S(1)}, f32[128,1024]{1,0:T(8,128)S(1)}, u32[]{:S(2)}, u32[]{:S(2)}) collective-permute-start(f32[128,1024]{1,0:T(8,128)S(1)} %collective-permute-done.15.refs_0_), channel_id=1, source_target_pairs={{0,64},{16,80},{32,96},{48,112},{64,0},{80,16},{96,32},{112,48},{1... | collective-permute-start | bytes 1572872 | tf_op jit(solution)/shard_map/ppermute | solution.py:522
  210.7 61.2 %collective-permute-start.16 = (f32[128,1024]{1,0:T(8,128)S(1)}, f32[128,1024]{1,0:T(8,128)S(1)}, u32[]{:S(2)}, u32[]{:S(2)}) collective-permute-start(f32[128,1024]{1,0:T(8,128)S(1)} %collective-permute-done.15.refs_0_), channel_id=1, source_target_pairs={{0,32},{16,48},{32,64},{48,80},{64,96},{80,112},{96,0},{112,16},{1... | collective-permute-start | bytes 1572872 | tf_op jit(solution)/shard_map/ppermute | solution.py:522
  211.2 1.0 copy-start.10
  212.2 1.0 copy-start.12
  269.8 2.1 copy-start
  271.9 121.7 %all-to-all-start.3 = ((f32[128,128,128]{2,1,0:T(8,128)}), f32[128,128,128]{2,1,0:T(8,128)}, u32[]{:S(2)}, u32[]{:S(2)}) async-start(f32[128,128,128]{2,1,0:T(8,128)} %pack.1), calls=%async_computation.3 | async-start | bytes 16777216 | tf_op jit(solution)/shard_map/all_to_all | solution.py:571
  284.8 2.0 collective-permute-start.19
  285.0 3.3 collective-permute-start.20
  285.4 3.0 collective-permute-start.21
  285.5 3.6 collective-permute-start.22
  289.1 2.2 copy-start.1
  298.1 1.3 copy-start.4
  299.4 1.3 copy-start.5
  300.7 1.3 copy-start.6
  302.0 1.4 copy-start.7
  (1 other events, 0.8 us)
Sparse Core Ops, SparseCore 0:
  84.1 51.8 all-gather.5
  204.6 75.3 all-gather.3

commit v9 on v8

--- a/solution.py
+++ b/solution.py
@@ -564,10 +564,10 @@
     owned = owner_rows(ids, cmap, start, after(owners, pivot[2::2]))
     to = [(at(r, c), at(c % 8, 2 * r + c // 8)) for r in range(ROWS) for c in range(COLS)]
     xc = lax.ppermute(owned, AXES, to)
-    xr = lax.all_gather(after(owned, xc), "pcol", axis=0, tiled=True)
-
-    w = factor(ids, after(pivot, xc))
-    xc, _ = lax.optimization_barrier((along_x(xc), w))
+    xr = lax.all_gather(owned, "pcol", axis=0, tiled=True)
+
+    w = factor(ids, pivot)
+    xc = along_x(after(xc, w))
     bulk = lax.all_to_all(after(bulk, (w, xc)), AXES, 0, 0, tiled=True)
     solved = columns(ids, w, across(xc))
     base = update(ids, pattern, w, solved, xr, own)

time: 418 us -> 414 us (level)
    ppermute x6, waiting for transfers between devices: 21.1 us -> 44.4 us  [along_x(): pieces.append(lax.ppermute(piece, 'prow', to))]
    ppermute x1, waiting for transfers between devices: 22.6 us -> 0.01 us  [body(): xc = lax.ppermute(owned, AXES, to)]
  transfers between devices with their start and end apart: 28 -> 28, of which waited for: 10 -> 11; matrix products, arithmetic and copies ran while one was open for 1% -> 1% of each run, Pallas kernels for 24% -> 25%
where the time goes in v9:
time: 414 us; the launch traced here: 412 us
  waiting for transfers between devices  176 us (43%)
  Pallas kernels  132 us (32%)
  starting transfers between devices  41.1 us (10%)
  local copies, waits for them, and re-layouts  22.2 us (5%)
  blocking collectives  20.8 us (5%)
  between operations  18.3 us (4%)
    all_to_all x1, waiting for transfers between devices, body(): bulk = lax.all_to_all(after(bulk, (w, xc)), AXES, 0, 0, tiled=True)  59 us
    pallas_call x1, Pallas kernels, factor(): pl.pallas_call(factor_kernel, out_shape=jax.ShapeDtypeStruct((W, W), F32)...  56.5 us
    all_gather x1, waiting for transfers between devices, body(): diag = lax.all_gather(diag, 'pcol', axis=0)  46.7 us
    ppermute x6, waiting for transfers between devices, along_x(): pieces.append(lax.ppermute(piece, 'prow', to))  44.4 us
    pallas_call x1, Pallas kernels, update(): pl.pallas_call(update_kernel, grid=(rows // CHUNK,), out_shape=jax.ShapeD...  31.2 us
    ppermute x8, waiting for transfers between devices, body(): piece = lax.ppermute(piece, AXES, moves[step])  23.4 us
    all_to_all x1, blocking collectives, body(): parent = lax.all_to_all(top, 'prow', 0, 0, tiled=True)  20.8 us
    unnamed x43, local copies, waits for them, and re-layouts  19.5 us
  transfers between devices with their start and end apart: 28, of which 11 were waited for; matrix products, arithmetic and copies ran while one was open for 1% of the time, Pallas kernels for 25%

profile of v9, /device:TPU:14, one launch (start us, length us, event | category | flops | bytes accessed | tf_op | source)
XLA Modules:
  0.0 412.4 jit_solution(4640979465629921559)
XLA Ops:
  7.9 1.3 copy.15.pattern
  9.2 6.2 %pack_parent.1 = (f32[8,128,128]{2,1,0:T(8,128)}, f32[8,128,128]{2,1,0:T(8,128)}, f32[8,128,128]{2,1,0:T(8,128)}, f32[8,128,128]{2,1,0:T(8,128)}, f32[8,128,128]...) custom-call(s32[8,2]{1,0:T(8,128)} %copy.13.sends, ...), custom_call_target="tpu_custom_call" | custom-call | tf_op jit(solution)/shard_map/pack_parent/pallas_call | solution.py:82
  16.1 0.7 collective-permute-start.1
  16.8 0.7 collective-permute-start.2
  17.5 0.7 constant_dynamic-slice_fusion
  18.8 0.7 pad_add_fusion.1.ids
  19.5 2.2 copy-done.2
  21.7 1.5 pack_small.1
  23.2 4.8 %all-to-all-start = ((f32[8,2,128,128]{3,2,1,0:T(8,128)}), f32[8,2,128,128]{3,2,1,0:T(8,128)S(1)}, u32[]{:S(2)}, u32[]{:S(2)}) async-start(f32[8,2,128,128]{3,2,1,0:T(8,128)} %pack_small.1), calls=%async_computation | async-start | bytes 2097152 | tf_op jit(solution)/shard_map/all_to_all | solution.py:550
  28.7 0.7 collective-permute-start.4
  29.4 1.3 collective-permute-start.5
  30.7 0.7 collective-permute-start.6
  36.7 23.4 %collective-permute-done.5 = f32[8,128,128]{2,1,0:T(8,128)S(1)} collective-permute-done((f32[8,128,128]{2,1,0:T(8,128)}, f32[8,128,128]{2,1,0:T(8,128)S(1)}, u32[]{:S(2)}, u32[]{:S(2)}) %collective-permute-start.5) | collective-permute-done | bytes 524320 | tf_op jit(solution)/shard_map/ppermute | solution.py:553
  60.6 20.8 %all_to_all.20.parent = f32[8,128,128]{2,1,0:T(8,128)} all-to-all(f32[8,128,128]{2,1,0:T(8,128)S(1)} %get-tuple-element.50), channel_id=1, replica_groups=mesh['prow'=8,'pcol'=16] {'prow'}, dimensions={0} | all-to-all | bytes 1048576 | tf_op jit(solution)/shard_map/all_to_all | solution.py:556
  81.4 2.6 relay.1
  84.0 5.3 %pack.1 = f32[128,128,128]{2,1,0:T(8,128)} custom-call(s32[3]{0:T(128)} %copy-done.15, s32[8,32]{1,0:T(8,128)} %cmap.9, f32[1024,1024]{1,0:T(8,128)} %child.3), custom_call_target="tpu_custom_call" | custom-call | tf_op jit(solution)/shard_map/pack/pallas_call | solution.py:136
  89.3 46.7 %all-gather.6.cloned.1.call-done = f32[48,128,128]{2,1,0:T(8,128)} async-done(((f32[3,128,128]{2,1,0:T(8,128)}), f32[48,128,128]{2,1,0:T(8,128)}) %all-gather.6.cloned.1.call-update) | async-done | bytes 3145744 | tf_op jit(solution)/shard_map/all_gather | solution.py:560
  136.0 1.9 copy-done.3
  137.9 2.9 diag_rows.1.refs_0_
  140.8 5.7 %all-to-all-start.2 = ((f32[16,2,128,128]{3,2,1,0:T(8,128)}), f32[16,2,128,128]{3,2,1,0:T(8,128)S(1)}, u32[]{:S(2)}, u32[]{:S(2)}) async-start(f32[16,2,128,128]{3,2,1,0:T(8,128)} %get-tuple-element.39), calls=%async_computation.2 | async-start | bytes 4194304 | tf_op jit(solution)/shard_map/all_to_all | solution.py:563
  146.6 1.1 collective-permute-start.12
  147.6 1.3 collective-permute-start.10
  148.9 1.9 collective-permute-start.8
  150.9 20.8 %collective-permute-done.12.refs_6_ = f32[128,1024]{1,0:T(8,128)S(1)} collective-permute-done((f32[128,1024]{1,0:T(8,128)S(1)}, f32[128,1024]{1,0:T(8,128)S(1)}, u32[]{:S(2)}, u32[]{:S(2)}) %collective-permute-start.12) | collective-permute-done | bytes 524320 | tf_op jit(solution)/shard_map/ppermute | solution.py:522
  171.7 0.8 copy-done.9
  172.5 0.8 copy-done.11
  173.3 3.0 owner_rows.1
  176.4 0.8 copy-done.8
  178.3 5.2 %collective-permute-start.15 = (f32[128,1024]{1,0:T(8,128)}, f32[128,1024]{1,0:T(8,128)S(1)}, u32[]{:S(2)}, u32[]{:S(2)}) collective-permute-start(f32[128,1024]{1,0:T(8,128)} %copy-done.8), channel_id=1, source_target_pairs={{0,0},{1,16},{2,32},{3,48},{4,64},{5,80},{6,96},{7,112},{8,1},{9,1... | collective-permute-start | bytes 1572872 | tf_op jit(solution)/shard_map/ppermute | solution.py:566
  183.5 1.0 copy-done.10
  184.5 1.0 copy-done.12
  185.6 56.5 %factor.1.w_ref = f32[1024,1024]{1,0:T(8,128)S(1)} custom-call(s32[3]{0:T(128)S(1)} %copy-done.16, f32[128,1024]{1,0:T(8,128)S(1)} %diag_rows.1.refs_0_, f32[128,1024]{1,0:T(8,128)S(1)} %collective-permute-done.7.refs_1_, f32[128,1024]{1,0:T(8,128)} %collective-permute-done.8.refs_2_, f32[128,1024]{1,0:T(8,128)S(1)} %collective-permute-done.9.refs_3_, ...), custom_call_target="tpu_custom_call" | custom-call | tf_op jit(solution)/shard_map/factor/pallas_call | solution.py:333
  242.1 2.1 copy-done
  244.2 4.0 collective-permute-start.19
  248.2 12.6 %collective-permute-done.21.refs_6_ = f32[128,1024]{1,0:T(8,128)S(1)} collective-permute-done((f32[128,1024]{1,0:T(8,128)S(1)}, f32[128,1024]{1,0:T(8,128)S(1)}, u32[]{:S(2)}, u32[]{:S(2)}) %collective-permute-start.21) | collective-permute-done | bytes 524320 | tf_op jit(solution)/shard_map/ppermute | solution.py:522
  260.8 10.4 %collective-permute-done.19.refs_4_ = f32[128,1024]{1,0:T(8,128)S(1)} collective-permute-done((f32[128,1024]{1,0:T(8,128)S(1)}, f32[128,1024]{1,0:T(8,128)S(1)}, u32[]{:S(2)}, u32[]{:S(2)}) %collective-permute-start.19) | collective-permute-done | bytes 524320 | tf_op jit(solution)/shard_map/ppermute | solution.py:522
  271.7 8.8 %all-to-all-start.3 = ((f32[128,128,128]{2,1,0:T(8,128)}), f32[128,128,128]{2,1,0:T(8,128)}, u32[]{:S(2)}, u32[]{:S(2)}) async-start(f32[128,128,128]{2,1,0:T(8,128)} %pack.1), calls=%async_computation.3 | async-start | bytes 16777216 | tf_op jit(solution)/shard_map/all_to_all | solution.py:571
  282.5 1.5 collective-permute-done.22.refs_7_
  284.1 0.8 collective-permute-done.18.refs_3_
  284.9 2.2 copy-done.1
  287.1 6.8 %columns.1 = (bf16[1024,1024]{1,0:T(8,128)(2,1)S(1)}, bf16[1024,1024]{1,0:T(8,128)(2,1)S(1)}, bf16[1024,1024]{1,0:T(8,128)(2,1)S(1)}, bf16[1024,1024]{1,0:T(8,128)(2,1)S(1)}) custom-call(s32[3]{0:T(128)S(1)} %copy-done.16, f32[1024,1024]{1,0:T(8,128)S(1)} %copy-done.1, f32[128,1024]{1,0:T(8,128)S(1)} %collective-permute-done.15.refs_0_, ...), custom_call_target="tpu_custom_call" | custom-call | tf_op jit(solution)/shard_map/columns/pallas_call | solution.py:393
  293.9 1.3 copy-done.4
  295.1 1.3 copy-done.5
  296.5 1.3 copy-done.6
  297.8 1.4 copy-done.7
  299.2 31.2 %update.1.base = f32[2048,1024]{1,0:T(8,128)} custom-call(s32[3]{0:T(128)} %copy-done.15, s32[16,8]{1,0:T(8,128)} %copy.15.pattern, f32[1024,1024]{1,0:T(8,128)} %copy-done, bf16[1024,1024]{1,0:T(8,128)(2,1)} %copy-done.4, bf16[1024,1024]{1,0:T(8,128)(2,1)} %copy-done.5, bf16[1024,1024]{1,0:T(8,128)(2,1)} %copy-done.6, bf16[1024,1024]{1,0:T(8,128)(2,1)} %copy-done.7, ...), custom_call_target="tpu_custom_call" | custom-call | tf_op jit(solution)/shard_map/update/pallas_call | solution.py:449
  330.4 59.0 %all-to-all-done.3.came = f32[128,128,128]{2,1,0:T(8,128)} async-done(((f32[128,128,128]{2,1,0:T(8,128)}), f32[128,128,128]{2,1,0:T(8,128)}, u32[]{:S(2)}, u32[]{:S(2)}) %all-to-all-start.3) | async-done | bytes 8388640 | tf_op jit(solution)/shard_map/all_to_all | solution.py:571
  389.4 16.1 %add.41 = f32[2048,1024]{1,0:T(8,128)} custom-call(s32[2,32]{1,0:T(2,128)} %pad_add_fusion.places, f32[2048,1024]{1,0:T(8,128)} %update.1.base, f32[128,128,128]{2,1,0:T(8,128)} %all-to-all-done.3.came), custom_call_target="tpu_custom_call" | custom-call | tf_op jit(solution)/shard_map/add/pallas_call | solution.py:497
  (73 shorter events, 8.3 us)
Async XLA Ops:
  9.2 10.3 %copy-start.13 = (s32[8,32]{1,0:T(8,128)S(1)}, s32[8,32]{1,0:T(8,128)}, u32[]{:S(2)}) copy-start(s32[8,32]{1,0:T(8,128)} %cmap.9) | copy-start | bytes 3076
  15.4 14.0 %collective-permute-start = (f32[8,128,128]{2,1,0:T(8,128)}, f32[8,128,128]{2,1,0:T(8,128)S(1)}, u32[]{:S(2)}, u32[]{:S(2)}) collective-permute-start(f32[8,128,128]{2,1,0:T(8,128)} %get-tuple-element.26), channel_id=1, source_target_pairs={{0,7},{1,14}} | collective-permute-start | bytes 1572872 | tf_op jit(solution)/shard_map/ppermute | solution.py:553
  16.1 14.6 %collective-permute-start.1 = (f32[8,128,128]{2,1,0:T(8,128)}, f32[8,128,128]{2,1,0:T(8,128)S(1)}, u32[]{:S(2)}, u32[]{:S(2)}) collective-permute-start(f32[8,128,128]{2,1,0:T(8,128)} %get-tuple-element.27), channel_id=1, source_target_pairs={{0,6},{1,13},{16,21},{32,38},{48,55},{64,77},{80,94},{96,111},{112... | collective-permute-start | bytes 1572872 | tf_op jit(solution)/shard_map/ppermute | solution.py:553
  16.8 14.7 %collective-permute-start.2 = (f32[8,128,128]{2,1,0:T(8,128)}, f32[8,128,128]{2,1,0:T(8,128)S(1)}, u32[]{:S(2)}, u32[]{:S(2)}) collective-permute-start(f32[8,128,128]{2,1,0:T(8,128)} %get-tuple-element.28), channel_id=1, source_target_pairs={{0,5},{1,12},{16,31},{3,24},{32,37},{5,41},{48,54},{7,58},{64,71},... | collective-permute-start | bytes 1572872 | tf_op jit(solution)/shard_map/ppermute | solution.py:553
  19.5 2.2 copy-start.2
  21.7 38.8 %copy-start.15 = (s32[3]{0:T(128)}, s32[3]{0:T(128)S(1)}, u32[]{:S(2)}) copy-start(s32[3]{0:T(128)S(1)} %pad_add_fusion.1.ids) | copy-start | bytes 40
  21.7 38.5 %copy-start.18 = (f32[8,128,128]{2,1,0:T(8,128)S(1)}, f32[8,128,128]{2,1,0:T(8,128)}, u32[]{:S(2)}) copy-start(f32[8,128,128]{2,1,0:T(8,128)} %get-tuple-element.33) | copy-start | bytes 1572868
  23.2 37.3 %all-to-all-start = ((f32[8,2,128,128]{3,2,1,0:T(8,128)}), f32[8,2,128,128]{3,2,1,0:T(8,128)S(1)}, u32[]{:S(2)}, u32[]{:S(2)}) async-start(f32[8,2,128,128]{3,2,1,0:T(8,128)} %pack_small.1), calls=%async_computation | async-start | bytes 2097152 | tf_op jit(solution)/shard_map/all_to_all | solution.py:550
  28.0 108.0 %all-gather.6.cloned.1.call-start = ((), (), s32[]{:S(2)}) async-start(), calls=%async_computation.5 | async-start | bytes 3342336 | tf_op jit(solution)/shard_map/all_gather | solution.py:560
  28.0 8.7 %collective-permute-start.3 = (f32[8,128,128]{2,1,0:T(8,128)}, f32[8,128,128]{2,1,0:T(8,128)S(1)}, u32[]{:S(2)}, u32[]{:S(2)}) collective-permute-start(f32[8,128,128]{2,1,0:T(8,128)} %get-tuple-element.29), channel_id=1, source_target_pairs={{0,4},{1,11},{2,17},{16,30},{3,28},{4,34},{32,47},{5,40},{6,51},{4... | collective-permute-start | bytes 1572872 | tf_op jit(solution)/shard_map/ppermute | solution.py:553
  28.7 8.0 %collective-permute-start.4 = (f32[8,128,128]{2,1,0:T(8,128)}, f32[8,128,128]{2,1,0:T(8,128)S(1)}, u32[]{:S(2)}, u32[]{:S(2)}) collective-permute-start(f32[8,128,128]{2,1,0:T(8,128)} %get-tuple-element.30), channel_id=1, source_target_pairs={{0,3},{1,10},{2,20},{16,29},{3,27},{4,33},{32,46},{5,44},{6,50},{4... | collective-permute-start | bytes 1572872 | tf_op jit(solution)/shard_map/ppermute | solution.py:553
  29.4 30.7 %collective-permute-start.5 = (f32[8,128,128]{2,1,0:T(8,128)}, f32[8,128,128]{2,1,0:T(8,128)S(1)}, u32[]{:S(2)}, u32[]{:S(2)}) collective-permute-start(f32[8,128,128]{2,1,0:T(8,128)} %get-tuple-element.31), channel_id=1, source_target_pairs={{0,2},{1,9},{2,19},{16,23},{3,26},{4,36},{32,45},{5,43},{6,49},{48... | collective-permute-start | bytes 1572872 | tf_op jit(solution)/shard_map/ppermute | solution.py:553
  30.7 29.4 %copy-start.19 = (f32[8,128,128]{2,1,0:T(8,128)}, f32[8,128,128]{2,1,0:T(8,128)S(1)}, u32[]{:S(2)}) copy-start(f32[8,128,128]{2,1,0:T(8,128)S(1)} %collective-permute-done.1) | copy-start | bytes 1572868
  30.7 29.4 %collective-permute-start.6 = (f32[8,128,128]{2,1,0:T(8,128)}, f32[8,128,128]{2,1,0:T(8,128)S(1)}, u32[]{:S(2)}, u32[]{:S(2)}) collective-permute-start(f32[8,128,128]{2,1,0:T(8,128)} %get-tuple-element.32), channel_id=1, source_target_pairs={{0,1},{1,8},{2,18},{16,22},{3,25},{4,35},{32,39},{5,42},{6,52},{48... | collective-permute-start | bytes 1572872 | tf_op jit(solution)/shard_map/ppermute | solution.py:553
  31.5 28.7 %copy-start.20 = (f32[8,128,128]{2,1,0:T(8,128)}, f32[8,128,128]{2,1,0:T(8,128)S(1)}, u32[]{:S(2)}) copy-start(f32[8,128,128]{2,1,0:T(8,128)S(1)} %collective-permute-done.2) | copy-start | bytes 1572868
  31.5 28.7 %collective-permute-start.14 = (f32[8,128,128]{2,1,0:T(8,128)}, f32[8,128,128]{2,1,0:T(8,128)S(1)}, u32[]{:S(2)}, u32[]{:S(2)}) collective-permute-start(f32[8,128,128]{2,1,0:T(8,128)} %get-tuple-element.37), channel_id=1, source_target_pairs={{1,15}} | collective-permute-start | bytes 1572872 | tf_op jit(solution)/shard_map/ppermute | solution.py:553
  60.5 20.8 %copy-start.17 = (f32[8,2,128,128]{3,2,1,0:T(8,128)}, f32[8,2,128,128]{3,2,1,0:T(8,128)S(1)}, u32[]{:S(2)}) copy-start(f32[8,2,128,128]{3,2,1,0:T(8,128)S(1)} %all-to-all-done.came) | copy-start | bytes 3145732
  84.0 52.0 %copy-start.14 = (s32[8,32]{1,0:T(8,128)S(1)}, s32[8,32]{1,0:T(8,128)}, u32[]{:S(2)}) copy-start(s32[8,32]{1,0:T(8,128)} %cmap.9) | copy-start | bytes 3076
  84.0 52.0 %copy-start.16 = (s32[3]{0:T(128)S(1)}, s32[3]{0:T(128)}, u32[]{:S(2)}) copy-start(s32[3]{0:T(128)} %copy-done.15) | copy-start | bytes 40
  136.0 1.9 copy-start.3
  140.8 32.5 %all-to-all-start.2 = ((f32[16,2,128,128]{3,2,1,0:T(8,128)}), f32[16,2,128,128]{3,2,1,0:T(8,128)S(1)}, u32[]{:S(2)}, u32[]{:S(2)}) async-start(f32[16,2,128,128]{3,2,1,0:T(8,128)} %get-tuple-element.39), calls=%async_computation.2 | async-start | bytes 4194304 | tf_op jit(solution)/shard_map/all_to_all | solution.py:563
  146.5 152.7 %all-gather.4.cloned.1.call-start = ((), (), s32[]{:S(2)}) async-start(), calls=%async_computation.4 | async-start | bytes 8912896 | tf_op jit(solution)/shard_map/all_gather | solution.py:567
  146.6 25.1 %collective-permute-start.12 = (f32[128,1024]{1,0:T(8,128)S(1)}, f32[128,1024]{1,0:T(8,128)S(1)}, u32[]{:S(2)}, u32[]{:S(2)}) collective-permute-start(f32[128,1024]{1,0:T(8,128)S(1)} %diag_rows.1.refs_0_), channel_id=1, source_target_pairs={{0,96},{16,112},{32,0},{48,16},{64,32},{80,48},{96,64},{112,80},{1... | collective-permute-start | bytes 1572872 | tf_op jit(solution)/shard_map/ppermute | solution.py:522
  147.6 24.1 %collective-permute-start.10 = (f32[128,1024]{1,0:T(8,128)S(1)}, f32[128,1024]{1,0:T(8,128)S(1)}, u32[]{:S(2)}, u32[]{:S(2)}) collective-permute-start(f32[128,1024]{1,0:T(8,128)S(1)} %diag_rows.1.refs_0_), channel_id=1, source_target_pairs={{0,64},{16,80},{32,96},{48,112},{64,0},{80,16},{96,32},{112,48},{1... | collective-permute-start | bytes 1572872 | tf_op jit(solution)/shard_map/ppermute | solution.py:522
  148.9 24.4 %collective-permute-start.8 = (f32[128,1024]{1,0:T(8,128)S(1)}, f32[128,1024]{1,0:T(8,128)}, u32[]{:S(2)}, u32[]{:S(2)}) collective-permute-start(f32[128,1024]{1,0:T(8,128)S(1)} %diag_rows.1.refs_0_), channel_id=1, source_target_pairs={{0,32},{16,48},{32,64},{48,80},{64,96},{80,112},{96,0},{112,16},{1... | collective-permute-start | bytes 1572872 | tf_op jit(solution)/shard_map/ppermute | solution.py:522
  171.7 0.8 copy-start.9
  176.3 0.8 copy-start.8
  177.2 6.3 %collective-permute-start.7 = (f32[128,1024]{1,0:T(8,128)S(1)}, f32[128,1024]{1,0:T(8,128)S(1)}, u32[]{:S(2)}, u32[]{:S(2)}) collective-permute-start(f32[128,1024]{1,0:T(8,128)S(1)} %diag_rows.1.refs_0_), channel_id=1, source_target_pairs={{0,16},{16,0},{32,48},{48,32},{64,80},{80,64},{96,112},{112,96},{1... | collective-permute-start | bytes 1572872 | tf_op jit(solution)/shard_map/ppermute | solution.py:529
  177.3 6.2 %collective-permute-start.13 = (f32[128,1024]{1,0:T(8,128)}, f32[128,1024]{1,0:T(8,128)S(1)}, u32[]{:S(2)}, u32[]{:S(2)}) collective-permute-start(f32[128,1024]{1,0:T(8,128)} %copy-done.9), channel_id=1, source_target_pairs={{0,16},{16,0},{32,48},{48,32},{64,80},{80,64},{96,112},{112,96},{1... | collective-permute-start | bytes 1572872 | tf_op jit(solution)/shard_map/ppermute | solution.py:529
  177.8 5.7 %collective-permute-start.11 = (f32[128,1024]{1,0:T(8,128)}, f32[128,1024]{1,0:T(8,128)S(1)}, u32[]{:S(2)}, u32[]{:S(2)}) collective-permute-start(f32[128,1024]{1,0:T(8,128)} %copy-done.11), channel_id=1, source_target_pairs={{0,16},{16,0},{32,48},{48,32},{64,80},{80,64},{96,112},{112,96},{1... | collective-permute-start | bytes 1572872 | tf_op jit(solution)/shard_map/ppermute | solution.py:529
  177.9 5.6 %collective-permute-start.9 = (f32[128,1024]{1,0:T(8,128)}, f32[128,1024]{1,0:T(8,128)S(1)}, u32[]{:S(2)}, u32[]{:S(2)}) collective-permute-start(f32[128,1024]{1,0:T(8,128)} %collective-permute-done.8.refs_2_), channel_id=1, source_target_pairs={{0,16},{16,0},{32,48},{48,32},{64,80},{80,64},{96,112},{112,96},{1... | collective-permute-start | bytes 1572872 | tf_op jit(solution)/shard_map/ppermute | solution.py:529
  178.3 65.9 %collective-permute-start.15 = (f32[128,1024]{1,0:T(8,128)}, f32[128,1024]{1,0:T(8,128)S(1)}, u32[]{:S(2)}, u32[]{:S(2)}) collective-permute-start(f32[128,1024]{1,0:T(8,128)} %copy-done.8), channel_id=1, source_target_pairs={{0,0},{1,16},{2,32},{3,48},{4,64},{5,80},{6,96},{7,112},{8,1},{9,1... | collective-permute-start | bytes 1572872 | tf_op jit(solution)/shard_map/ppermute | solution.py:566
  183.5 1.0 copy-start.10
  184.5 1.0 copy-start.12
  242.1 2.1 copy-start
  244.2 16.6 %collective-permute-start.21 = (f32[128,1024]{1,0:T(8,128)S(1)}, f32[128,1024]{1,0:T(8,128)S(1)}, u32[]{:S(2)}, u32[]{:S(2)}) collective-permute-start(f32[128,1024]{1,0:T(8,128)S(1)} %collective-permute-done.15.refs_0_), channel_id=1, source_target_pairs={{0,96},{16,112},{32,0},{48,16},{64,32},{80,48},{96,64},{112,80},{1... | collective-permute-start | bytes 1572872 | tf_op jit(solution)/shard_map/ppermute | solution.py:522
  244.2 27.0 %collective-permute-start.19 = (f32[128,1024]{1,0:T(8,128)S(1)}, f32[128,1024]{1,0:T(8,128)S(1)}, u32[]{:S(2)}, u32[]{:S(2)}) collective-permute-start(f32[128,1024]{1,0:T(8,128)S(1)} %collective-permute-done.15.refs_0_), channel_id=1, source_target_pairs={{0,64},{16,80},{32,96},{48,112},{64,0},{80,16},{96,32},{112,48},{1... | collective-permute-start | bytes 1572872 | tf_op jit(solution)/shard_map/ppermute | solution.py:522
  248.2 23.5 %collective-permute-start.17 = (f32[128,1024]{1,0:T(8,128)S(1)}, f32[128,1024]{1,0:T(8,128)S(1)}, u32[]{:S(2)}, u32[]{:S(2)}) collective-permute-start(f32[128,1024]{1,0:T(8,128)S(1)} %collective-permute-done.15.refs_0_), channel_id=1, source_target_pairs={{0,32},{16,48},{32,64},{48,80},{64,96},{80,112},{96,0},{112,16},{1... | collective-permute-start | bytes 1572872 | tf_op jit(solution)/shard_map/ppermute | solution.py:522
  271.7 117.7 %all-to-all-start.3 = ((f32[128,128,128]{2,1,0:T(8,128)}), f32[128,128,128]{2,1,0:T(8,128)}, u32[]{:S(2)}, u32[]{:S(2)}) async-start(f32[128,128,128]{2,1,0:T(8,128)} %pack.1), calls=%async_computation.3 | async-start | bytes 16777216 | tf_op jit(solution)/shard_map/all_to_all | solution.py:571
  280.5 2.0 collective-permute-start.16
  280.7 3.3 collective-permute-start.22
  281.1 3.0 collective-permute-start.20
  281.3 3.6 collective-permute-start.18
  284.9 2.2 copy-start.1
  293.9 1.3 copy-start.4
  295.1 1.3 copy-start.5
  296.5 1.3 copy-start.6
  297.8 1.4 copy-start.7
  (1 other events, 0.8 us)
Sparse Core Ops, SparseCore 0:
  84.1 51.8 all-gather.5
  177.3 87.3 all-gather.3
